TPU v7x, 32 devices: a whole 2x2x4 slice. The times are simulated.
32 devices in a mesh: rep: 4 (over y, x), shard: 8 (over z, core).
Axes of the slice: x: 2, y: 2, z: 4, core: 2. Of those that a mesh axis runs over, the one named last changes fastest.
Arguments:
- block_input: bfloat16 [16384, 960], P(('rep', 'shard')), may hold values from -6 to 6
- block_cotangent: bfloat16 [16384, 960], P(('rep', 'shard')), may hold values from -6 to 6
- lengths: int32 [4, 3], P('rep'), may hold values from 1 to 2048, 4096 in all within a row
- attend_gain: bfloat16 [960], P('shard'), may hold values from 0.5 to 1.5
- attend_weight: bfloat16 [960, 1600], P('shard'), may hold values from -0.25 to 0.25
- output_weight: bfloat16 [960, 960], P(None, 'shard'), may hold values from -0.375 to 0.375
- expand_gain: bfloat16 [960], P('shard'), may hold values from 0.5 to 1.5
- expand_weight: bfloat16 [960, 5120], P('shard'), may hold values from -0.1875 to 0.1875
- shrink_weight: bfloat16 [2560, 960], P(None, 'shard'), may hold values from -0.125 to 0.125
- attend_gain_first: float32 [960], P('shard'), may hold values from -6 to 6
- attend_weight_first: float32 [960, 1600], P('shard'), may hold values from -6 to 6
- output_weight_first: float32 [960, 960], P(None, 'shard'), may hold values from -4 to 4
- expand_gain_first: float32 [960], P('shard'), may hold values from -5 to 5
- expand_weight_first: float32 [960, 5120], P('shard'), may hold values from -2.5 to 2.5
- shrink_weight_first: float32 [2560, 960], P(None, 'shard'), may hold values from -4 to 4
- attend_gain_second: float32 [960], P('shard'), may hold values from 10 to 40
- attend_weight_second: float32 [960, 1600], P('shard'), may hold values from 3 to 13
- output_weight_second: float32 [960, 960], P(None, 'shard'), may hold values from 0.3 to 1.2
- expand_gain_second: float32 [960], P('shard'), may hold values from 0.6 to 2.4
- expand_weight_second: float32 [960, 5120], P('shard'), may hold values from 0.12 to 0.5
- shrink_weight_second: float32 [2560, 960], P(None, 'shard'), may hold values from 0.3 to 1.2
Outputs:
- block_output: float32 [16384, 960], P(('rep', 'shard'))
- input_gradient: float32 [16384, 960], P(('rep', 'shard'))
- attend_gain_gradient: float32 [960], P('shard')
- attend_weight_gradient: float32 [960, 1600], P('shard')
- output_weight_gradient: float32 [960, 960], P(None, 'shard')
- expand_gain_gradient: float32 [960], P('shard')
- expand_weight_gradient: float32 [960, 5120], P('shard')
- shrink_weight_gradient: float32 [2560, 960], P(None, 'shard')
- attend_gain_moment: float32 [960], P('shard')
- attend_weight_moment: float32 [960, 1600], P('shard')
- output_weight_moment: float32 [960, 960], P(None, 'shard')
- expand_gain_moment: float32 [960], P('shard')
- expand_weight_moment: float32 [960, 5120], P('shard')
- shrink_weight_moment: float32 [2560, 960], P(None, 'shard')
- attend_gain_square: float32 [960], P('shard')
- attend_weight_square: float32 [960, 1600], P('shard')
- output_weight_square: float32 [960, 960], P(None, 'shard')
- expand_gain_square: float32 [960], P('shard')
- expand_weight_square: float32 [960, 5120], P('shard')
- shrink_weight_square: float32 [2560, 960], P(None, 'shard')
- attend_gain_update: float32 [960], P('shard')
- attend_weight_next: float32 [960, 1600], P('shard')
- output_weight_next: float32 [960, 960], P(None, 'shard')
- expand_gain_update: float32 [960], P('shard')
- expand_weight_next: float32 [960, 5120], P('shard')
- shrink_weight_next: float32 [2560, 960], P(None, 'shard')
Inputs may be any that keep to these rules, and one draw needn't show every extreme that they name: In each replica group's row the 3 lengths sum to 4096 and the longest is exactly 2048; the sequences lie back to back, in this order, in the group's token rows.
All inputs are finite; a program needn't handle non-finite values.
Results may differ from a plain program's by a relative error of at most 0.015.
Values may be sent and summed in bfloat16 or wider, within the bound.
A program may use at most 136 MiB of HBM per device.

v0:
```python
import jax
import jax.numpy as jnp
from jax import lax
from jax.sharding import PartitionSpec as P

HEADS = 15
KV_HEADS = 5
HEAD_DIM = 64
FF = 2560
MAXLEN = 2048
STEP = 10
QW = 960
KW = 320


eps_norm = 1e-05
rope_base = 100000.0
beta_one = 0.9
beta_two = 0.95
adam_eps = 1e-08
learn_rate = 0.05
decay_rate = 0.1
grad_factor = 4.0
masked_score = -1e30


def passed_along(block, axis, distance):
    devices = range(lax.axis_size(axis))
    route = [(i - distance, i) for i in devices if i - distance in devices]
    return lax.ppermute(block, axis, route)


def sequence_starts(lengths, group_index):
    ends_at = jnp.cumsum(lengths, dtype=jnp.int32)
    before = (ends_at[None, :] <= group_index[:, None]).astype(jnp.int32)
    return jnp.sum(before * lengths[None, :], axis=1, dtype=jnp.int32)


def angles(positions):
    half_dim = HEAD_DIM // 2
    inverse = rope_base ** (-(2.0 * jnp.arange(half_dim, dtype=jnp.float32) / HEAD_DIM))
    phases = positions.astype(jnp.float32)[:, None] * inverse[None, :]
    return (jnp.cos(phases)[:, None, :], jnp.sin(phases)[:, None, :])


def rotate(tensor, cosine_table, sine_table):
    half_dim = tensor.shape[-1] // 2
    front_half = tensor[..., :half_dim]
    back_half = tensor[..., half_dim:]
    return jnp.concatenate(
        [
            front_half * cosine_table - back_half * sine_table,
            back_half * cosine_table + front_half * sine_table,
        ],
        axis=-1,
    )


def unrotate(tensor, cosine_table, sine_table):
    half_dim = tensor.shape[-1] // 2
    front_half = tensor[..., :half_dim]
    back_half = tensor[..., half_dim:]
    return jnp.concatenate(
        [
            front_half * cosine_table + back_half * sine_table,
            back_half * cosine_table - front_half * sine_table,
        ],
        axis=-1,
    )


def norm_back(upstream, normed, scale_rows):
    return scale_rows * (upstream - normed * jnp.mean(upstream * normed, axis=-1, keepdims=True))


def adam_step(weight_now, gradient, first, second, decay_factor):
    old_weight = weight_now.astype(jnp.float32)
    moment = beta_one * first + (1.0 - beta_one) * gradient
    square = beta_two * second + (1.0 - beta_two) * gradient * gradient
    corrected = moment / (1.0 - beta_one**STEP)
    divisor = jnp.sqrt(square / (1.0 - beta_two**STEP)) + adam_eps
    update = -learn_rate * (corrected / divisor + decay_factor * old_weight)
    return (gradient, moment, square, old_weight + update, update)


def shards(
    block_input,
    block_cotangent,
    lengths,
    attend_gain,
    attend_weight,
    output_weight,
    expand_gain,
    expand_weight,
    shrink_weight,
    attend_gain_first,
    attend_weight_first,
    output_weight_first,
    expand_gain_first,
    expand_weight_first,
    shrink_weight_first,
    attend_gain_second,
    attend_weight_second,
    output_weight_second,
    expand_gain_second,
    expand_weight_second,
    shrink_weight_second,
):
    row_count = block_input.shape[0]
    token_count = row_count * lax.axis_size("shard") * lax.axis_size("rep")
    reach_count = (MAXLEN - 2) // row_count + 1
    window_rows = (reach_count + 1) * row_count
    group_size = HEADS // KV_HEADS
    head_scale = HEAD_DIM ** (-0.5)
    first_row = lax.axis_index("shard") * row_count
    local_index = first_row + jnp.arange(row_count, dtype=jnp.int32)
    start_index = sequence_starts(lengths[0], local_index)
    key_index = first_row - reach_count * row_count + jnp.arange(window_rows, dtype=jnp.int32)
    allowed = (key_index[None, :] >= start_index[:, None]) & (
        key_index[None, :] <= local_index[:, None]
    )
    cosine_table, sine_table = angles(local_index - start_index)
    gain_one, joint_weight, out_weight = (
        lax.all_gather(attend_gain, "shard", axis=0, tiled=True),
        lax.all_gather(attend_weight, "shard", axis=0, tiled=True),
        lax.all_gather(output_weight, "shard", axis=1, tiled=True),
    )
    inputs = block_input.astype(jnp.float32)
    scale_one = lax.rsqrt(jnp.mean(inputs * inputs, axis=-1, keepdims=True) + eps_norm)
    normed_one = inputs * scale_one
    hidden_one = (normed_one * gain_one.astype(jnp.float32)).astype(jnp.bfloat16)
    joint_out = jnp.dot(hidden_one, joint_weight, preferred_element_type=jnp.float32)
    queries = rotate(
        joint_out[:, :QW].reshape(row_count, HEADS, HEAD_DIM), cosine_table, sine_table
    ).astype(jnp.bfloat16)
    key_rows = rotate(
        joint_out[:, QW : QW + KW].reshape(row_count, KV_HEADS, HEAD_DIM), cosine_table, sine_table
    ).astype(jnp.bfloat16)
    own_pairs = jnp.concatenate(
        [key_rows.reshape(row_count, KW), joint_out[:, QW + KW :].astype(jnp.bfloat16)], axis=1
    )
    earlier = []
    for distance in range(reach_count, 0, -1):
        earlier.append(passed_along(own_pairs, "shard", distance))
    window = jnp.concatenate(earlier + [own_pairs], axis=0)
    key_heads = jnp.repeat(
        window[:, :KW].reshape(window_rows, KV_HEADS, HEAD_DIM).transpose(1, 0, 2),
        group_size,
        axis=0,
    )
    value_heads = jnp.repeat(
        window[:, KW:].reshape(window_rows, KV_HEADS, HEAD_DIM).transpose(1, 0, 2),
        group_size,
        axis=0,
    )
    query_heads = queries.transpose(1, 0, 2)

    def head_scores(query_head, key_head):
        raw_scores = (
            jnp.einsum("qd,wd->qw", query_head, key_head, preferred_element_type=jnp.float32)
            * head_scale
        )
        return jnp.where(allowed, raw_scores, masked_score)

    def forward_head(element):
        query_head, key_head, value_head = element
        scores = head_scores(query_head, key_head)
        highest = jnp.max(scores, axis=-1, keepdims=True)
        powers = jnp.exp(scores - highest)
        totals = jnp.sum(powers, axis=-1, keepdims=True)
        probs_low = (powers / totals).astype(jnp.bfloat16)
        mixed_head = jnp.einsum(
            "qw,wd->qd", probs_low, value_head, preferred_element_type=jnp.float32
        )
        return (mixed_head.astype(jnp.bfloat16), (highest + jnp.log(totals))[:, 0])

    mixed_heads, log_totals = lax.map(forward_head, (query_heads, key_heads, value_heads))
    mixed_rows = mixed_heads.transpose(1, 0, 2).reshape(row_count, QW)
    middle = inputs + jnp.dot(mixed_rows, out_weight, preferred_element_type=jnp.float32)
    gain_two, expand_full, shrink_full = (
        lax.all_gather(expand_gain, "shard", axis=0, tiled=True),
        lax.all_gather(expand_weight, "shard", axis=0, tiled=True),
        lax.all_gather(shrink_weight, "shard", axis=1, tiled=True),
    )
    scale_two = lax.rsqrt(jnp.mean(middle * middle, axis=-1, keepdims=True) + eps_norm)
    normed_two = middle * scale_two
    hidden_two = (normed_two * gain_two.astype(jnp.float32)).astype(jnp.bfloat16)
    gate_up = jnp.dot(hidden_two, expand_full, preferred_element_type=jnp.float32)
    gate_value = gate_up[:, :FF]
    upper_value = gate_up[:, FF:]
    sigmoid_gate = jax.nn.sigmoid(gate_value)
    inner_rows = (gate_value * sigmoid_gate * upper_value).astype(jnp.bfloat16)
    block_output = middle + jnp.dot(inner_rows, shrink_full, preferred_element_type=jnp.float32)
    gain_two, expand_full, shrink_full = (
        lax.all_gather(expand_gain, "shard", axis=0, tiled=True),
        lax.all_gather(expand_weight, "shard", axis=0, tiled=True),
        lax.all_gather(shrink_weight, "shard", axis=1, tiled=True),
    )
    cotangent_rows = block_cotangent.astype(jnp.float32)
    shrink_term = jnp.einsum(
        "tf,td->fd", inner_rows, block_cotangent, preferred_element_type=jnp.float32
    )
    inner_grad = jnp.einsum(
        "td,fd->tf", block_cotangent, shrink_full, preferred_element_type=jnp.float32
    )
    gate_grad = (
        inner_grad * upper_value * sigmoid_gate * (1.0 + gate_value * (1.0 - sigmoid_gate))
    ).astype(jnp.bfloat16)
    upper_grad = (inner_grad * gate_value * sigmoid_gate).astype(jnp.bfloat16)
    gate_up_grad = jnp.concatenate([gate_grad, upper_grad], axis=1)
    expand_term = jnp.einsum(
        "td,tf->df", hidden_two, gate_up_grad, preferred_element_type=jnp.float32
    )
    hidden_two_grad = jnp.einsum(
        "tf,df->td", gate_up_grad, expand_full, preferred_element_type=jnp.float32
    )
    gain_two_term = jnp.sum(hidden_two_grad * normed_two, axis=0)
    middle_grad = cotangent_rows + norm_back(
        hidden_two_grad * gain_two.astype(jnp.float32), normed_two, scale_two
    )
    gain_two_sum, expand_sum, shrink_sum = (
        lax.psum_scatter(gain_two_term, "shard", scatter_dimension=0, tiled=True),
        lax.psum_scatter(expand_term, "shard", scatter_dimension=0, tiled=True),
        lax.psum_scatter(shrink_term, "shard", scatter_dimension=1, tiled=True),
    )
    gain_one, joint_weight, out_weight = (
        lax.all_gather(attend_gain, "shard", axis=0, tiled=True),
        lax.all_gather(attend_weight, "shard", axis=0, tiled=True),
        lax.all_gather(output_weight, "shard", axis=1, tiled=True),
    )
    branch_grad = middle_grad.astype(jnp.bfloat16)
    output_term = jnp.einsum(
        "tq,td->qd", mixed_rows, branch_grad, preferred_element_type=jnp.float32
    )
    mixed_grad = jnp.einsum(
        "td,qd->tq", branch_grad, out_weight, preferred_element_type=jnp.float32
    ).astype(jnp.bfloat16)
    grad_heads = mixed_grad.reshape(row_count, HEADS, HEAD_DIM).transpose(1, 0, 2)

    def backward_head(element):
        query_head, key_head, value_head, grad_head, log_total = element
        weights = jnp.exp(head_scores(query_head, key_head) - log_total[:, None])
        prob_grad = jnp.einsum(
            "qd,wd->qw", grad_head, value_head, preferred_element_type=jnp.float32
        )
        row_total = jnp.sum(weights * prob_grad, axis=-1, keepdims=True)
        score_grad = (weights * (prob_grad - row_total)).astype(jnp.bfloat16)
        query_grad = (
            jnp.einsum("qw,wd->qd", score_grad, key_head, preferred_element_type=jnp.float32)
            * head_scale
        )
        key_grad = (
            jnp.einsum("qw,qd->wd", score_grad, query_head, preferred_element_type=jnp.float32)
            * head_scale
        )
        value_grad = jnp.einsum(
            "qw,qd->wd", weights.astype(jnp.bfloat16), grad_head, preferred_element_type=jnp.float32
        )
        return (query_grad, key_grad, value_grad)

    query_grads, key_grads, value_grads = lax.map(
        backward_head, (query_heads, key_heads, value_heads, grad_heads, log_totals)
    )
    key_sum = (
        jnp.sum(key_grads.reshape(KV_HEADS, group_size, window_rows, HEAD_DIM), axis=1)
        .transpose(1, 0, 2)
        .reshape(window_rows, KW)
    )
    value_sum = (
        jnp.sum(value_grads.reshape(KV_HEADS, group_size, window_rows, HEAD_DIM), axis=1)
        .transpose(1, 0, 2)
        .reshape(window_rows, KW)
    )
    pair_grads = jnp.concatenate([key_sum, value_sum], axis=1)
    own_grads = pair_grads[reach_count * row_count :]
    for distance in range(1, reach_count + 1):
        sent_rows = pair_grads[
            (reach_count - distance) * row_count : (reach_count - distance + 1) * row_count
        ]
        own_grads = own_grads + passed_along(sent_rows, "shard", -distance)
    query_raw = unrotate(query_grads.transpose(1, 0, 2), cosine_table, sine_table).reshape(
        row_count, QW
    )
    key_raw = unrotate(
        own_grads[:, :KW].reshape(row_count, KV_HEADS, HEAD_DIM), cosine_table, sine_table
    ).reshape(row_count, KW)
    joint_grad = jnp.concatenate([query_raw, key_raw, own_grads[:, KW:]], axis=1).astype(
        jnp.bfloat16
    )
    joint_term = jnp.einsum("td,tj->dj", hidden_one, joint_grad, preferred_element_type=jnp.float32)
    hidden_one_grad = jnp.einsum(
        "tj,dj->td", joint_grad, joint_weight, preferred_element_type=jnp.float32
    )
    gain_one_term = jnp.sum(hidden_one_grad * normed_one, axis=0)
    input_gradient = middle_grad + norm_back(
        hidden_one_grad * gain_one.astype(jnp.float32), normed_one, scale_one
    )
    gain_one_sum, joint_sum, output_sum = (
        lax.psum_scatter(gain_one_term, "shard", scatter_dimension=0, tiled=True),
        lax.psum_scatter(joint_term, "shard", scatter_dimension=0, tiled=True),
        lax.psum_scatter(output_term, "shard", scatter_dimension=1, tiled=True),
    )
    gain_one_sum, joint_sum, output_sum, gain_two_sum, expand_sum, shrink_sum = lax.psum(
        (gain_one_sum, joint_sum, output_sum, gain_two_sum, expand_sum, shrink_sum), "rep"
    )
    grad_scale = grad_factor * token_count ** (-0.5)
    first_gain = adam_step(
        attend_gain, gain_one_sum * grad_scale, attend_gain_first, attend_gain_second, 0.0
    )
    first_joint = adam_step(
        attend_weight, joint_sum * grad_scale, attend_weight_first, attend_weight_second, decay_rate
    )
    first_output = adam_step(
        output_weight,
        output_sum * grad_scale,
        output_weight_first,
        output_weight_second,
        decay_rate,
    )
    second_gain = adam_step(
        expand_gain, gain_two_sum * grad_scale, expand_gain_first, expand_gain_second, 0.0
    )
    second_expand = adam_step(
        expand_weight,
        expand_sum * grad_scale,
        expand_weight_first,
        expand_weight_second,
        decay_rate,
    )
    second_shrink = adam_step(
        shrink_weight,
        shrink_sum * grad_scale,
        shrink_weight_first,
        shrink_weight_second,
        decay_rate,
    )
    return (
        block_output,
        input_gradient,
        first_gain[0],
        first_joint[0],
        first_output[0],
        second_gain[0],
        second_expand[0],
        second_shrink[0],
        first_gain[1],
        first_joint[1],
        first_output[1],
        second_gain[1],
        second_expand[1],
        second_shrink[1],
        first_gain[2],
        first_joint[2],
        first_output[2],
        second_gain[2],
        second_expand[2],
        second_shrink[2],
        first_gain[4],
        first_joint[3],
        first_output[3],
        second_gain[4],
        second_expand[3],
        second_shrink[3],
    )


def solution(mesh):
    placed = (
        P(("rep", "shard"), None),
        P(("rep", "shard"), None),
        P("rep", None),
        P("shard"),
        P("shard", None),
        P(None, "shard"),
        P("shard"),
        P("shard", None),
        P(None, "shard"),
        P("shard"),
        P("shard", None),
        P(None, "shard"),
        P("shard"),
        P("shard", None),
        P(None, "shard"),
        P("shard"),
        P("shard", None),
        P(None, "shard"),
        P("shard"),
        P("shard", None),
        P(None, "shard"),
    )
    return jax.shard_map(
        shards,
        mesh=mesh,
        in_specs=placed,
        out_specs=(
            P(("rep", "shard"), None),
            P(("rep", "shard"), None),
            P("shard"),
            P("shard", None),
            P(None, "shard"),
            P("shard"),
            P("shard", None),
            P(None, "shard"),
            P("shard"),
            P("shard", None),
            P(None, "shard"),
            P("shard"),
            P("shard", None),
            P(None, "shard"),
            P("shard"),
            P("shard", None),
            P(None, "shard"),
            P("shard"),
            P("shard", None),
            P(None, "shard"),
            P("shard"),
            P("shard", None),
            P(None, "shard"),
            P("shard"),
            P("shard", None),
            P(None, "shard"),
        ),
        check_vma=False,
    )
```

profile of v0, /device:TPU:0, one launch (start us, length us, event | category | flops | bytes accessed | tf_op | source)
XLA Modules:
  0.0 1244.7 jit_solution(8630276343134944831)
XLA Ops:
  14.3 18.6 %all-reduce.8 = (bf16[960]{0:T(1024)(128)(2,1)S(1)}, bf16[960]{0:T(1024)(128)(2,1)S(1)}) all-reduce(bf16[960]{0:T(1024)(128)(2,1)S(1)} %dynamic-update-slice, bf16[960]{0:T(1024)(128)(2,1)S(1)} %dynamic-update-slice.1), channel_id=1, replica_groups=mesh['rep'=4,'shard'=8] {'shard'}, use_global_device_ids=true, to_apply=%add | all-reduce | flops 1920 | bytes 7680
  35.1 16.2 %all-gather.5.cloned.1.call-done = bf16[960,1600]{1,0:T(8,128)(2,1)} async-done(((bf16[120,1600]{1,0:T(8,128)(2,1)}), bf16[960,1600]{1,0:T(8,128)(2,1)}) %all-gather.5.cloned.1.call-update) | async-done | bytes 3072016 | tf_op jit(solution)/shard_map/all_gather | solution.py:125
  51.3 4.0 fusion.77
  72.2 16.7 %collective-permute-done = bf16[512,640]{0,1:T(8,128)(2,1)S(1)} collective-permute-done((bf16[512,640]{0,1:T(8,128)(2,1)S(1)}, bf16[512,640]{0,1:T(8,128)(2,1)S(1)}, u32[]{:S(2)}, u32[]{:S(2)}) %collective-permute-start) | collective-permute-done | bytes 655392 | tf_op jit(solution)/shard_map/ppermute | solution.py:30
  88.9 15.6 %collective-permute-done.1 = bf16[512,640]{0,1:T(8,128)(2,1)} collective-permute-done((bf16[512,640]{0,1:T(8,128)(2,1)S(1)}, bf16[512,640]{0,1:T(8,128)(2,1)}, u32[]{:S(2)}, u32[]{:S(2)}) %collective-permute-start.1) | collective-permute-done | bytes 655392 | tf_op jit(solution)/shard_map/ppermute | solution.py:30
  105.6 12.9 %collective-permute-done.2 = bf16[512,640]{0,1:T(8,128)(2,1)} collective-permute-done((bf16[512,640]{0,1:T(8,128)(2,1)S(1)}, bf16[512,640]{0,1:T(8,128)(2,1)}, u32[]{:S(2)}, u32[]{:S(2)}) %collective-permute-start.2) | collective-permute-done | bytes 655392 | tf_op jit(solution)/shard_map/ppermute | solution.py:30
  123.0 3.3 copy.58
  126.3 4.5 copy.59
  130.8 7.5 broadcast_in_dim.64
  138.4 5.7 broadcast_in_dim.40
  144.1 95.7 %while.28 = (s32[]{:T(128)}, bf16[15,512,64]{1,2,0:T(8,128)(2,1)}, f32[15,512]{1,0:T(8,128)S(1)}, bf16[15,512,64]{2,1,0:T(8,128)(2,1)}, bf16[15,2560,64]{2,1,0:T...) while((s32[]{:T(128)}, bf16[15,512,64]{1,2,0:T(8,128)(2,1)}, ...), condition=%wide.region_6.7_spmd.clone, body=%wide.region_3.6_spmd.clone.sunk | while | flops 349994496 | bytes 17272952 | solution.py:177
  242.9 13.0 %fusion.83 = f32[512,5120]{1,0:T(8,128)} fusion(bf16[960,5120]{1,0:T(8,128)(2,1)} %all-gather.9.cloned.1.call-done, f32[512,960]{0,1:T(8,128)S(1)} %get-tuple-element.344, f32[960]{0:T(1024)S(1)} %convert_element_type.86, f32[512]{0:T(512)S(1)} %add_rsqrt_fusion), kind=kOutput, calls=%fused_computation.175 | convolution fusion | flops 5034639360 | bytes 22288128 | tf_op jit(solution)/shard_map/dot_general | solution.py:188
  256.0 27.1 %all-gather.11.cloned.1.call-done = bf16[2560,960]{0,1:T(8,128)(2,1)} async-done(((bf16[2560,120]{0,1:T(8,128)(2,1)}), bf16[2560,960]{0,1:T(8,128)(2,1)}) %all-gather.11.cloned.1.call-update) | async-done | bytes 4915216 | tf_op jit(solution)/shard_map/all_gather | solution.py:183
  283.0 10.6 multiply_convert_fusion.2
  293.7 5.5 multiply_reduce_fusion.1
  308.5 183.4 %while.29 = (s32[]{:T(128)}, f32[15,512,64]{1,2,0:T(8,128)}, f32[15,2560,64]{1,2,0:T(8,128)}, f32[15,2560,64]{1,2,0:T(8,128)}, bf16[15,512,64]{2,1,0:T(8,128)(2,...) while((s32[]{:T(128)}, f32[15,512,64]{1,2,0:T(8,128)}, ...), condition=%wide.region_11.12_spmd.clone, body=%wide.region_9.11_spmd.clone.sunk | while | flops 854785536 | bytes 43283592 | solution.py:261
  310.7 3.2 multiply_reduce_fusion.5
  322.8 3.2 multiply_reduce_fusion.5
  335.1 3.2 multiply_reduce_fusion.5
  347.3 3.2 multiply_reduce_fusion.5
  359.5 3.2 multiply_reduce_fusion.5
  371.7 3.2 multiply_reduce_fusion.5
  383.9 3.2 multiply_reduce_fusion.5
  396.1 3.2 multiply_reduce_fusion.5
  408.4 3.2 multiply_reduce_fusion.5
  420.6 3.2 multiply_reduce_fusion.5
  432.8 3.2 multiply_reduce_fusion.5
  445.0 3.2 multiply_reduce_fusion.5
  457.2 3.2 multiply_reduce_fusion.5
  469.4 3.2 multiply_reduce_fusion.5
  481.6 3.2 multiply_reduce_fusion.5
  491.9 5.1 reduce_sum.104
  497.0 6.8 reduce_sum.103
  511.9 73.8 %collective-permute-done.5 = f32[512,640]{0,1:T(8,128)S(1)} collective-permute-done((f32[512,640]{0,1:T(8,128)S(1)}, f32[512,640]{0,1:T(8,128)S(1)}, u32[]{:S(2)}, u32[]{:S(2)}) %collective-permute-start.5) | collective-permute-done | bytes 1310752 | tf_op jit(solution)/shard_map/ppermute | solution.py:30
  585.6 122.4 %collective-permute-done.7 = f32[512,640]{0,1:T(8,128)S(1)} collective-permute-done((f32[512,640]{0,1:T(8,128)S(1)}, f32[512,640]{0,1:T(8,128)S(1)}, u32[]{:S(2)}, u32[]{:S(2)}) %collective-permute-start.7) | collective-permute-done | bytes 1310752 | tf_op jit(solution)/shard_map/ppermute | solution.py:30
  710.1 4.7 fusion.70
  715.9 7.2 fusion.87
  724.7 12.3 fusion.43
  739.1 59.9 %reduce-scatter.15.cloned.1.call-done = f32[120,1600]{1,0:T(8,128)} async-done(((f32[960,1600]{1,0:T(8,128)}), f32[120,1600]{1,0:T(8,128)}) %reduce-scatter.15.cloned.1.call-update) | async-done | bytes 768016
  799.0 104.0 %reduce-scatter.11.cloned.1.call-done = f32[2560,120]{0,1:T(8,128)} async-done(((f32[2560,960]{0,1:T(8,128)}), f32[2560,120]{0,1:T(8,128)}) %reduce-scatter.11.cloned.1.call-update) | async-done | bytes 1228816 | tf_op jit(solution)/shard_map/reduce_scatter | solution.py:224
  903.1 196.1 %reduce-scatter.9.cloned.1.call-done = f32[120,5120]{1,0:T(8,128)} async-done(((f32[960,5120]{1,0:T(8,128)}), f32[120,5120]{1,0:T(8,128)}) %reduce-scatter.9.cloned.1.call-update) | async-done | bytes 2457616 | tf_op jit(solution)/shard_map/reduce_scatter | solution.py:223
  1099.9 7.3 convolution_add_fusion
  1107.3 3.3 fusion.56
  1110.6 13.9 %all-reduce.5 = (f32[960]{0:T(1024)S(1)}, f32[960]{0:T(1024)S(1)}) all-reduce(f32[960]{0:T(1024)S(1)} %get-tuple-element.240, f32[960]{0:T(1024)S(1)} %get-tuple-element.238), channel_id=2, replica_groups=mesh['rep'=4,'shard'=8] {'shard'}, use_global_device_ids=true, to_apply=%region_16.17.clone | all-reduce | flops 1920 | bytes 15360
  1124.7 10.4 all-reduce.6
  1135.8 3.3 fusion.55
  1139.1 81.4 %all-reduce.11.cloned.1.call-done = (f32[120,1600]{1,0:T(8,128)}, f32[960,120]{1,0:T(8,128)}, f32[120,5120]{1,0:T(8,128)}, f32[2560,120]{0,1:T(8,128)}) async-done(((f32[120,1600]{1,0:T(8,128)}, f32[960,120]{1,0:T(8,128)}, f32[120,5120]{1,0:T(8,128)}, f32[2560,120]{0,1:T(8,128)}), (f32[120,1600]{1,0:T(8,128)}, f32[960,120]{1,0:T(8,128)}, f32[120,5120]{1,0:T(8,128)}, ...) | async-done | bytes 4915216 | tf_op jit(solution)/shard_map/psum | solution.py:303
  1232.1 5.5 convert_add_fusion
  (353 shorter events, 300.1 us)
Async XLA Ops:
  7.2 27.3 %copy-start.7 = (bf16[512,960]{0,1:T(8,128)(2,1)S(1)}, bf16[512,960]{0,1:T(8,128)(2,1)}, u32[]{:S(2)}) copy-start(bf16[512,960]{0,1:T(8,128)(2,1)} %param.25) | copy-start | bytes 2949124
  7.2 44.1 %all-gather.5.cloned.1.call-start = ((), (), s32[]{:S(2)}) async-start(), calls=%async_computation.4 | async-start | bytes 3594240 | tf_op jit(solution)/shard_map/all_gather | solution.py:125
  7.9 231.9 %all-gather.7.cloned.1.call-start = ((), (), s32[]{:S(2)}) async-start(), calls=%async_computation.5 | async-start | bytes 2211840 | tf_op jit(solution)/shard_map/all_gather | solution.py:126
  9.8 233.1 %all-gather.9.cloned.1.call-start = ((), (), s32[]{:S(2)}) async-start(), calls=%async_computation.6 | async-start | bytes 11059200 | tf_op jit(solution)/shard_map/all_gather | solution.py:182
  10.5 272.5 %all-gather.11.cloned.1.call-start = ((), (), s32[]{:S(2)}) async-start(), calls=%async_computation.7 | async-start | bytes 5529600 | tf_op jit(solution)/shard_map/all_gather | solution.py:183
  32.9 18.5 %copy-start.35 = (f32[960]{0:T(1024)}, f32[960]{0:T(1024)S(1)}, u32[]{:S(2)}) copy-start(f32[960]{0:T(1024)S(1)} %convert_element_type.82) | copy-start | bytes 11524
  34.8 16.6 %copy-start.37 = (f32[512]{0:T(512)}, f32[512]{0:T(512)S(1)}, u32[]{:S(2)}) copy-start(f32[512]{0:T(512)S(1)} %add_rsqrt_fusion.1) | copy-start | bytes 6148
  35.1 34.9 %copy-start.17 = (f32[512,32]{0,1:T(8,128)}, f32[512,32]{0,1:T(8,128)S(1)}, u32[]{:S(2)}) copy-start(f32[512,32]{0,1:T(8,128)S(1)} %get-tuple-element.339) | copy-start | bytes 196612
  35.1 34.9 %copy-start.19 = (f32[512,32]{0,1:T(8,128)}, f32[512,32]{0,1:T(8,128)S(1)}, u32[]{:S(2)}) copy-start(f32[512,32]{0,1:T(8,128)S(1)} %get-tuple-element.340) | copy-start | bytes 196612
  57.0 31.9 %collective-permute-start = (bf16[512,640]{0,1:T(8,128)(2,1)S(1)}, bf16[512,640]{0,1:T(8,128)(2,1)S(1)}, u32[]{:S(2)}, u32[]{:S(2)}) collective-permute-start(bf16[512,640]{0,1:T(8,128)(2,1)S(1)} %pad_maximum_fusion.8), channel_id=1, source_target_pairs={{0,4},{1,5},{2,6},{3,7},{8,12},{9,13},{10,14},{11,15},{16,20},{17,... | collective-permute-start | bytes 1966088 | tf_op jit(solution)/shard_map/ppermute | solution.py:30
  60.3 676.8 %reduce-scatter.13.cloned.1.call-start = ((), (), s32[]{:S(2)}) async-start(), calls=%async_computation.10 | async-start | bytes 4423680
  60.4 44.1 %collective-permute-start.1 = (bf16[512,640]{0,1:T(8,128)(2,1)S(1)}, bf16[512,640]{0,1:T(8,128)(2,1)}, u32[]{:S(2)}, u32[]{:S(2)}) collective-permute-start(bf16[512,640]{0,1:T(8,128)(2,1)S(1)} %pad_maximum_fusion.8), channel_id=1, source_target_pairs={{0,3},{1,4},{2,5},{3,6},{4,7},{8,11},{9,12},{10,13},{11,14},{12,15... | collective-permute-start | bytes 1966088 | tf_op jit(solution)/shard_map/ppermute | solution.py:30
  65.0 54.7 %collective-permute-start.3 = (bf16[512,640]{0,1:T(8,128)(2,1)S(1)}, bf16[512,640]{0,1:T(8,128)(2,1)}, u32[]{:S(2)}, u32[]{:S(2)}) collective-permute-start(bf16[512,640]{0,1:T(8,128)(2,1)S(1)} %pad_maximum_fusion.8), channel_id=1, source_target_pairs={{0,1},{1,2},{2,3},{3,4},{4,5},{5,6},{6,7},{8,9},{9,10},{10,11},{11... | collective-permute-start | bytes 1966088 | tf_op jit(solution)/shard_map/ppermute | solution.py:30
  67.2 51.4 %collective-permute-start.2 = (bf16[512,640]{0,1:T(8,128)(2,1)S(1)}, bf16[512,640]{0,1:T(8,128)(2,1)}, u32[]{:S(2)}, u32[]{:S(2)}) collective-permute-start(bf16[512,640]{0,1:T(8,128)(2,1)S(1)} %pad_maximum_fusion.8), channel_id=1, source_target_pairs={{0,2},{1,3},{2,4},{3,5},{4,6},{5,7},{8,10},{9,11},{10,12},{11,13},... | collective-permute-start | bytes 1966088 | tf_op jit(solution)/shard_map/ppermute | solution.py:30
  144.1 95.8 %copy-start.8 = (bf16[512,960]{0,1:T(8,128)(2,1)S(1)}, bf16[512,960]{0,1:T(8,128)(2,1)}, u32[]{:S(2)}) copy-start(bf16[512,960]{0,1:T(8,128)(2,1)} %param.25) | copy-start | bytes 2949124
  242.9 50.8 %copy-start.4 = (f32[512,960]{0,1:T(8,128)}, f32[512,960]{0,1:T(8,128)S(1)}, u32[]{:S(2)}) copy-start(f32[512,960]{0,1:T(8,128)S(1)} %get-tuple-element.344) | copy-start | bytes 5898244
  242.9 40.1 %copy-start.26 = (bf16[512,960]{0,1:T(8,128)(2,1)S(1)}, bf16[512,960]{0,1:T(8,128)(2,1)}, u32[]{:S(2)}) copy-start(bf16[512,960]{0,1:T(8,128)(2,1)} %param.26) | copy-start | bytes 2949124
  283.0 10.7 copy-start.3
  293.7 5.5 copy-start.46
  293.7 5.5 copy-start.47
  308.5 490.6 %reduce-scatter.15.cloned.1.call-start = ((), (), s32[]{:S(2)}) async-start(), calls=%async_computation.11 | async-start | bytes 7188480
  503.7 7.6 copy-start.16
  503.7 7.7 copy-start.18
  503.7 7.7 copy-start.20
  506.2 5.7 collective-permute-start.4
  507.5 78.2 %collective-permute-start.5 = (f32[512,640]{0,1:T(8,128)S(1)}, f32[512,640]{0,1:T(8,128)S(1)}, u32[]{:S(2)}, u32[]{:S(2)}) collective-permute-start(f32[512,640]{0,1:T(8,128)S(1)} %get-tuple-element.326), channel_id=1, source_target_pairs={{2,0},{3,1},{4,2},{5,3},{6,4},{7,5},{10,8},{11,9},{12,10},{13,11},... | collective-permute-start | bytes 3932168 | tf_op jit(solution)/shard_map/ppermute | solution.py:30
  508.8 199.3 %collective-permute-start.7 = (f32[512,640]{0,1:T(8,128)S(1)}, f32[512,640]{0,1:T(8,128)S(1)}, u32[]{:S(2)}, u32[]{:S(2)}) collective-permute-start(f32[512,640]{0,1:T(8,128)S(1)} %get-tuple-element.327), channel_id=1, source_target_pairs={{4,0},{5,1},{6,2},{7,3},{12,8},{13,9},{14,10},{15,11},{20,16},{21,... | collective-permute-start | bytes 3932168 | tf_op jit(solution)/shard_map/ppermute | solution.py:30
  510.1 198.0 %collective-permute-start.6 = (f32[512,640]{0,1:T(8,128)S(1)}, f32[512,640]{0,1:T(8,128)S(1)}, u32[]{:S(2)}, u32[]{:S(2)}) collective-permute-start(f32[512,640]{0,1:T(8,128)S(1)} %get-tuple-element.328), channel_id=1, source_target_pairs={{3,0},{4,1},{5,2},{6,3},{7,4},{11,8},{12,9},{13,10},{14,11},{15,12... | collective-permute-start | bytes 3932168 | tf_op jit(solution)/shard_map/ppermute | solution.py:30
  511.4 196.7 %copy-start = (f32[5,2560,64]{1,2,0:T(8,128)S(1)}, f32[5,2560,64]{1,2,0:T(8,128)}, u32[]{:S(2)}) copy-start(f32[5,2560,64]{1,2,0:T(8,128)} %reduce_sum.103) | copy-start | bytes 9830404
  511.8 197.3 %copy-start.28 = (bf16[512,15,64]{0,2,1:T(8,128)(2,1)}, bf16[512,15,64]{0,2,1:T(8,128)(2,1)S(1)}, u32[]{:S(2)}) copy-start(bf16[512,15,64]{0,2,1:T(8,128)(2,1)S(1)} %pad_maximum_fusion.5) | copy-start | bytes 2949124
  714.8 188.3 %reduce-scatter.11.cloned.1.call-start = ((), (), s32[]{:S(2)}) async-start(), calls=%async_computation.9 | async-start | bytes 11059200 | tf_op jit(solution)/shard_map/reduce_scatter | solution.py:224
  723.1 376.1 %reduce-scatter.9.cloned.1.call-start = ((), (), s32[]{:S(2)}) async-start(), calls=%async_computation.8 | async-start | bytes 22118400 | tf_op jit(solution)/shard_map/reduce_scatter | solution.py:223
  737.0 483.5 %all-reduce.11.cloned.1.call-start = ((), (), s32[]{:S(2)}) async-start(), calls=%async_computation.12 | async-start | bytes 9953280 | tf_op jit(solution)/shard_map/psum | solution.py:303
  1099.9 7.4 copy-start.29
  1099.9 7.4 copy-start.34
  1099.9 7.3 copy-start.45
  1107.2 27.9 %copy-start.39 = (bf16[120]{0:T(256)(128)(2,1)S(1)}, bf16[120]{0:T(256)(128)(2,1)}, u32[]{:S(2)}) copy-start(bf16[120]{0:T(256)(128)(2,1)} %param.28) | copy-start | bytes 724
  1107.3 27.9 %copy-start.40 = (bf16[120]{0:T(256)(128)(2,1)S(1)}, bf16[120]{0:T(256)(128)(2,1)}, u32[]{:S(2)}) copy-start(bf16[120]{0:T(256)(128)(2,1)} %param.31) | copy-start | bytes 724
  1107.3 27.9 %copy-start.41 = (f32[120]{0:T(128)S(1)}, f32[120]{0:T(128)}, u32[]{:S(2)}) copy-start(f32[120]{0:T(128)} %param.43) | copy-start | bytes 1444
  1107.3 27.9 %copy-start.42 = (f32[120]{0:T(128)S(1)}, f32[120]{0:T(128)}, u32[]{:S(2)}) copy-start(f32[120]{0:T(128)} %param.37) | copy-start | bytes 1444
  1107.3 27.9 %copy-start.43 = (f32[120]{0:T(128)S(1)}, f32[120]{0:T(128)}, u32[]{:S(2)}) copy-start(f32[120]{0:T(128)} %param.40) | copy-start | bytes 1444
  1107.3 27.9 %copy-start.44 = (f32[120]{0:T(128)S(1)}, f32[120]{0:T(128)}, u32[]{:S(2)}) copy-start(f32[120]{0:T(128)} %param.34) | copy-start | bytes 1444
  1107.3 28.4 %copy-start.2 = (f32[512,960]{0,1:T(8,128)S(1)}, f32[512,960]{0,1:T(8,128)}, u32[]{:S(2)}) copy-start(f32[512,960]{0,1:T(8,128)} %copy-done.1) | copy-start | bytes 5898244
  1135.8 84.7 %copy-start.25 = (bf16[960,120]{1,0:T(8,128)(2,1)S(1)}, bf16[960,120]{1,0:T(8,128)(2,1)}, u32[]{:S(2)}) copy-start(bf16[960,120]{1,0:T(8,128)(2,1)} %param.30) | copy-start | bytes 691204
  1139.1 84.3 %copy-start.21 = (bf16[120,1600]{1,0:T(8,128)(2,1)S(1)}, bf16[120,1600]{1,0:T(8,128)(2,1)}, u32[]{:S(2)}) copy-start(bf16[120,1600]{1,0:T(8,128)(2,1)} %param.29) | copy-start | bytes 1152004
  1139.1 84.3 %copy-start.30 = (f32[120,1600]{1,0:T(8,128)S(1)}, f32[120,1600]{1,0:T(8,128)}, u32[]{:S(2)}) copy-start(f32[120,1600]{1,0:T(8,128)} %param.41) | copy-start | bytes 2304004
  1139.1 84.3 %copy-start.31 = (f32[120,1600]{1,0:T(8,128)S(1)}, f32[120,1600]{1,0:T(8,128)}, u32[]{:S(2)}) copy-start(f32[120,1600]{1,0:T(8,128)} %param.35) | copy-start | bytes 2304004
  1226.8 5.3 copy-start.15
  (17 other events, 38.8 us)
Sparse Core Ops, SparseCore 0:
  9.7 41.5 all-gather.4
  53.5 40.1 all-gather.6
  95.4 109.6 all-gather.8
  206.5 76.4 all-gather.10
  308.6 118.8 reduce-scatter.12
  714.9 84.0 reduce-scatter.14
  801.5 101.5 reduce-scatter.10
  905.4 193.7 reduce-scatter.8
  1104.1 116.3 all-reduce.10
where the time goes:
time: 1250 us; the launch traced here: 1240 us
  waiting for transfers between devices  728 us (58%)
  matrix products  334 us (27%)
  other arithmetic  58.8 us (5%)
  local copies, waits for them, and re-layouts  47.4 us (4%)
  blocking collectives  43 us (3%)
  starting transfers between devices  16.7 us (1%)
  between operations  16.5 us (1%)
    ppermute x8, waiting for transfers between devices, passed_along(): return lax.ppermute(block, axis, route)  241 us
    reduce_scatter x1, waiting for transfers between devices, shards(): lax.psum_scatter(expand_term, 'shard', scatter_dimension=0, tiled=True)  196 us
    reduce_scatter x1, waiting for transfers between devices, shards(): lax.psum_scatter(shrink_term, 'shard', scatter_dimension=1, tiled=True)  104 us
    dot_general x30, matrix products, head_scores(): jnp.einsum('qd,wd->qw', query_head, key_head, preferred_element_type=jnp....  87.2 us
    psum x1, waiting for transfers between devices, shards(): lax.psum((gain_one_sum, joint_sum, output_sum, gain_two_sum, expand_sum,...  81.4 us
    unnamed x11, waiting for transfers between devices  61.4 us
    dot_general x15, matrix products, forward_head(): jnp.einsum('qw,wd->qd', probs_low, value_head, preferred_element_type=jnp...  43.4 us
    dot_general x15, matrix products, backward_head(): jnp.einsum('qw,wd->qd', score_grad, key_head, preferred_element_type=jnp....  40 us
  transfers between devices with their start and end apart: 17, of which 11 were waited for; matrix products, arithmetic and copies ran while one was open for 32% of the time, Pallas kernels for 0%

commit v1 on v0

v1 whole, which is shorter than its diff:
```python
import functools
import math

import jax
import jax.numpy as jnp
from jax import lax
from jax.experimental import pallas as pl
from jax.experimental.pallas import tpu as pltpu
from jax.sharding import PartitionSpec as P

HEADS = 15
KV_HEADS = 5
HEAD_DIM = 64
GROUP = HEADS // KV_HEADS
FF = 2560
MAXLEN = 2048
STEP = 10
QW = 960
KW = 320
JW = QW + 2 * KW
D = 960

eps_norm = 1e-05
rope_base = 100000.0
beta_one = 0.9
beta_two = 0.95
adam_eps = 1e-08
learn_rate = 0.05
decay_rate = 0.1
grad_factor = 4.0

F32 = jnp.float32
BF = jnp.bfloat16
MESH = pl.DeviceIdType.MESH
ANY = pl.ANY
VMEM = pltpu.VMEM
DMA = pltpu.SemaphoreType.DMA

QC = 256
KB = 768
HALF = 64
ONES = 112
NEG = -1e30
EXP_SCALE = HEAD_DIM**-0.5 * math.log2(math.e)
BIG_VMEM = 60 * 2**20


def dot(a, b, ca=1, cb=0):
    return lax.dot_general(a, b, (((ca,), (cb,)), ((), ())), preferred_element_type=F32)


def causal_tile():
    key = lax.broadcasted_iota(jnp.int32, (QC, QC), 0)
    query = lax.broadcasted_iota(jnp.int32, (QC, QC), 1)
    return key <= query


def mask_last(scores, causal):
    last = jnp.where(causal, scores[KB - QC :], NEG)
    return jnp.concatenate([scores[: KB - QC], last], axis=0)


def attend_forward_kernel(
    kv_ref, feat_ref, qt_ref, qfeat_ref, mixed_ref, lse_ref, kvf, vt, qa, sb
):
    blocks, kv_heads, rows, lanes = kv_ref.shape
    window = blocks * rows
    tokens = qt_ref.shape[1]
    span = window - (tokens - QC)
    steps = span // KB
    kvf[:, lanes:] = feat_ref[...]
    qa[HALF:lanes, :] = jnp.zeros((HALF, tokens), BF)
    qa[lanes:, :] = qfeat_ref[...]
    vt[HALF:, :] = jnp.ones((vt.shape[0] - HALF, window), BF)
    causal = causal_tile()

    def key_head(j, _):
        for block in range(blocks):
            part = kv_ref[block, j]
            kvf[block * rows : (block + 1) * rows, :lanes] = part
            vt[:HALF, block * rows : (block + 1) * rows] = part.T[HALF:, :]

        def head(g, _):
            h = j * GROUP + g
            row = pl.multiple_of(h * HEAD_DIM, HEAD_DIM)
            qa[:HALF, :] = qt_ref[pl.ds(row, HEAD_DIM), :]
            tops = []
            for chunk in range(tokens // QC):
                low = chunk * QC
                highest = None
                for b in range(steps):
                    first = low + b * KB
                    s = dot(kvf[first : first + KB, :], qa[:, low : low + QC])
                    if b == steps - 1:
                        s = mask_last(s, causal)
                    sb[chunk, b * KB : (b + 1) * KB, :] = s
                    peak = jnp.max(s.reshape(KB // 8, 8, QC), axis=0)
                    highest = peak if highest is None else jnp.maximum(highest, peak)
                tops.append(jnp.max(highest, axis=0, keepdims=True))
            for chunk in range(tokens // QC):
                low = chunk * QC
                shift = tops[chunk] * EXP_SCALE
                total = None
                for b in range(steps):
                    first = low + b * KB
                    s = sb[chunk, b * KB : (b + 1) * KB, :]
                    p = jnp.exp2(s * EXP_SCALE - shift).astype(BF)
                    term = dot(vt[:, first : first + KB], p)
                    total = term if total is None else total + term
                weight = total[HALF : HALF + 1, :]
                mixed_ref[pl.ds(row, HEAD_DIM), low : low + QC] = (
                    total[:HALF, :] * (1.0 / weight)
                ).astype(BF)
                lse_ref[pl.ds(h, 1), :, low : low + QC] = (
                    tops[chunk] * HEAD_DIM**-0.5 + jnp.log(weight)
                )[None]
            return 0

        lax.fori_loop(0, GROUP, head, 0)
        return 0

    lax.fori_loop(0, kv_heads, key_head, 0)


def attend_forward(window, feat, qt, qfeat):
    blocks, kv_heads, rows, lanes = window.shape
    keys = blocks * rows
    tokens = qt.shape[1]
    span = keys - (tokens - QC)
    return pl.pallas_call(
        attend_forward_kernel,
        out_shape=(
            jax.ShapeDtypeStruct(qt.shape, BF),
            jax.ShapeDtypeStruct((HEADS, 1, tokens), F32),
        ),
        scratch_shapes=[
            VMEM((keys, 2 * lanes), BF),
            VMEM((HALF + 16, keys), BF),
            VMEM((2 * lanes, tokens), BF),
            VMEM((tokens // QC, span, QC), F32),
        ],
        compiler_params=pltpu.CompilerParams(vmem_limit_bytes=BIG_VMEM),
        name="attend_forward",
    )(window, feat, qt, qfeat)


def three_parts(value, rows):
    one = value.astype(BF).astype(F32)
    two = (value - one).astype(BF).astype(F32)
    three = value - one - two
    shape = (rows, value.shape[1])
    place = lax.broadcasted_iota(jnp.int32, shape, 0)
    parts = [jnp.broadcast_to(part, shape) for part in (one, two, three)]
    chosen = jnp.where(
        place == 0, parts[0], jnp.where(place == 1, parts[1], jnp.where(place == 2, parts[2], 0.0))
    )
    return chosen.astype(BF)


def attend_backward_kernel(
    kv_ref,
    feat_ref,
    qt_ref,
    qfeat_ref,
    gradt_ref,
    mixed_ref,
    lse_ref,
    dq_ref,
    dkv_ref,
    kvf,
    kt,
    qa,
    da,
    acc,
    rhs,
):
    blocks, kv_heads, rows, lanes = kv_ref.shape
    window = blocks * rows
    tokens = qt_ref.shape[1]
    span = window - (tokens - QC)
    steps = span // KB
    kvf[:, lanes:] = feat_ref[...]
    qa[HALF:lanes, :] = jnp.zeros((HALF, tokens), BF)
    da[...] = jnp.zeros_like(da)
    rhs[...] = jnp.zeros_like(rhs)
    causal = causal_tile()
    extra = lanes - ONES

    def key_head(j, _):
        for block in range(blocks):
            part = kv_ref[block, j]
            kvf[block * rows : (block + 1) * rows, :lanes] = part
            kt[:, block * rows : (block + 1) * rows] = part.T[:HALF, :]
        acc[...] = jnp.zeros_like(acc)

        def head(g, _):
            h = j * GROUP + g
            row = pl.multiple_of(h * HEAD_DIM, HEAD_DIM)
            q = qt_ref[pl.ds(row, HEAD_DIM), :]
            grad = gradt_ref[pl.ds(row, HEAD_DIM), :]
            qa[:HALF, :] = q
            da[HALF:lanes, :] = grad
            mixed = mixed_ref[pl.ds(row, HEAD_DIM), :].astype(F32)
            row_total = jnp.sum(grad.astype(F32) * mixed, axis=0, keepdims=True)
            lse = lse_ref[pl.ds(h, 1), :, :][0]
            qa[lanes : lanes + ONES, :] = qfeat_ref[:ONES, :]
            qa[lanes + ONES :, :] = three_parts(-(HEAD_DIM**0.5) * lse, extra)
            da[lanes + ONES :, :] = three_parts(-row_total, extra)
            query_grads = [None] * (tokens // QC)
            for chunk in range(tokens // QC):
                low = chunk * QC
                rhs[chunk, :HALF, :QC] = q[:, low : low + QC]
                rhs[chunk, HALF:, QC:] = grad[:, low : low + QC]
            for b in range(steps):
                for chunk in range(tokens // QC):
                    low = chunk * QC
                    first = low + b * KB
                    keys = kvf[first : first + KB, :]
                    s = dot(keys, qa[:, low : low + QC])
                    if b == steps - 1:
                        s = mask_last(s, causal)
                    p = jnp.exp2(s * EXP_SCALE)
                    dp = dot(keys, da[:, low : low + QC])
                    ds = (p * dp).astype(BF)
                    both = jnp.concatenate([ds, p.astype(BF)], axis=1)
                    acc[first : first + KB, :] += dot(both, rhs[chunk], 1, 1)
                    term = dot(kt[:, first : first + KB], ds)
                    old = query_grads[chunk]
                    query_grads[chunk] = term if old is None else old + term
            for chunk in range(tokens // QC):
                low = chunk * QC
                dq_ref[pl.ds(row, HEAD_DIM), low : low + QC] = query_grads[chunk] * HEAD_DIM**-0.5
            return 0

        lax.fori_loop(0, GROUP, head, 0)
        lane = lax.broadcasted_iota(jnp.int32, (1, lanes), 1)
        factor = jnp.where(lane < HALF, HEAD_DIM**-0.5, 1.0)
        for block in range(blocks):
            part = acc[block * rows : (block + 1) * rows, :]
            dkv_ref[block, j] = (part * factor).astype(dkv_ref.dtype)
        return 0

    lax.fori_loop(0, kv_heads, key_head, 0)


def attend_backward(window, feat, qt, qfeat, gradt, mixed, lse):
    blocks, kv_heads, rows, lanes = window.shape
    keys = blocks * rows
    tokens = qt.shape[1]
    return pl.pallas_call(
        attend_backward_kernel,
        out_shape=(
            jax.ShapeDtypeStruct(qt.shape, F32),
            jax.ShapeDtypeStruct(window.shape, BF),
        ),
        scratch_shapes=[
            VMEM((keys, 2 * lanes), BF),
            VMEM((HALF, keys), BF),
            VMEM((2 * lanes, tokens), BF),
            VMEM((2 * lanes, tokens), BF),
            VMEM((keys, lanes), F32),
            VMEM((tokens // QC, lanes, 2 * QC), BF),
        ],
        compiler_params=pltpu.CompilerParams(vmem_limit_bytes=BIG_VMEM),
        name="attend_backward",
    )(window, feat, qt, qfeat, gradt, mixed, lse)


class Place:
    def __init__(self):
        self.r = lax.axis_index("rep")
        self.s = lax.axis_index("shard")
        self.x, self.y = lax.rem(self.r, 2), self.r // 2
        self.z, self.c = self.s // 2, lax.rem(self.s, 2)
        self.rx = self.y * 2 + (1 - self.x)
        self.ry = (1 - self.y) * 2 + self.x
        self.rd = 3 - self.r
        self.x_side = (self.rx, self.s)
        self.y_side = (self.ry, self.s)
        self.core_side = (self.r, self.z * 2 + (1 - self.c))

    def z_to(self, k):
        return lax.rem(self.z + k, 4)

    def z_from(self, k):
        return lax.rem(self.z + 4 - k, 4)

    def z_side(self, k):
        return (self.r, self.z_to(k) * 2 + self.c)


def greet(devices):
    barrier = pltpu.get_barrier_semaphore()
    for device in devices:
        pl.semaphore_signal(barrier, inc=1, device_id=device, device_id_type=MESH)
    pl.semaphore_wait(barrier, len(devices))


def remote(src, dst, send, recv, device):
    return pltpu.make_async_remote_copy(
        src_ref=src, dst_ref=dst, send_sem=send, recv_sem=recv, device_id=device, device_id_type=MESH
    )


def gather_kernel(own_ref, full_ref, local_sem, send, recv):
    rows = own_ref.shape[0]
    quarter, half = rows // 4, rows // 8
    at = Place()
    greet([at.x_side, at.y_side, at.core_side] + [at.z_side(k) for k in (1, 2, 3)])

    def piece(plane, owner, part=None):
        start = owner * quarter + (0 if part is None else part * half)
        size = quarter if part is None else half
        return full_ref.at[plane, pl.ds(pl.multiple_of(start, half), size), :]

    sent = []

    def push(index, src, dst, device):
        copy = remote(src, dst, send.at[index], recv.at[index], device)
        copy.start()
        sent.append(copy)

    def arrive(index, ref):
        remote(ref, ref, send.at[index], recv.at[index], at.core_side).wait_recv()

    local = pltpu.make_async_copy(own_ref, full_ref.at[at.s], local_sem)
    local.start()
    mine = own_ref.at[pl.ds(pl.multiple_of(at.r * quarter, quarter), quarter), :]
    for k in (1, 2, 3):
        push(k - 1, mine, piece(at.s, at.r), at.z_side(k))
    push(3, own_ref, full_ref.at[at.s], at.core_side)
    planes = [at.z_from(k) * 2 + at.c for k in (1, 2, 3)]
    twins = [at.z_from(k) * 2 + (1 - at.c) for k in (1, 2, 3)]
    for k, plane in enumerate(planes):
        got = piece(plane, at.r)
        arrive(k, got)
        push(4 + k, got, got, at.x_side)
        push(7 + k, got, got, at.y_side)
        push(10 + k, got, got, at.core_side)
    for k, plane in enumerate(planes):
        got = piece(plane, at.rx)
        arrive(4 + k, got)
        push(13 + k, piece(plane, at.rx, 0), piece(plane, at.rx, 0), at.y_side)
        push(16 + k, got, got, at.core_side)
        got = piece(plane, at.ry)
        arrive(7 + k, got)
        push(19 + k, piece(plane, at.ry, 1), piece(plane, at.ry, 1), at.x_side)
        push(22 + k, got, got, at.core_side)
    for k, plane in enumerate(planes):
        arrive(13 + k, piece(plane, at.rd, 0))
        arrive(19 + k, piece(plane, at.rd, 1))
        got = piece(plane, at.rd)
        push(25 + k, got, got, at.core_side)
    arrive(3, full_ref.at[at.core_side[1]])
    for k, plane in enumerate(twins):
        arrive(10 + k, piece(plane, at.r))
        arrive(16 + k, piece(plane, at.rx))
        arrive(22 + k, piece(plane, at.ry))
        arrive(25 + k, piece(plane, at.rd))
    for copy in sent:
        copy.wait_send()
    local.wait()


def gather_rows(own, shards, direct, number):
    if not direct:
        return lax.all_gather(own, "shard", axis=0)
    return pl.pallas_call(
        gather_kernel,
        out_shape=jax.ShapeDtypeStruct((shards,) + own.shape, own.dtype),
        in_specs=[pl.BlockSpec(memory_space=ANY)],
        out_specs=pl.BlockSpec(memory_space=ANY),
        scratch_shapes=[DMA, DMA((28,)), DMA((28,))],
        compiler_params=pltpu.CompilerParams(collective_id=number, has_side_effects=True),
        name=f"gather_{number}",
    )(own)


def reduce_kernel(parts_ref, out_ref, own, r0, r1a, r1b, r2a, r2b, r3, local_sem, send, recv):
    rows = out_ref.shape[0]
    quarter, half = rows // 4, rows // 8
    at = Place()
    greet([at.x_side, at.y_side, at.core_side] + [at.z_side(k) for k in (1, 2, 3)])
    sent = []

    def push(index, src, dst, device):
        copy = remote(src, dst, send.at[index], recv.at[index], device)
        copy.start()
        sent.append(copy)

    def arrive(index, ref):
        remote(ref, ref, send.at[index], recv.at[index], at.core_side).wait_recv()

    def spot(owner, part):
        return pl.ds(pl.multiple_of(owner * quarter + part * half, half), half)

    def add_into(k, where, ref):
        own[k, where, :] = (own[k, where, :].astype(F32) + ref[...].astype(F32)).astype(BF)

    order = [at.z_to(k) for k in (1, 2, 3, 0)]
    local = []
    for k, z in enumerate(order):
        copy = pltpu.make_async_copy(parts_ref.at[z * 2 + at.c], own.at[k], local_sem.at[k])
        copy.start()
        local.append(copy)
        push(k, parts_ref.at[z * 2 + (1 - at.c)], r0.at[k], at.core_side)
    for k in range(4):
        local[k].wait()
        arrive(k, r0.at[k])

        def add_rows(i, _, k=k):
            where = pl.ds(pl.multiple_of(i * half, half), half)
            add_into(k, where, r0.at[k, where, :])
            return 0

        lax.fori_loop(0, rows // half, add_rows, 0)
        for i in range(2):
            push(4 + 4 * k + i, own.at[k, spot(i * 2 + 1 - at.x, 0), :], r1a.at[k, i], at.x_side)
            push(
                6 + 4 * k + i, own.at[k, spot((1 - at.y) * 2 + i, 1), :], r1b.at[k, i], at.y_side
            )
    for k in range(4):
        for i in range(2):
            arrive(4 + 4 * k + i, r1a.at[k, i])
            arrive(6 + 4 * k + i, r1b.at[k, i])
            add_into(k, spot(i * 2 + at.x, 0), r1a.at[k, i])
            add_into(k, spot(at.y * 2 + i, 1), r1b.at[k, i])
        push(20 + 2 * k, own.at[k, spot(at.ry, 0), :], r2a.at[k], at.y_side)
        push(21 + 2 * k, own.at[k, spot(at.rx, 1), :], r2b.at[k], at.x_side)
    mine = pl.ds(pl.multiple_of(at.r * quarter, quarter), quarter)
    for k in range(4):
        arrive(20 + 2 * k, r2a.at[k])
        arrive(21 + 2 * k, r2b.at[k])
        add_into(k, spot(at.r, 0), r2a.at[k])
        add_into(k, spot(at.r, 1), r2b.at[k])
        if k < 3:
            push(28 + k, own.at[k, mine, :], r3.at[k], at.z_side(k + 1))
    for k in range(3):
        arrive(28 + k, r3.at[k])
    for i in range(2):
        where = pl.ds(i * half, half)
        total = own[3, spot(at.r, i), :].astype(F32)
        for k in range(3):
            total += r3[k, where, :].astype(F32)
        out_ref[spot(at.r, i), :] = total.astype(BF)

    def piece(owner):
        return out_ref.at[pl.ds(pl.multiple_of(owner * quarter, quarter), quarter), :]

    push(31, piece(at.r), piece(at.r), at.x_side)
    push(32, piece(at.r), piece(at.r), at.y_side)
    arrive(31, piece(at.rx))
    push(33, out_ref.at[spot(at.rx, 0), :], out_ref.at[spot(at.rx, 0), :], at.y_side)
    arrive(32, piece(at.ry))
    push(34, out_ref.at[spot(at.ry, 1), :], out_ref.at[spot(at.ry, 1), :], at.x_side)
    arrive(33, out_ref.at[spot(at.rd, 0), :])
    arrive(34, out_ref.at[spot(at.rd, 1), :])
    for copy in sent:
        copy.wait_send()


def reduce_rows(parts, direct, number):
    shards, rows, columns = parts.shape
    if not direct:
        own = lax.psum_scatter(parts, "shard", scatter_dimension=0)
        return lax.psum(own, "rep").astype(F32)
    half = rows // 8
    return pl.pallas_call(
        reduce_kernel,
        out_shape=jax.ShapeDtypeStruct((rows, columns), BF),
        in_specs=[pl.BlockSpec(memory_space=ANY)],
        out_specs=pl.BlockSpec(memory_space=VMEM),
        scratch_shapes=[
            VMEM((4, rows, columns), BF),
            VMEM((4, rows, columns), BF),
            VMEM((4, 2, half, columns), BF),
            VMEM((4, 2, half, columns), BF),
            VMEM((4, half, columns), BF),
            VMEM((4, half, columns), BF),
            VMEM((3, 2 * half, columns), BF),
            DMA((4,)),
            DMA((35,)),
            DMA((35,)),
        ],
        compiler_params=pltpu.CompilerParams(
            collective_id=number, has_side_effects=True, vmem_limit_bytes=BIG_VMEM
        ),
        name=f"reduce_{number}",
    )(parts).astype(F32)


def greet_line(at):
    barrier = pltpu.get_barrier_semaphore()
    pl.semaphore_signal(barrier, inc=1, device_id=at.core_side, device_id_type=MESH)

    @pl.when(at.z < 3)
    def _():
        pl.semaphore_signal(barrier, inc=1, device_id=(at.r, at.s + 2), device_id_type=MESH)

    @pl.when(at.z > 0)
    def _():
        pl.semaphore_signal(barrier, inc=1, device_id=(at.r, at.s - 2), device_id_type=MESH)

    count = 1 + jnp.where(at.z < 3, 1, 0) + jnp.where(at.z > 0, 1, 0)
    pl.semaphore_wait(barrier, count)


def spread_kernel(kv_ref, win_ref, send, recv):
    kv_heads = kv_ref.shape[0]
    last = win_ref.shape[0] - 1
    at = Place()
    greet_line(at)
    later = (at.r, lax.min(at.s + 2, 7))

    for block in range(last):
        @pl.when(at.s < last - block)
        def _(block=block):
            win_ref[block] = jnp.zeros(win_ref.shape[1:], win_ref.dtype)

    win_ref[last] = kv_ref[...]
    near, far = jnp.where(at.c == 0, 1, 3), jnp.where(at.c == 0, 3, 1)

    def first(j):
        return remote(kv_ref.at[j], win_ref.at[2, j], send.at[0, j], recv.at[0, j], later)

    def twin_own(j):
        return remote(kv_ref.at[j], win_ref.at[3, j], send.at[1, j], recv.at[1, j], at.core_side)

    def second(j):
        return remote(win_ref.at[2, j], win_ref.at[0, j], send.at[2, j], recv.at[2, j], later)

    def twin_near(j, place):
        return remote(
            win_ref.at[2, j], win_ref.at[place, j], send.at[3, j], recv.at[3, j], at.core_side
        )

    def twin_far(j):
        return remote(win_ref.at[0, j], win_ref.at[1, j], send.at[4, j], recv.at[4, j], at.core_side)

    for j in range(kv_heads):
        @pl.when(at.z < 3)
        def _(j=j):
            first(j).start()

        @pl.when(at.c == 0)
        def _(j=j):
            twin_own(j).start()

    for j in range(kv_heads):
        @pl.when(at.z > 0)
        def _(j=j):
            first(j).wait_recv()
            twin_near(j, near).start()

            @pl.when(at.z < 3)
            def _():
                second(j).start()

    for j in range(kv_heads):
        @pl.when(at.z > 1)
        def _(j=j):
            second(j).wait_recv()

            @pl.when(at.c == 1)
            def _():
                twin_far(j).start()

    for j in range(kv_heads):
        @pl.when(at.c == 1)
        def _(j=j):
            twin_own(j).wait_recv()

        @pl.when(at.z > 0)
        def _(j=j):
            twin_near(j, far).wait_recv()
            twin_near(j, near).wait_send()

        @pl.when((at.c == 0) & (at.z > 1))
        def _(j=j):
            twin_far(j).wait_recv()

        @pl.when((at.c == 1) & (at.z > 1))
        def _(j=j):
            twin_far(j).wait_send()

        @pl.when(at.z < 3)
        def _(j=j):
            first(j).wait_send()

        @pl.when((at.z < 3) & (at.z > 0))
        def _(j=j):
            second(j).wait_send()

        @pl.when(at.c == 0)
        def _(j=j):
            twin_own(j).wait_send()


def spread_pairs(pairs, reach, direct, number):
    if not direct or reach != 4:
        devices = range(lax.axis_size("shard"))
        blocks = []
        for distance in range(reach, 0, -1):
            route = [(i - distance, i) for i in devices if i - distance in devices]
            blocks.append(lax.ppermute(pairs, "shard", route))
        return jnp.stack(blocks + [pairs])
    return pl.pallas_call(
        spread_kernel,
        out_shape=jax.ShapeDtypeStruct((reach + 1,) + pairs.shape, pairs.dtype),
        in_specs=[pl.BlockSpec(memory_space=VMEM)],
        out_specs=pl.BlockSpec(memory_space=VMEM),
        scratch_shapes=[DMA((5, pairs.shape[0])), DMA((5, pairs.shape[0]))],
        compiler_params=pltpu.CompilerParams(
            collective_id=number, has_side_effects=True, vmem_limit_bytes=BIG_VMEM
        ),
        name=f"spread_{number}",
    )(pairs)


def collect_kernel(grad_ref, out_ref, ra, rb, r2, r1, t2, t1, send, recv):
    kv_heads = out_ref.shape[0]
    at = Place()
    greet_line(at)
    earlier = (at.r, lax.max(at.s - 2, 0))

    def twin_a(j):
        return remote(grad_ref.at[3, j], ra.at[j], send.at[0, j], recv.at[0, j], at.core_side)

    def twin_b(j):
        return remote(grad_ref.at[1, j], rb.at[j], send.at[1, j], recv.at[1, j], at.core_side)

    def far(j):
        return remote(t2.at[j], r2.at[j], send.at[2, j], recv.at[2, j], earlier)

    def near(j):
        return remote(t1.at[j], r1.at[j], send.at[3, j], recv.at[3, j], earlier)

    for j in range(kv_heads):
        twin_b(j).start()
        twin_a(j).start()
    even = at.c == 0
    for j in range(kv_heads):
        twin_b(j).wait_recv()
        twin_a(j).wait_recv()
        from_a, from_b = ra[j].astype(F32), rb[j].astype(F32)
        none = jnp.zeros_like(from_a)
        t2[j] = (grad_ref[0, j].astype(F32) + jnp.where(even, none, from_b)).astype(BF)

        @pl.when(at.z > 1)
        def _(j=j):
            far(j).start()

        t1[j] = (grad_ref[2, j].astype(F32) + jnp.where(even, from_b, from_a)).astype(BF)
        out_ref[j] = grad_ref[4, j].astype(F32) + jnp.where(even, from_a, none)
    for j in range(kv_heads):
        @pl.when((at.z > 0) & (at.z < 3))
        def _(j=j):
            far(j).wait_recv()
            t1[j] = (t1[j].astype(F32) + r2[j].astype(F32)).astype(BF)

        @pl.when(at.z > 0)
        def _(j=j):
            near(j).start()

    for j in range(kv_heads):
        @pl.when(at.z < 3)
        def _(j=j):
            near(j).wait_recv()
            out_ref[j] += r1[j].astype(F32)

        @pl.when(at.z > 1)
        def _(j=j):
            far(j).wait_send()

        @pl.when(at.z > 0)
        def _(j=j):
            near(j).wait_send()

        twin_a(j).wait_send()
        twin_b(j).wait_send()


def collect_pairs(grads, reach, direct, number):
    if not direct or reach != 4:
        devices = range(lax.axis_size("shard"))
        own = grads[reach].astype(F32)
        for distance in range(1, reach + 1):
            route = [(i, i - distance) for i in devices if i - distance in devices]
            own = own + lax.ppermute(grads[reach - distance], "shard", route).astype(F32)
        return own
    shape = grads.shape[1:]
    return pl.pallas_call(
        collect_kernel,
        out_shape=jax.ShapeDtypeStruct(shape, F32),
        in_specs=[pl.BlockSpec(memory_space=VMEM)],
        out_specs=pl.BlockSpec(memory_space=VMEM),
        scratch_shapes=[VMEM(shape, BF)] * 6 + [DMA((4, shape[0])), DMA((4, shape[0]))],
        compiler_params=pltpu.CompilerParams(
            collective_id=number, has_side_effects=True, vmem_limit_bytes=BIG_VMEM
        ),
        name=f"collect_{number}",
    )(grads)


def angles(positions):
    half_dim = HEAD_DIM // 2
    inverse = rope_base ** (-(2.0 * jnp.arange(half_dim, dtype=F32) / HEAD_DIM))
    phases = positions.astype(F32)[:, None] * inverse[None, :]
    return (jnp.cos(phases)[:, None, :], jnp.sin(phases)[:, None, :])


def rotate(tensor, cosine_table, sine_table):
    half_dim = HEAD_DIM // 2
    front, back = tensor[..., :half_dim], tensor[..., half_dim:]
    return jnp.concatenate(
        [front * cosine_table - back * sine_table, back * cosine_table + front * sine_table],
        axis=-1,
    )


def norm_back(upstream, normed, scale_rows):
    mean = jnp.sum(upstream * normed, axis=-1, keepdims=True) * (1.0 / D)
    return scale_rows * (upstream - normed * mean)


def adam_step(weight_now, gradient, first, second, decay_factor):
    old_weight = weight_now.astype(F32)
    moment = beta_one * first + (1.0 - beta_one) * gradient
    square = beta_two * second + (1.0 - beta_two) * gradient * gradient
    corrected = moment / (1.0 - beta_one**STEP)
    divisor = jnp.sqrt(square / (1.0 - beta_two**STEP)) + adam_eps
    update = -learn_rate * (corrected / divisor + decay_factor * old_weight)
    return (gradient, moment, square, old_weight + update, update)


def shards(
    direct,
    block_input,
    block_cotangent,
    lengths,
    attend_gain,
    attend_weight,
    output_weight,
    expand_gain,
    expand_weight,
    shrink_weight,
    attend_gain_first,
    attend_weight_first,
    output_weight_first,
    expand_gain_first,
    expand_weight_first,
    shrink_weight_first,
    attend_gain_second,
    attend_weight_second,
    output_weight_second,
    expand_gain_second,
    expand_weight_second,
    shrink_weight_second,
):
    tokens = block_input.shape[0]
    shard_count = lax.axis_size("shard")
    token_count = tokens * shard_count * lax.axis_size("rep")
    reach = (MAXLEN - 2) // tokens + 1
    own_rows = attend_weight.shape[0]
    rows = -(-(own_rows + 2) // 16) * 16
    width = shard_count * rows

    def padded(tensor):
        blocks = tensor.reshape(tokens, shard_count, own_rows)
        return jnp.pad(blocks, ((0, 0), (0, 0), (0, rows - own_rows))).reshape(tokens, width)

    def unpadded(tensor):
        return tensor.reshape(tokens, shard_count, rows)[:, :, :own_rows].reshape(tokens, D)

    def with_gain(weight, gain):
        tail = jnp.pad(gain[None, :], ((0, rows - own_rows - 1), (0, weight.shape[1] - own_rows)))
        return jnp.concatenate([weight, tail], axis=0)

    def gain_of(planes):
        return jnp.pad(
            planes[:, own_rows, :own_rows], ((0, 0), (0, rows - own_rows))
        ).reshape(1, width).astype(F32)

    def add_gain(planes, term):
        row = term.reshape(shard_count, 1, rows).astype(planes.dtype)
        return lax.dynamic_update_slice(planes, row, (0, own_rows, 0))

    first_row = lax.axis_index("shard") * tokens
    local_index = first_row + jnp.arange(tokens, dtype=jnp.int32)
    key_index = first_row - reach * tokens + jnp.arange((reach + 1) * tokens, dtype=jnp.int32)
    ends = jnp.cumsum(lengths[0], dtype=jnp.int32)
    starts = ends - lengths[0]
    seq_count = lengths.shape[1]
    in_key = (key_index[:, None] >= starts[None, :]) & (key_index[:, None] < ends[None, :])
    in_query = (local_index[None, :] >= starts[:, None]) & (local_index[None, :] < ends[:, None])
    lanes = 2 * HEAD_DIM
    feat = jnp.concatenate(
        [
            in_key.astype(BF),
            (key_index < 0).astype(BF)[:, None],
            jnp.zeros((key_index.shape[0], ONES - seq_count - 1), BF),
            jnp.ones((key_index.shape[0], lanes - ONES), BF),
        ],
        axis=1,
    )
    qfeat = jnp.concatenate(
        [
            jnp.where(in_query, 0.0, NEG).astype(BF),
            jnp.full((1, tokens), NEG, BF),
            jnp.zeros((lanes - seq_count - 1, tokens), BF),
        ],
        axis=0,
    )
    start_index = jnp.sum(in_query * starts[:, None], axis=0, dtype=jnp.int32)
    cosine_table, sine_table = angles(local_index - start_index)

    attend_own = with_gain(attend_weight, attend_gain)
    rest_own = with_gain(
        jnp.concatenate([expand_weight, shrink_weight.T, output_weight.T], axis=1), expand_gain
    )
    attend_planes = gather_rows(attend_own, shard_count, direct, 0)
    rest_planes = gather_rows(rest_own, shard_count, direct, 1)
    gain_one, gain_two = gain_of(attend_planes), gain_of(rest_planes)
    joint_weight = attend_planes.reshape(width, JW)
    rest = rest_planes.reshape(width, rest_own.shape[1])
    expand_full, shrink_full, out_full = rest[:, : 2 * FF], rest[:, 2 * FF : 3 * FF], rest[:, 3 * FF :]
    real = (jnp.arange(width, dtype=jnp.int32) % rows < own_rows)[None, :]

    inputs = padded(block_input).astype(F32)
    scale_one = lax.rsqrt(jnp.sum(inputs * inputs, axis=-1, keepdims=True) * (1.0 / D) + eps_norm)
    normed_one = inputs * scale_one
    hidden_one = (normed_one * gain_one).astype(BF)
    joint = dot(hidden_one, joint_weight)
    queries = rotate(joint[:, :QW].reshape(tokens, HEADS, HEAD_DIM), cosine_table, sine_table)
    key_rows = rotate(
        joint[:, QW : QW + KW].reshape(tokens, KV_HEADS, HEAD_DIM), cosine_table, sine_table
    )
    values = joint[:, QW + KW :].reshape(tokens, KV_HEADS, HEAD_DIM)
    pairs = jnp.concatenate([key_rows, values], axis=-1).astype(BF).transpose(1, 0, 2)
    qt = queries.astype(BF).reshape(tokens, QW).T
    window = spread_pairs(pairs, reach, direct, 2)
    mixedt, lse = attend_forward(window, feat, qt, qfeat)
    middle = inputs + dot(mixedt, out_full, 0, 1)
    scale_two = lax.rsqrt(jnp.sum(middle * middle, axis=-1, keepdims=True) * (1.0 / D) + eps_norm)
    normed_two = middle * scale_two
    hidden_two = (normed_two * gain_two).astype(BF)
    gate_up = dot(hidden_two, expand_full)
    gate_value, upper_value = gate_up[:, :FF], gate_up[:, FF:]
    sigmoid_gate = jax.nn.sigmoid(gate_value)
    inner_rows = (gate_value * sigmoid_gate * upper_value).astype(BF)
    block_output = middle + dot(inner_rows, shrink_full, 1, 1)

    cotangent = padded(block_cotangent)
    shrink_term = dot(cotangent, inner_rows, 0, 0)
    inner_grad = dot(cotangent, shrink_full)
    gate_grad = (
        inner_grad * upper_value * sigmoid_gate * (1.0 + gate_value * (1.0 - sigmoid_gate))
    ).astype(BF)
    upper_grad = (inner_grad * gate_value * sigmoid_gate).astype(BF)
    gate_up_grad = jnp.concatenate([gate_grad, upper_grad], axis=1)
    expand_term = dot(hidden_two, gate_up_grad, 0, 0)
    hidden_two_grad = jnp.where(real, dot(gate_up_grad, expand_full, 1, 1), 0.0)
    gain_two_term = jnp.sum(hidden_two_grad * normed_two, axis=0)
    middle_grad = cotangent.astype(F32) + norm_back(
        hidden_two_grad * gain_two, normed_two, scale_two
    )
    branch_grad = middle_grad.astype(BF)
    output_term = dot(branch_grad, mixedt, 0, 1)
    gradt = dot(out_full, branch_grad, 0, 1).astype(BF)
    rest_term = jnp.concatenate(
        [expand_term.astype(BF), shrink_term.astype(BF), output_term.astype(BF)], axis=1
    ).reshape(shard_count, rows, rest_own.shape[1])
    rest_sum = reduce_rows(add_gain(rest_term, gain_two_term), direct, 3)

    dqt, dwindow = attend_backward(window, feat, qt, qfeat, gradt, mixedt, lse)
    own_pairs = collect_pairs(dwindow, reach, direct, 4).transpose(1, 0, 2)
    dq = dqt.T.reshape(tokens, HEADS, HEAD_DIM)
    query_raw = rotate(dq, cosine_table, -sine_table).reshape(tokens, QW)
    key_raw = rotate(own_pairs[..., :HEAD_DIM], cosine_table, -sine_table).reshape(tokens, KW)
    value_raw = own_pairs[..., HEAD_DIM:].reshape(tokens, KW)
    joint_grad = jnp.concatenate([query_raw, key_raw, value_raw], axis=1).astype(BF)
    joint_term = dot(hidden_one, joint_grad, 0, 0).astype(BF)
    hidden_one_grad = jnp.where(real, dot(joint_grad, joint_weight, 1, 1), 0.0)
    gain_one_term = jnp.sum(hidden_one_grad * normed_one, axis=0)
    input_gradient = middle_grad + norm_back(hidden_one_grad * gain_one, normed_one, scale_one)
    attend_sum = reduce_rows(
        add_gain(joint_term.reshape(shard_count, rows, JW), gain_one_term), direct, 5
    )

    grad_scale = grad_factor * token_count ** (-0.5)
    rest_grad, attend_grad = rest_sum * grad_scale, attend_sum * grad_scale
    first_gain = adam_step(
        attend_gain, attend_grad[own_rows, :own_rows], attend_gain_first, attend_gain_second, 0.0
    )
    first_joint = adam_step(
        attend_weight,
        attend_grad[:own_rows],
        attend_weight_first,
        attend_weight_second,
        decay_rate,
    )
    first_output = adam_step(
        output_weight,
        rest_grad[:own_rows, 3 * FF :].T,
        output_weight_first,
        output_weight_second,
        decay_rate,
    )
    second_gain = adam_step(
        expand_gain, rest_grad[own_rows, :own_rows], expand_gain_first, expand_gain_second, 0.0
    )
    second_expand = adam_step(
        expand_weight,
        rest_grad[:own_rows, : 2 * FF],
        expand_weight_first,
        expand_weight_second,
        decay_rate,
    )
    second_shrink = adam_step(
        shrink_weight,
        rest_grad[:own_rows, 2 * FF : 3 * FF].T,
        shrink_weight_first,
        shrink_weight_second,
        decay_rate,
    )
    steps = (first_gain, first_joint, first_output, second_gain, second_expand, second_shrink)
    changed = [step[4] if step[0].ndim == 1 else step[3] for step in steps]
    return (
        unpadded(block_output),
        unpadded(input_gradient),
        *[step[0] for step in steps],
        *[step[1] for step in steps],
        *[step[2] for step in steps],
        *changed,
    )


def solution(mesh):
    whole_rows = P(("rep", "shard"), None)
    state = (P("shard"), P("shard", None), P(None, "shard")) * 2
    state = (state[0], state[1], state[2], state[3], state[4], state[5])
    direct = mesh.shape["rep"] == 4 and mesh.shape["shard"] == 8
    return jax.shard_map(
        functools.partial(shards, direct),
        mesh=mesh,
        in_specs=(whole_rows, whole_rows, P("rep", None), *state, *state, *state),
        out_specs=(whole_rows, whole_rows, *state, *state, *state, *state),
        check_vma=False,
    )
```

time: 1250 us -> 647 us (0.52)
  waiting for transfers between devices: 728 us -> 0 us
  Pallas kernels: 0 us -> 458 us
  matrix products: 334 us -> 78.3 us
  blocking collectives: 43 us -> 0 us
  starting transfers between devices: 16.7 us -> 0 us
  between operations: 16.5 us -> 1.63 us
    pallas_call x0 -> x8, Pallas kernels: none -> 458 us  [the longest x2 180 us: reduce_rows(): pl.pallas_call(reduce_kernel, out_shape=jax.ShapeDtypeStruct((rows, colum...]
    reduce_scatter x2 -> x0, waiting for transfers between devices: 300 us -> none  [the longest x1 196 us: shards(): lax.psum_scatter(expand_term, 'shard', scatter_dimension=0, tiled=True)]
    dot_general x116 -> x12, matrix products: 331 us -> 78.3 us  [dot(): lax.dot_general(a, b, (((ca,), (cb,)), ((), ())), preferred_element_type=...]
    ppermute x8 -> x0, waiting for transfers between devices: 241 us -> none  [passed_along(): return lax.ppermute(block, axis, route)]
    psum x1 -> x0, waiting for transfers between devices: 81.4 us -> none  [shards(): lax.psum((gain_one_sum, joint_sum, output_sum, gain_two_sum, expand_sum,...]
    unnamed x11 -> x0, waiting for transfers between devices: 61.4 us -> none
    all_gather x4 -> x0, waiting for transfers between devices: 43.3 us -> none  [the longest x1 27.1 us: shards(): lax.all_gather(shrink_weight, 'shard', axis=1, tiled=True)]
    unnamed x2 -> x0, blocking collectives: 32.5 us -> none
  transfers between devices with their start and end apart: 17 -> 0, of which waited for: 11 -> 0; matrix products, arithmetic and copies ran while one was open for 32% -> 0% of each run, Pallas kernels for 0% -> 0%
where the time goes in v1:
time: 647 us; the launch traced here: 641 us
  Pallas kernels  458 us (71%)
  matrix products  78.3 us (12%)
  other arithmetic  56 us (9%)
  local copies, waits for them, and re-layouts  47 us (7%)
    pallas_call x2, Pallas kernels, reduce_rows(): pl.pallas_call(reduce_kernel, out_shape=jax.ShapeDtypeStruct((rows, colum...  180 us
    pallas_call x2, Pallas kernels, gather_rows(): pl.pallas_call(gather_kernel, out_shape=jax.ShapeDtypeStruct((shards,) +...  130 us
    dot_general x12, matrix products, dot(): lax.dot_general(a, b, (((ca,), (cb,)), ((), ())), preferred_element_type=...  78.3 us
    pallas_call x1, Pallas kernels, attend_backward(): pl.pallas_call(attend_backward_kernel, out_shape=(jax.ShapeDtypeStruct(qt...  59.2 us
    pallas_call x1, Pallas kernels, collect_pairs(): pl.pallas_call(collect_kernel, out_shape=jax.ShapeDtypeStruct(shape, F32)...  38.7 us
    pallas_call x1, Pallas kernels, attend_forward(): pl.pallas_call(attend_forward_kernel, out_shape=(jax.ShapeDtypeStruct(qt....  30.7 us
    pallas_call x1, Pallas kernels, spread_pairs(): pl.pallas_call(spread_kernel, out_shape=jax.ShapeDtypeStruct((reach + 1,)...  18.5 us
    add x4, other arithmetic, adam_step(): return (gradient, moment, square, old_weight + update, update)  16.8 us

profile of v1, /device:TPU:0, one launch (start us, length us, event | category | flops | bytes accessed | tf_op | source)
XLA Modules:
  0.0 640.6 jit_solution(15245907428517059284)
XLA Ops:
  0.7 1.8 fusion.51.own_ref
  2.5 27.5 %gather_0.1 = bf16[8,128,1600]{2,1,0:T(8,128)(2,1)} custom-call(bf16[128,1600]{1,0:T(8,128)(2,1)} %fusion.51.own_ref), custom_call_target="tpu_custom_call" | custom-call | tf_op jit(solution)/shard_map/gather_0/pallas_call | solution.py:368
  31.7 4.0 convolution_bitcast_fusion
  35.7 1.7 copy-done.5
  39.3 1.4 copy.125
  40.7 1.5 copy.124
  43.7 1.8 subtract_convert_fusion.1
  45.5 1.4 maximum_bitcast_fusion.kv_ref
  47.0 18.5 %spread_2.1.kv_ref = bf16[5,5,512,128]{3,2,1,0:T(8,128)(2,1)} custom-call(bf16[5,512,128]{2,1,0:T(8,128)(2,1)} %maximum_bitcast_fusion.kv_ref), custom_call_target="tpu_custom_call" | custom-call | tf_op jit(solution)/shard_map/spread_2/pallas_call | solution.py:607
  67.1 1.3 maximum_maximum_fusion.feat_ref
  68.4 1.5 slice-done.1
  72.3 30.7 %attend_forward.1 = (bf16[960,512]{1,0:T(8,128)(2,1)}, f32[15,1,512]{2,1,0:T(1,128)}) custom-call(bf16[5,5,512,128]{3,2,1,0:T(8,128)(2,1)} %spread_2.1.kv_ref, bf16[2560,128]{1,0:T(8,128)(2,1)} %maximum_maximum_fusion.feat_ref, bf16[960,512]{1,0:T(8,128)(2,1)} %bitcast.127, bf16[128,512]{1,0:T(8,128)(2,1)} %maximum_maximum_fusion.1.qfeat_ref), custom_call_target="tpu_custom_call" | custom-call | tf_op jit(solution)/shard_map/attend_forward/pallas_call | solution.py:130
  104.1 2.0 fusion.12.own_ref
  106.2 102.9 %gather_1.1 = bf16[8,128,8640]{2,1,0:T(8,128)(2,1)} custom-call(bf16[128,8640]{1,0:T(8,128)(2,1)} %fusion.12.own_ref), custom_call_target="tpu_custom_call" | custom-call | tf_op jit(solution)/shard_map/gather_1/pallas_call | solution.py:368
  209.1 3.0 multiply_reduce_fusion.4
  212.9 12.4 %fusion.2 = f32[512,5120]{1,0:T(8,128)} fusion(bf16[1024,8640]{1,0:T(8,128)(2,1)} %bitcast.119, f32[512,1024]{1,0:T(8,128)S(1)} %get-tuple-element.158, f32[1024]{0:T(1024)S(1)} %bitcast_convert_fusion, f32[512]{0:T(512)S(1)} %add_rsqrt_fusion), kind=kOutput, calls=%fused_computation.4 | convolution fusion | flops 5370281984 | bytes 23074816 | tf_op jit(solution)/shard_map/dot_general | solution.py:49
  226.2 10.1 %multiply_convert_fusion.1 = (bf16[512,2560]{1,0:T(8,128)(2,1)}, bf16[512,2560]{1,0:T(8,128)(2,1)}, bf16[512,2560]{1,0:T(8,128)(2,1)S(1)}) fusion(f32[512,5120]{1,0:T(8,128)} %fusion.2, bf16[1024,8640]{1,0:T(8,128)(2,1)} %bitcast.120, bf16[64,8,8,128]{3,2,1,0:T(8,128)(2,1)S(1)} %bitcast.133), kind=kOutput, calls=%fused_computation.9 | convolution fusion | flops 2705326080 | bytes 24641536 | tf_op jit(solution)/shard_map/dot_general | solution.py:49
  236.4 5.8 add_bitcast_fusion.1
  242.2 1.8 copy.127
  244.0 2.9 copy.104
  246.8 12.8 %multiply_reduce_fusion = (bf16[1024]{0:T(1024)(128)(2,1)}, f32[512]{0:T(512)S(1)}, f32[512,1024]{1,0:T(8,128)S(1)}) fusion(f32[512,1024]{1,0:T(8,128)} %copy-done.14, f32[512]{0:T(512)S(1)} %add_rsqrt_fusion, pred[1024]{0:T(1024)(128)(4,1)S(1)} %fusion.53, f32[1024]{0:T(1024)S(1)} %bitcast_convert_fusion, bf16[1024,8640]{1,0:T(8,128)(2,1)} %bitcast.122, ...), kind=kOutput, calls=%fused_computation.37 | convolution fusion | flops 5382863360 | bytes 19934208 | tf_op jit(solution)/shard_map/dot_general | solution.py:49
  260.2 4.7 fusion.24.gradt_ref
  264.9 59.2 %attend_backward.1 = (f32[960,512]{1,0:T(8,128)}, bf16[5,5,512,128]{3,2,1,0:T(8,128)(2,1)}) custom-call(bf16[5,5,512,128]{3,2,1,0:T(8,128)(2,1)} %spread_2.1.kv_ref, bf16[2560,128]{1,0:T(8,128)(2,1)} %maximum_maximum_fusion.feat_ref, bf16[960,512]{1,0:T(8,128)(2,1)} %bitcast.128, bf16[128,512]{1,0:T(8,128)(2,1)} %maximum_maximum_fusion.1.qfeat_ref, ...), custom_call_target="tpu_custom_call" | custom-call | tf_op jit(solution)/shard_map/attend_backward/pallas_call | solution.py:250
  324.1 38.7 %collect_4.1 = f32[5,512,128]{2,1,0:T(8,128)} custom-call(bf16[5,5,512,128]{3,2,1,0:T(8,128)(2,1)} %get-tuple-element.33.grad_ref), custom_call_target="tpu_custom_call" | custom-call | tf_op jit(solution)/shard_map/collect_4/pallas_call | solution.py:692
  362.8 2.5 slice.183
  365.3 2.0 copy.108
  368.1 1.5 subtract_convert_fusion
  370.3 2.0 subtract_convert_fusion.2
  373.0 2.6 multiply_reduce_fusion.1
  376.3 1.8 copy.129
  378.1 3.1 copy.109
  381.2 4.1 convolution_convert_fusion.3
  385.2 3.9 copy.112
  389.1 6.6 %convolution_convert_fusion.1 = bf16[1024,2560]{1,0:T(8,128)(2,1)} fusion(bf16[512,2560]{1,0:T(8,128)(2,1)} %copy-done.43, bf16[64,8,8,128]{3,2,1,0:T(8,128)(2,1)S(1)} %bitcast.135), kind=kOutput, calls=%fused_computation.6 | convolution fusion | flops 2686976000 | bytes 8912896 | tf_op jit(solution)/shard_map/dot_general | solution.py:49
  395.7 8.7 %convolution_convert_fusion = bf16[1024,5120]{1,0:T(8,128)(2,1)S(1)} fusion(bf16[512,2560]{1,0:T(8,128)(2,1)} %get-tuple-element.140, bf16[512,2560]{1,0:T(8,128)(2,1)} %get-tuple-element.139, f32[512,1024]{1,0:T(8,128)S(1)} %copy-done.17, f32[1024]{0:T(1024)S(1)} %bitcast_convert_fusion, f32[512]{0:T(512)S(1)} %add_rsqrt_fusion), kind=kOutput, calls=%fused_computation.1 | convolution fusion | flops 5386010624 | bytes 17831936 | tf_op jit(solution)/shard_map/dot_general | solution.py:49
  404.5 14.6 %pad_maximum_fusion = bf16[1024,8640]{1,0:T(8,128)(2,1)} fusion(bf16[1024,960]{1,0:T(8,128)(2,1)S(1)} %copy-done.4, bf16[1024,2560]{1,0:T(8,128)(2,1)} %convolution_convert_fusion.1, bf16[1024,5120]{1,0:T(8,128)(2,1)S(1)} %convolution_convert_fusion), kind=kLoop, calls=%fused_computation | loop fusion | flops 53084160 | bytes 35389440 | tf_op jit(solution)/shard_map/concatenate | solution.py:870
  419.0 1.5 dynamic_update_slice.7.parts_ref
  420.5 134.7 %reduce_3.1 = bf16[128,8640]{1,0:T(8,128)(2,1)} custom-call(bf16[8,128,8640]{2,1,0:T(8,128)(2,1)} %dynamic_update_slice.7.parts_ref), custom_call_target="tpu_custom_call" | custom-call | tf_op jit(solution)/shard_map/reduce_3/pallas_call | solution.py:468
  555.2 4.2 convert_multiply_fusion
  559.5 3.7 convolution_convert_fusion.2
  563.1 4.3 copy.110
  567.8 1.7 copy-done.1
  569.6 45.5 %reduce_5.1 = bf16[128,1600]{1,0:T(8,128)(2,1)} custom-call(bf16[8,128,1600]{2,1,0:T(8,128)(2,1)} %copy-done.1), custom_call_target="tpu_custom_call" | custom-call | tf_op jit(solution)/shard_map/reduce_5/pallas_call | solution.py:468
  616.2 1.2 add_multiply_fusion
  617.4 3.2 convert_add_fusion.2
  622.8 8.1 %convert_add_fusion = (f32[120,5120]{1,0:T(8,128)}, f32[120,5120]{1,0:T(8,128)}, f32[120,5120]{1,0:T(8,128)}, f32[120,5120]{1,0:T(8,128)}) fusion(bf16[120,5120]{1,0:T(8,128)(2,1)S(1)} %copy-done.7, f32[120,5120]{1,0:T(8,128)} %param.40, f32[120,5120]{1,0:T(8,128)} %param.34, f32[128,8640]{1,0:T(8,128)} %convert_multiply_fusion), kind=kLoop, calls=%fused_computation.25 | loop fusion | flops 9830400 | bytes 18432000 | tf_op jit(solution)/shard_map/add | solution.py:733
  631.0 4.0 convert_add_fusion.1
  635.9 1.4 convert_add_fusion.3
  (149 shorter events, 22.8 us)
Async XLA Ops:
  2.5 28.2 %copy-start.21 = (bf16[512,960]{0,1:T(8,128)(2,1)S(1)}, bf16[512,960]{0,1:T(8,128)(2,1)}, u32[]{:S(2)}) copy-start(bf16[512,960]{0,1:T(8,128)(2,1)} %param.21) | copy-start | bytes 2949124
  35.7 1.7 copy-start.5
  37.4 1.1 slice-start
  38.5 3.6 copy-start.42
  43.7 1.8 copy-start.11
  68.4 1.5 slice-start.1
  72.3 31.8 %copy-start.6 = (bf16[120,5120]{1,0:T(8,128)(2,1)S(1)}, bf16[120,5120]{1,0:T(8,128)(2,1)}, u32[]{:S(2)}) copy-start(bf16[120,5120]{1,0:T(8,128)(2,1)} %param.28) | copy-start | bytes 3686404
  72.3 31.8 %copy-start.9 = (bf16[2560,120]{0,1:T(8,128)(2,1)S(1)}, bf16[2560,120]{0,1:T(8,128)(2,1)}, u32[]{:S(2)}) copy-start(bf16[2560,120]{0,1:T(8,128)(2,1)} %param.29) | copy-start | bytes 1843204
  72.3 31.8 %copy-start.34 = (bf16[120]{0:T(256)(128)(2,1)S(1)}, bf16[120]{0:T(256)(128)(2,1)}, u32[]{:S(2)}) copy-start(bf16[120]{0:T(256)(128)(2,1)} %param.27) | copy-start | bytes 724
  104.1 2.1 copy-start.12
  106.2 102.9 %copy-start.23 = (bf16[960,512]{1,0:T(8,128)(2,1)S(1)}, bf16[960,512]{1,0:T(8,128)(2,1)}, u32[]{:S(2)}) copy-start(bf16[960,512]{1,0:T(8,128)(2,1)} %get-tuple-element.30.mixed_ref) | copy-start | bytes 2949124
  212.1 13.1 %copy-start.14 = (f32[512,1024]{1,0:T(8,128)}, f32[512,1024]{1,0:T(8,128)S(1)}, u32[]{:S(2)}) copy-start(f32[512,1024]{1,0:T(8,128)S(1)} %get-tuple-element.158) | copy-start | bytes 6291460
  212.8 12.4 %copy-start.22 = (bf16[512,960]{0,1:T(8,128)(2,1)S(1)}, bf16[512,960]{0,1:T(8,128)(2,1)}, u32[]{:S(2)}) copy-start(bf16[512,960]{0,1:T(8,128)(2,1)} %param.22) | copy-start | bytes 2949124
  226.2 10.1 %copy-start.15 = (f32[512,1024]{1,0:T(8,128)S(1)}, f32[512,1024]{1,0:T(8,128)}, u32[]{:S(2)}) copy-start(f32[512,1024]{1,0:T(8,128)} %copy-done.14) | copy-start | bytes 6291460
  236.3 5.8 copy-start.43
  246.8 12.8 %copy-start.32 = (pred[1024]{0:T(1024)(128)(4,1)}, pred[1024]{0:T(1024)(128)(4,1)S(1)}, u32[]{:S(2)}) copy-start(pred[1024]{0:T(1024)(128)(4,1)S(1)} %fusion.53) | copy-start | bytes 3076
  246.8 12.8 %copy-start.16 = (f32[512,1024]{1,0:T(8,128)S(1)}, f32[512,1024]{1,0:T(8,128)}, u32[]{:S(2)}) copy-start(f32[512,1024]{1,0:T(8,128)} %copy-done.14) | copy-start | bytes 6291460
  260.2 4.7 copy-start.2
  362.8 5.4 copy-start
  370.3 2.1 copy-start.30
  370.3 2.7 copy-start.8
  370.3 2.7 copy-start.29
  370.3 2.7 copy-start.33
  372.4 3.2 copy-start.25
  373.0 2.6 copy-start.3
  378.1 3.1 copy-start.24
  389.1 6.6 %copy-start.17 = (f32[512,1024]{1,0:T(8,128)S(1)}, f32[512,1024]{1,0:T(8,128)}, u32[]{:S(2)}) copy-start(f32[512,1024]{1,0:T(8,128)} %copy-done.14) | copy-start | bytes 6291460
  395.7 8.7 %copy-start.4 = (bf16[1024,960]{1,0:T(8,128)(2,1)S(1)}, bf16[1024,960]{1,0:T(8,128)(2,1)}, u32[]{:S(2)}) copy-start(bf16[1024,960]{1,0:T(8,128)(2,1)} %copy.112) | copy-start | bytes 5898244
  404.5 14.6 %copy-start.36 = (bf16[1024]{0:T(1024)(128)(2,1)S(1)}, bf16[1024]{0:T(1024)(128)(2,1)}, u32[]{:S(2)}) copy-start(bf16[1024]{0:T(1024)(128)(2,1)} %get-tuple-element.112) | copy-start | bytes 6148
  555.2 4.3 copy-start.26
  555.2 4.3 copy-start.31
  567.8 1.7 copy-start.1
  569.5 46.6 %copy-start.35 = (bf16[120]{0:T(256)(128)(2,1)S(1)}, bf16[120]{0:T(256)(128)(2,1)}, u32[]{:S(2)}) copy-start(bf16[120]{0:T(256)(128)(2,1)} %param.27) | copy-start | bytes 724
  569.5 46.6 %copy-start.37 = (bf16[120]{0:T(256)(128)(2,1)S(1)}, bf16[120]{0:T(256)(128)(2,1)}, u32[]{:S(2)}) copy-start(bf16[120]{0:T(256)(128)(2,1)} %param.24) | copy-start | bytes 724
  569.5 46.6 %copy-start.38 = (f32[120]{0:T(128)S(1)}, f32[120]{0:T(128)}, u32[]{:S(2)}) copy-start(f32[120]{0:T(128)} %param.39) | copy-start | bytes 1444
  569.5 46.6 %copy-start.39 = (f32[120]{0:T(128)S(1)}, f32[120]{0:T(128)}, u32[]{:S(2)}) copy-start(f32[120]{0:T(128)} %param.33) | copy-start | bytes 1444
  569.5 46.6 %copy-start.40 = (f32[120]{0:T(128)S(1)}, f32[120]{0:T(128)}, u32[]{:S(2)}) copy-start(f32[120]{0:T(128)} %param.36) | copy-start | bytes 1444
  569.5 46.6 %copy-start.41 = (f32[120]{0:T(128)S(1)}, f32[120]{0:T(128)}, u32[]{:S(2)}) copy-start(f32[120]{0:T(128)} %param.30) | copy-start | bytes 1444
  569.6 47.8 %copy-start.18 = (bf16[120,1600]{1,0:T(8,128)(2,1)S(1)}, bf16[120,1600]{1,0:T(8,128)(2,1)}, u32[]{:S(2)}) copy-start(bf16[120,1600]{1,0:T(8,128)(2,1)} %param.25) | copy-start | bytes 1152004
  620.6 2.2 copy-start.7
  622.8 8.2 %copy-start.10 = (bf16[2560,120]{0,1:T(8,128)(2,1)S(1)}, bf16[2560,120]{0,1:T(8,128)(2,1)}, u32[]{:S(2)}) copy-start(bf16[2560,120]{0,1:T(8,128)(2,1)} %param.29) | copy-start | bytes 1843204
  622.8 8.2 %copy-start.19 = (f32[2560,120]{0,1:T(8,128)S(1)}, f32[2560,120]{0,1:T(8,128)}, u32[]{:S(2)}) copy-start(f32[2560,120]{0,1:T(8,128)} %param.41) | copy-start | bytes 3686404
  622.8 8.2 %copy-start.20 = (f32[2560,120]{0,1:T(8,128)S(1)}, f32[2560,120]{0,1:T(8,128)}, u32[]{:S(2)}) copy-start(f32[2560,120]{0,1:T(8,128)} %param.35) | copy-start | bytes 3686404
  630.9 4.0 copy-start.27
  631.0 4.2 copy-start.28
  635.0 0.9 copy-start.13

commit v2 on v1

v2 whole, which is shorter than its diff:
```python
import functools
import math

import jax
import jax.numpy as jnp
from jax import lax
from jax.experimental import pallas as pl
from jax.experimental.pallas import tpu as pltpu
from jax.sharding import PartitionSpec as P

HEADS = 15
KV_HEADS = 5
HEAD_DIM = 64
GROUP = HEADS // KV_HEADS
FF = 2560
MAXLEN = 2048
STEP = 10
QW = 960
KW = 320
JW = QW + 2 * KW
D = 960

eps_norm = 1e-05
rope_base = 100000.0
beta_one = 0.9
beta_two = 0.95
adam_eps = 1e-08
learn_rate = 0.05
decay_rate = 0.1
grad_factor = 4.0

F32 = jnp.float32
BF = jnp.bfloat16
MESH = pl.DeviceIdType.MESH
ANY = pl.ANY
VMEM = pltpu.VMEM
DMA = pltpu.SemaphoreType.DMA

QC = 256
KB = 768
HALF = 64
ONES = 112
NEG = -1e30
EXP_SCALE = HEAD_DIM**-0.5 * math.log2(math.e)
BIG_VMEM = 60 * 2**20


def dot(a, b, ca=1, cb=0):
    return lax.dot_general(a, b, (((ca,), (cb,)), ((), ())), preferred_element_type=F32)


def causal_tile():
    key = lax.broadcasted_iota(jnp.int32, (QC, QC), 0)
    query = lax.broadcasted_iota(jnp.int32, (QC, QC), 1)
    return key <= query


def mask_last(scores, causal):
    last = jnp.where(causal, scores[KB - QC :], NEG)
    return jnp.concatenate([scores[: KB - QC], last], axis=0)


def attend_forward_setup(feat_ref, qfeat_ref, kvf, vt, qa):
    lanes = feat_ref.shape[1]
    kvf[:, lanes:] = feat_ref[...]
    qa[HALF:lanes, :] = jnp.zeros((lanes - HALF, qa.shape[1]), BF)
    qa[lanes:, :] = qfeat_ref[...]
    vt[HALF:, :] = jnp.ones((vt.shape[0] - HALF, vt.shape[1]), BF)


def attend_forward_keys(j, kv_ref, kvf, vt):
    blocks, _, rows, lanes = kv_ref.shape
    for block in range(blocks):
        part = kv_ref[block, j]
        kvf[block * rows : (block + 1) * rows, :lanes] = part
        vt[:HALF, block * rows : (block + 1) * rows] = part.T[HALF:, :]


def attend_forward_head(h, qt_ref, mixed_ref, lse_ref, kvf, vt, qa, sb):
    tokens = qt_ref.shape[1]
    steps = (kvf.shape[0] - (tokens - QC)) // KB
    causal = causal_tile()
    row = pl.multiple_of(h * HEAD_DIM, HEAD_DIM)
    qa[:HALF, :] = qt_ref[pl.ds(row, HEAD_DIM), :]
    tops = []
    for chunk in range(tokens // QC):
        low = chunk * QC
        highest = None
        for b in range(steps):
            first = low + b * KB
            s = dot(kvf[first : first + KB, :], qa[:, low : low + QC])
            if b == steps - 1:
                s = mask_last(s, causal)
            sb[chunk, b * KB : (b + 1) * KB, :] = s
            peak = jnp.max(s.reshape(KB // 8, 8, QC), axis=0)
            highest = peak if highest is None else jnp.maximum(highest, peak)
        tops.append(jnp.max(highest, axis=0, keepdims=True))
    for chunk in range(tokens // QC):
        low = chunk * QC
        shift = tops[chunk] * EXP_SCALE
        total = None
        for b in range(steps):
            first = low + b * KB
            s = sb[chunk, b * KB : (b + 1) * KB, :]
            p = jnp.exp2(s * EXP_SCALE - shift).astype(BF)
            term = dot(vt[:, first : first + KB], p)
            total = term if total is None else total + term
        weight = total[HALF : HALF + 1, :]
        mixed_ref[pl.ds(row, HEAD_DIM), low : low + QC] = (
            total[:HALF, :] * (1.0 / weight)
        ).astype(BF)
        lse_ref[pl.ds(h, 1), :, low : low + QC] = (
            tops[chunk] * HEAD_DIM**-0.5 + jnp.log(weight)
        )[None]


def attend_forward_scratch(keys, lanes, tokens):
    return [
        VMEM((keys, 2 * lanes), BF),
        VMEM((HALF + 16, keys), BF),
        VMEM((2 * lanes, tokens), BF),
        VMEM((tokens // QC, keys - (tokens - QC), QC), F32),
    ]


def attend_forward_kernel(
    kv_ref, feat_ref, qt_ref, qfeat_ref, mixed_ref, lse_ref, kvf, vt, qa, sb
):
    attend_forward_setup(feat_ref, qfeat_ref, kvf, vt, qa)

    def key_head(j, _):
        attend_forward_keys(j, kv_ref, kvf, vt)

        def head(g, _):
            attend_forward_head(j * GROUP + g, qt_ref, mixed_ref, lse_ref, kvf, vt, qa, sb)
            return 0

        lax.fori_loop(0, GROUP, head, 0)
        return 0

    lax.fori_loop(0, kv_ref.shape[1], key_head, 0)


def attend_forward(window, feat, qt, qfeat):
    blocks, kv_heads, rows, lanes = window.shape
    tokens = qt.shape[1]
    return pl.pallas_call(
        attend_forward_kernel,
        out_shape=(
            jax.ShapeDtypeStruct(qt.shape, BF),
            jax.ShapeDtypeStruct((HEADS, 1, tokens), F32),
        ),
        scratch_shapes=attend_forward_scratch(blocks * rows, lanes, tokens),
        compiler_params=pltpu.CompilerParams(vmem_limit_bytes=BIG_VMEM),
        name="attend_forward",
    )(window, feat, qt, qfeat)


def three_parts(value, rows):
    one = value.astype(BF).astype(F32)
    two = (value - one).astype(BF).astype(F32)
    three = value - one - two
    shape = (rows, value.shape[1])
    place = lax.broadcasted_iota(jnp.int32, shape, 0)
    parts = [jnp.broadcast_to(part, shape) for part in (one, two, three)]
    chosen = jnp.where(
        place == 0, parts[0], jnp.where(place == 1, parts[1], jnp.where(place == 2, parts[2], 0.0))
    )
    return chosen.astype(BF)


def attend_backward_setup(feat_ref, kvf, qa, da, rhs):
    lanes = feat_ref.shape[1]
    kvf[:, lanes:] = feat_ref[...]
    qa[HALF:lanes, :] = jnp.zeros((lanes - HALF, qa.shape[1]), BF)
    da[...] = jnp.zeros_like(da)
    rhs[...] = jnp.zeros_like(rhs)


def attend_backward_keys(j, kv_ref, kvf, kt, acc):
    blocks, _, rows, lanes = kv_ref.shape
    for block in range(blocks):
        part = kv_ref[block, j]
        kvf[block * rows : (block + 1) * rows, :lanes] = part
        kt[:, block * rows : (block + 1) * rows] = part.T[:HALF, :]
    acc[...] = jnp.zeros_like(acc)


def attend_backward_head(
    h, qt_ref, qfeat_ref, gradt_ref, mixed_ref, lse_ref, dq_ref, kvf, kt, qa, da, acc, rhs
):
    tokens = qt_ref.shape[1]
    lanes = qfeat_ref.shape[0]
    steps = (kvf.shape[0] - (tokens - QC)) // KB
    causal = causal_tile()
    extra = lanes - ONES
    row = pl.multiple_of(h * HEAD_DIM, HEAD_DIM)
    q = qt_ref[pl.ds(row, HEAD_DIM), :]
    grad = gradt_ref[pl.ds(row, HEAD_DIM), :]
    qa[:HALF, :] = q
    da[HALF:lanes, :] = grad
    mixed = mixed_ref[pl.ds(row, HEAD_DIM), :].astype(F32)
    row_total = jnp.sum(grad.astype(F32) * mixed, axis=0, keepdims=True)
    lse = lse_ref[pl.ds(h, 1), :, :][0]
    qa[lanes : lanes + ONES, :] = qfeat_ref[:ONES, :]
    qa[lanes + ONES :, :] = three_parts(-(HEAD_DIM**0.5) * lse, extra)
    da[lanes + ONES :, :] = three_parts(-row_total, extra)
    query_grads = [None] * (tokens // QC)
    for chunk in range(tokens // QC):
        low = chunk * QC
        rhs[chunk, :HALF, :QC] = q[:, low : low + QC]
        rhs[chunk, HALF:, QC:] = grad[:, low : low + QC]
    for b in range(steps):
        for chunk in range(tokens // QC):
            low = chunk * QC
            first = low + b * KB
            keys = kvf[first : first + KB, :]
            s = dot(keys, qa[:, low : low + QC])
            if b == steps - 1:
                s = mask_last(s, causal)
            p = jnp.exp2(s * EXP_SCALE)
            dp = dot(keys, da[:, low : low + QC])
            ds = (p * dp).astype(BF)
            both = jnp.concatenate([ds, p.astype(BF)], axis=1)
            acc[first : first + KB, :] += dot(both, rhs[chunk], 1, 1)
            term = dot(kt[:, first : first + KB], ds)
            old = query_grads[chunk]
            query_grads[chunk] = term if old is None else old + term
    for chunk in range(tokens // QC):
        low = chunk * QC
        dq_ref[pl.ds(row, HEAD_DIM), low : low + QC] = query_grads[chunk] * HEAD_DIM**-0.5


def attend_backward_done(j, acc, dkv_ref):
    blocks, _, rows, lanes = dkv_ref.shape
    lane = lax.broadcasted_iota(jnp.int32, (1, lanes), 1)
    factor = jnp.where(lane < HALF, HEAD_DIM**-0.5, 1.0)
    for block in range(blocks):
        part = acc[block * rows : (block + 1) * rows, :]
        dkv_ref[block, j] = (part * factor).astype(dkv_ref.dtype)


def attend_backward_scratch(keys, lanes, tokens):
    return [
        VMEM((keys, 2 * lanes), BF),
        VMEM((HALF, keys), BF),
        VMEM((2 * lanes, tokens), BF),
        VMEM((2 * lanes, tokens), BF),
        VMEM((keys, lanes), F32),
        VMEM((tokens // QC, lanes, 2 * QC), BF),
    ]


def attend_backward_kernel(
    kv_ref, feat_ref, qt_ref, qfeat_ref, gradt_ref, mixed_ref, lse_ref, dq_ref, dkv_ref, *scratch
):
    kvf, kt, qa, da, acc, rhs = scratch
    attend_backward_setup(feat_ref, kvf, qa, da, rhs)

    def key_head(j, _):
        attend_backward_keys(j, kv_ref, kvf, kt, acc)

        def head(g, _):
            attend_backward_head(
                j * GROUP + g, qt_ref, qfeat_ref, gradt_ref, mixed_ref, lse_ref, dq_ref, *scratch
            )
            return 0

        lax.fori_loop(0, GROUP, head, 0)
        attend_backward_done(j, acc, dkv_ref)
        return 0

    lax.fori_loop(0, kv_ref.shape[1], key_head, 0)


def attend_backward(window, feat, qt, qfeat, gradt, mixed, lse):
    blocks, kv_heads, rows, lanes = window.shape
    tokens = qt.shape[1]
    return pl.pallas_call(
        attend_backward_kernel,
        out_shape=(
            jax.ShapeDtypeStruct(qt.shape, F32),
            jax.ShapeDtypeStruct(window.shape, BF),
        ),
        scratch_shapes=attend_backward_scratch(blocks * rows, lanes, tokens),
        compiler_params=pltpu.CompilerParams(vmem_limit_bytes=BIG_VMEM),
        name="attend_backward",
    )(window, feat, qt, qfeat, gradt, mixed, lse)


class Place:
    def __init__(self):
        self.r = lax.axis_index("rep")
        self.s = lax.axis_index("shard")
        self.x, self.y = lax.rem(self.r, 2), self.r // 2
        self.z, self.c = self.s // 2, lax.rem(self.s, 2)
        self.rx = self.y * 2 + (1 - self.x)
        self.ry = (1 - self.y) * 2 + self.x
        self.rd = 3 - self.r
        self.x_side = (self.rx, self.s)
        self.y_side = (self.ry, self.s)
        self.core_side = (self.r, self.z * 2 + (1 - self.c))
        self.has_later, self.has_earlier = self.z < 3, self.z > 0
        self.later = (self.r, lax.min(self.s + 2, 7))
        self.earlier = (self.r, lax.max(self.s - 2, 0))

    def z_to(self, k):
        return lax.rem(self.z + k, 4)

    def z_side(self, k):
        return (self.r, self.z_to(k) * 2 + self.c)

    def arrival(self, i):
        low = self.z < 2
        first = jnp.where(self.z == 0, 1, jnp.where(self.z == 1, 0, jnp.where(self.z == 2, 3, 2)))
        if i == 0:
            return first
        if i == 1:
            return jnp.where(low, 2, 1)
        return jnp.where(low, 3, 0)


def greet(at, whole_line):
    barrier = pltpu.get_barrier_semaphore()

    def signal(device):
        pl.semaphore_signal(barrier, inc=1, device_id=device, device_id_type=MESH)

    for device in (at.x_side, at.y_side, at.core_side):
        signal(device)
    if whole_line:
        for k in (1, 2, 3):
            signal(at.z_side(k))
        pl.semaphore_wait(barrier, 6)
        return

    @pl.when(at.has_later)
    def _():
        signal(at.later)

    @pl.when(at.has_earlier)
    def _():
        signal(at.earlier)

    count = 3 + jnp.where(at.has_later, 1, 0) + jnp.where(at.has_earlier, 1, 0)
    pl.semaphore_wait(barrier, count)


def remote(src, dst, send, recv, device):
    return pltpu.make_async_remote_copy(
        src_ref=src, dst_ref=dst, send_sem=send, recv_sem=recv, device_id=device, device_id_type=MESH
    )


class Gather:
    COUNT = 31

    def __init__(self, at, own, full, columns, local_sem, send, recv):
        self.at, self.own, self.full, self.columns = at, own, full, columns
        self.local_sem, self.send, self.recv = local_sem, send, recv
        self.rows = own.shape[0]
        self.quarter, self.half = self.rows // 4, self.rows // 8

    def piece(self, plane, owner, part=None):
        start = owner * self.quarter + (0 if part is None else part * self.half)
        size = self.quarter if part is None else self.half
        return self.full.at[
            plane, pl.ds(pl.multiple_of(start, self.half), size), pl.ds(*self.columns)
        ]

    def copy(self, index, src, dst, device, landed=None):
        return remote(
            src, dst, self.send.at[index], self.recv.at[index if landed is None else landed], device
        )

    def core_copy(self):
        src = self.own.at[:, pl.ds(*self.columns)]
        return self.copy(
            28, src, self.full.at[self.at.s, :, pl.ds(*self.columns)], self.at.core_side
        )

    def local_copy(self):
        return pltpu.make_async_copy(
            self.own.at[:, pl.ds(*self.columns)],
            self.full.at[self.at.s, :, pl.ds(*self.columns)],
            self.local_sem,
        )

    def z_copy(self, up):
        at = self.at
        src = self.own.at[
            pl.ds(pl.multiple_of(at.r * self.quarter, self.quarter), self.quarter),
            pl.ds(*self.columns),
        ]
        device = at.later if up else at.earlier
        return self.copy(29 if up else 30, src, self.piece(at.s, at.r), device, at.z)

    def start_core(self):
        self.local_copy().start()
        self.core_copy().start()

    def start_z(self):
        @pl.when(self.at.has_later)
        def _():
            self.z_copy(True).start()

        @pl.when(self.at.has_earlier)
        def _():
            self.z_copy(False).start()

    def plane(self, i, other=False):
        c = 1 - self.at.c if other else self.at.c
        return self.at.arrival(i) * 2 + c

    def forwards(self, i):
        at = self.at
        chip = at.arrival(i)
        got = self.piece(self.plane(i), at.r)
        return [
            ((chip < at.z) & at.has_later, self.copy(i, got, got, at.later, chip)),
            ((chip > at.z) & at.has_earlier, self.copy(i, got, got, at.earlier, chip)),
        ]

    def out_copies(self, i):
        at, plane = self.at, self.plane(i)
        got = self.piece(plane, at.r)
        return [
            self.copy(4 + i, got, got, at.x_side),
            self.copy(7 + i, got, got, at.y_side),
            self.copy(10 + i, got, got, at.core_side),
        ]

    def cross_copies(self, i):
        at, plane = self.at, self.plane(i)
        one, two = self.piece(plane, at.rx, 0), self.piece(plane, at.ry, 1)
        from_x, from_y = self.piece(plane, at.rx), self.piece(plane, at.ry)
        return [
            self.copy(13 + i, one, one, at.y_side),
            self.copy(16 + i, from_x, from_x, at.core_side),
            self.copy(19 + i, two, two, at.x_side),
            self.copy(22 + i, from_y, from_y, at.core_side),
        ]

    def last_copy(self, i):
        got = self.piece(self.plane(i), self.at.rd)
        return self.copy(25 + i, got, got, self.at.core_side)

    def arrive(self, landed, ref):
        remote(
            ref, ref, self.send.at[landed], self.recv.at[landed], self.at.core_side
        ).wait_recv()

    def z(self, i):
        at = self.at
        self.arrive(at.arrival(i), self.piece(self.plane(i), at.r))
        for condition, copy in self.forwards(i):
            pl.when(condition)(copy.start)
        for copy in self.out_copies(i):
            copy.start()

    def cross(self, i):
        at, plane = self.at, self.plane(i)
        copies = self.cross_copies(i)
        self.arrive(4 + i, self.piece(plane, at.rx))
        copies[0].start()
        copies[1].start()
        self.arrive(7 + i, self.piece(plane, at.ry))
        copies[2].start()
        copies[3].start()

    def last(self, i):
        at, plane = self.at, self.plane(i)
        self.arrive(13 + i, self.piece(plane, at.rd, 0))
        self.arrive(19 + i, self.piece(plane, at.rd, 1))
        self.last_copy(i).start()

    def landed(self):
        at = self.at
        self.arrive(28, self.full.at[at.core_side[1], :, pl.ds(*self.columns)])
        for i in range(3):
            plane = self.plane(i, True)
            self.arrive(10 + i, self.piece(plane, at.r))
            self.arrive(16 + i, self.piece(plane, at.rx))
            self.arrive(22 + i, self.piece(plane, at.ry))
            self.arrive(25 + i, self.piece(plane, at.rd))
        self.local_copy().wait()

    def sent(self):
        at = self.at
        self.core_copy().wait_send()
        pl.when(at.has_later)(self.z_copy(True).wait_send)
        pl.when(at.has_earlier)(self.z_copy(False).wait_send)
        for i in range(3):
            for condition, copy in self.forwards(i):
                pl.when(condition)(copy.wait_send)
            for copy in self.out_copies(i) + self.cross_copies(i) + [self.last_copy(i)]:
                copy.wait_send()


class Spread:
    def __init__(self, at, win, send, recv):
        self.at, self.win, self.sems = at, win, (send, recv)
        even = at.c == 0
        self.near, self.far = jnp.where(even, 1, 3), jnp.where(even, 3, 1)

    def copy(self, n, j, src, dst, device):
        send, recv = self.sems
        return remote(
            self.win.at[src, j], self.win.at[dst, j], send.at[n, j], recv.at[n, j], device
        )

    def first(self, j):
        return self.copy(0, j, 4, 2, self.at.later)

    def twin_own(self, j):
        return self.copy(1, j, 4, 3, self.at.core_side)

    def second(self, j):
        return self.copy(2, j, 2, 0, self.at.later)

    def twin_near(self, j, place):
        return self.copy(3, j, 2, place, self.at.core_side)

    def twin_far(self, j):
        return self.copy(4, j, 0, 1, self.at.core_side)

    def clear(self):
        for block in range(4):
            @pl.when(self.at.s < 4 - block)
            def _(block=block):
                self.win[block] = jnp.zeros(self.win.shape[1:], self.win.dtype)

    def start(self, j):
        pl.when(self.at.has_later)(self.first(j).start)
        pl.when(self.at.c == 0)(self.twin_own(j).start)

    def one(self, j):
        at = self.at

        @pl.when(at.has_earlier)
        def _():
            self.first(j).wait_recv()
            self.twin_near(j, self.near).start()
            pl.when(at.has_later)(self.second(j).start)

    def two(self, j):
        at = self.at

        @pl.when(at.z > 1)
        def _():
            self.second(j).wait_recv()
            pl.when(at.c == 1)(self.twin_far(j).start)

    def landed(self, j):
        at = self.at
        pl.when(at.c == 1)(self.twin_own(j).wait_recv)
        pl.when(at.has_earlier)(self.twin_near(j, self.far).wait_recv)
        pl.when((at.c == 0) & (at.z > 1))(self.twin_far(j).wait_recv)

    def sent(self, j):
        at = self.at
        pl.when(at.has_later)(self.first(j).wait_send)
        pl.when(at.c == 0)(self.twin_own(j).wait_send)
        pl.when(at.has_earlier)(self.twin_near(j, self.near).wait_send)
        pl.when(at.has_earlier & at.has_later)(self.second(j).wait_send)
        pl.when((at.c == 1) & (at.z > 1))(self.twin_far(j).wait_send)


class Collect:
    def __init__(self, at, grads, out, ra, rb, r2, r1, t2, t1, send, recv):
        self.at, self.grads, self.out = at, grads, out
        self.ra, self.rb, self.r2, self.r1, self.t2, self.t1 = ra, rb, r2, r1, t2, t1
        self.sems = (send, recv)

    def copy(self, n, j, src, dst, device):
        send, recv = self.sems
        return remote(src, dst, send.at[n, j], recv.at[n, j], device)

    def twin_a(self, j):
        return self.copy(0, j, self.grads.at[3, j], self.ra.at[j], self.at.core_side)

    def twin_b(self, j):
        return self.copy(1, j, self.grads.at[1, j], self.rb.at[j], self.at.core_side)

    def far(self, j):
        return self.copy(2, j, self.t2.at[j], self.r2.at[j], self.at.earlier)

    def near(self, j):
        return self.copy(3, j, self.t1.at[j], self.r1.at[j], self.at.earlier)

    def start(self, j):
        self.twin_b(j).start()
        self.twin_a(j).start()

    def one(self, j):
        self.twin_b(j).wait_recv()
        self.twin_a(j).wait_recv()
        even = self.at.c == 0
        from_a, from_b = self.ra[j].astype(F32), self.rb[j].astype(F32)
        none = jnp.zeros_like(from_a)
        self.t2[j] = (self.grads[0, j].astype(F32) + jnp.where(even, none, from_b)).astype(BF)
        pl.when(self.at.z > 1)(self.far(j).start)
        self.t1[j] = (self.grads[2, j].astype(F32) + jnp.where(even, from_b, from_a)).astype(BF)
        self.out[j] = self.grads[4, j].astype(F32) + jnp.where(even, from_a, none)

    def two(self, j):
        at = self.at

        @pl.when(at.has_earlier & at.has_later)
        def _():
            self.far(j).wait_recv()
            self.t1[j] = (self.t1[j].astype(F32) + self.r2[j].astype(F32)).astype(BF)

        pl.when(at.has_earlier)(self.near(j).start)

    def three(self, j):
        at = self.at

        @pl.when(at.has_later)
        def _():
            self.near(j).wait_recv()
            self.out[j] = self.out[j] + self.r1[j].astype(F32)

    def sent(self, j):
        at = self.at
        self.twin_a(j).wait_send()
        self.twin_b(j).wait_send()
        pl.when(at.z > 1)(self.far(j).wait_send)
        pl.when(at.has_earlier)(self.near(j).wait_send)


class Reduce:
    COUNT = 35

    def __init__(self, at, parts, out, own, r0, r1a, r1b, r2a, r2b, r3, local_sem, send, recv):
        self.at, self.parts, self.out, self.own = at, parts, out, own
        self.r0, self.r1a, self.r1b, self.r2a, self.r2b, self.r3 = r0, r1a, r1b, r2a, r2b, r3
        self.local_sem, self.send, self.recv = local_sem, send, recv
        self.rows = out.shape[0]
        self.quarter, self.half = self.rows // 4, self.rows // 8

    @staticmethod
    def scratch(rows, columns):
        half = rows // 8
        return [
            VMEM((4, rows, columns), BF),
            VMEM((4, rows, columns), BF),
            VMEM((4, 2, half, columns), BF),
            VMEM((4, 2, half, columns), BF),
            VMEM((4, half, columns), BF),
            VMEM((4, half, columns), BF),
            VMEM((3, 2 * half, columns), BF),
            DMA((4,)),
            DMA((Reduce.COUNT,)),
            DMA((Reduce.COUNT,)),
        ]

    def copy(self, index, src, dst, device):
        return remote(src, dst, self.send.at[index], self.recv.at[index], device)

    def arrive(self, index, ref):
        self.copy(index, ref, ref, self.at.core_side).wait_recv()

    def spot(self, owner, part):
        start = owner * self.quarter + part * self.half
        return pl.ds(pl.multiple_of(start, self.half), self.half)

    def piece(self, owner):
        start = pl.multiple_of(owner * self.quarter, self.quarter)
        return self.out.at[pl.ds(start, self.quarter), :]

    def add_into(self, k, where, ref):
        old = self.own[k, where, :].astype(F32)
        self.own[k, where, :] = (old + ref[...].astype(F32)).astype(BF)

    def local_copy(self, k):
        z = self.at.z_to(k + 1 if k < 3 else 0)
        return pltpu.make_async_copy(
            self.parts.at[z * 2 + self.at.c], self.own.at[k], self.local_sem.at[k]
        )

    def core_copy(self, k):
        z = self.at.z_to(k + 1 if k < 3 else 0)
        return self.copy(k, self.parts.at[z * 2 + 1 - self.at.c], self.r0.at[k], self.at.core_side)

    def one_copies(self, k):
        at, copies = self.at, []
        for i in range(2):
            a = self.own.at[k, self.spot(i * 2 + 1 - at.x, 0), :]
            b = self.own.at[k, self.spot((1 - at.y) * 2 + i, 1), :]
            copies.append(self.copy(4 + 4 * k + i, a, self.r1a.at[k, i], at.x_side))
            copies.append(self.copy(6 + 4 * k + i, b, self.r1b.at[k, i], at.y_side))
        return copies

    def two_copies(self, k):
        at = self.at
        a, b = self.own.at[k, self.spot(at.ry, 0), :], self.own.at[k, self.spot(at.rx, 1), :]
        return [
            self.copy(20 + 2 * k, a, self.r2a.at[k], at.y_side),
            self.copy(21 + 2 * k, b, self.r2b.at[k], at.x_side),
        ]

    def z_copy(self, k):
        at = self.at
        mine = pl.ds(pl.multiple_of(at.r * self.quarter, self.quarter), self.quarter)
        return self.copy(28 + k, self.own.at[k, mine, :], self.r3.at[k], at.z_side(k + 1))

    def back_copies(self):
        at, piece = self.at, self.piece
        a, b = self.out.at[self.spot(at.rx, 0), :], self.out.at[self.spot(at.ry, 1), :]
        return [
            self.copy(31, piece(at.r), piece(at.r), at.x_side),
            self.copy(32, piece(at.r), piece(at.r), at.y_side),
            self.copy(33, a, a, at.y_side),
            self.copy(34, b, b, at.x_side),
        ]

    def start(self, k):
        self.local_copy(k).start()
        self.core_copy(k).start()

    def zero(self, k):
        self.local_copy(k).wait()
        self.arrive(k, self.r0.at[k])

        def add_rows(i, _):
            where = pl.ds(pl.multiple_of(i * self.half, self.half), self.half)
            self.add_into(k, where, self.r0.at[k, where, :])
            return 0

        lax.fori_loop(0, self.rows // self.half, add_rows, 0)
        for copy in self.one_copies(k):
            copy.start()

    def one(self, k):
        at = self.at
        for i in range(2):
            self.arrive(4 + 4 * k + i, self.r1a.at[k, i])
            self.arrive(6 + 4 * k + i, self.r1b.at[k, i])
            self.add_into(k, self.spot(i * 2 + at.x, 0), self.r1a.at[k, i])
            self.add_into(k, self.spot(at.y * 2 + i, 1), self.r1b.at[k, i])
        for copy in self.two_copies(k):
            copy.start()

    def two(self, k):
        at = self.at
        self.arrive(20 + 2 * k, self.r2a.at[k])
        self.arrive(21 + 2 * k, self.r2b.at[k])
        self.add_into(k, self.spot(at.r, 0), self.r2a.at[k])
        self.add_into(k, self.spot(at.r, 1), self.r2b.at[k])
        if k < 3:
            self.z_copy(k).start()

    def three(self):
        at = self.at
        for k in range(3):
            self.arrive(28 + k, self.r3.at[k])
        for i in range(2):
            where = pl.ds(i * self.half, self.half)
            total = self.own[3, self.spot(at.r, i), :].astype(F32)
            for k in range(3):
                total += self.r3[k, where, :].astype(F32)
            self.out[self.spot(at.r, i), :] = total.astype(BF)
        copies = self.back_copies()
        copies[0].start()
        copies[1].start()

    def four(self):
        at = self.at
        copies = self.back_copies()
        self.arrive(31, self.piece(at.rx))
        copies[2].start()
        self.arrive(32, self.piece(at.ry))
        copies[3].start()

    def five(self):
        at = self.at
        self.arrive(33, self.out.at[self.spot(at.rd, 0), :])
        self.arrive(34, self.out.at[self.spot(at.rd, 1), :])
        for k in range(4):
            for copy in [self.core_copy(k)] + self.one_copies(k) + self.two_copies(k):
                copy.wait_send()
        for k in range(3):
            self.z_copy(k).wait_send()
        for copy in self.back_copies():
            copy.wait_send()


def at_steps(i, events):
    for n, event in events:
        pl.when(i == n)(event)


def front_kernel(
    x_ref,
    cos_ref,
    sin_ref,
    feat_ref,
    qfeat_ref,
    attend_own,
    rest_own,
    attend_ref,
    rest_ref,
    win_ref,
    qt_ref,
    mixed_ref,
    lse_ref,
    kvf,
    vt,
    qa,
    sb,
    hidden,
    kvt,
    local_sems,
    gather_send,
    gather_recv,
    spread_send,
    spread_recv,
):
    at = Place()
    shard_count, rows, columns = attend_ref.shape
    width = shard_count * rows
    tokens = x_ref.shape[0]
    kv_heads = win_ref.shape[1]
    own_rows = D // shard_count
    cut = 2 * FF
    greet(at, False)

    def gather(n, own, full, cols):
        return Gather(
            at, own, full, cols, local_sems.at[n], gather_send.at[n], gather_recv.at[n]
        )

    first = gather(0, attend_own, attend_ref, (0, columns))
    second = gather(1, rest_own, rest_ref, (0, cut))
    third = gather(2, rest_own, rest_ref, (cut, rest_own.shape[1] - cut))
    spread = Spread(at, win_ref, spread_send, spread_recv)

    first.start_z()
    first.start_core()
    second.start_core()
    third.start_core()
    spread.clear()
    attend_forward_setup(feat_ref, qfeat_ref, kvf, vt, qa)
    for i in range(3):
        first.z(i)
    second.start_z()
    for i in range(3):
        first.cross(i)
    second.z(0)
    for i in range(3):
        first.last(i)
    first.landed()

    inputs = x_ref[...].astype(F32)
    scale = lax.rsqrt(jnp.sum(inputs * inputs, axis=-1, keepdims=True) * (1.0 / D) + eps_norm)
    for s in range(shard_count):
        lane = slice(s * rows, (s + 1) * rows)
        gain = attend_ref[s, own_rows : own_rows + 1, :rows].astype(F32)
        hidden[:, lane] = (x_ref[:, lane].astype(F32) * scale * gain).astype(BF)

    def project(start):
        stop = min(start + 256, columns)
        weight = attend_ref[:, :, start:stop].reshape(width, stop - start)
        flipped = dot(hidden[...], weight).T
        for low in range(0, stop - start, HEAD_DIM):
            column = start + low
            head = flipped[low : low + HEAD_DIM, :]
            if column < QW + KW:
                half = HEAD_DIM // 2
                front, back = head[:half], head[half:]
                head = jnp.concatenate(
                    [
                        front * cos_ref[...] - back * sin_ref[...],
                        back * cos_ref[...] + front * sin_ref[...],
                    ],
                    axis=0,
                )
            if column < QW:
                qt_ref[column : column + HEAD_DIM, :] = head.astype(BF)
            elif column < QW + KW:
                kvt[(column - QW) // HEAD_DIM, :HALF, :] = head.astype(BF)
            else:
                kvt[(column - QW - KW) // HEAD_DIM, HALF:, :] = head.astype(BF)

    split = QW // 128 * 128
    for start in range(split, columns, 256):
        project(start)
    for j in range(kv_heads):
        win_ref[4, j] = kvt[j].T
        spread.start(j)
    second.z(1)
    third.start_z()
    for start in range(0, split, 256):
        project(start)
    spread.one(0)
    second.z(2)
    spread.one(1)
    spread.two(0)
    events = [
        (0, lambda: third.z(0)),
        (1, lambda: second.cross(0)),
        (2, lambda: third.z(1)),
        (3, lambda: second.cross(1)),
        (4, lambda: third.z(2)),
        (5, lambda: second.cross(2)),
        (6, lambda: third.cross(0)),
        (7, lambda: second.last(0)),
        (8, lambda: third.cross(1)),
        (9, lambda: second.last(1)),
        (10, lambda: third.cross(2)),
        (11, lambda: second.last(2)),
        (12, lambda: third.last(0)),
        (13, lambda: third.last(1)),
        (14, lambda: third.last(2)),
    ]

    def key_head(j, _):
        pl.when(j + 2 < kv_heads)(lambda: spread.one(j + 2))
        pl.when(j + 1 < kv_heads)(lambda: spread.two(j + 1))
        spread.landed(j)
        attend_forward_keys(j, win_ref, kvf, vt)

        def head(g, _):
            h = j * GROUP + g
            attend_forward_head(h, qt_ref, mixed_ref, lse_ref, kvf, vt, qa, sb)
            at_steps(h, events)
            return 0

        lax.fori_loop(0, GROUP, head, 0)
        spread.sent(j)
        return 0

    lax.fori_loop(0, kv_heads, key_head, 0)
    second.landed()
    third.landed()
    for part in (first, second, third):
        part.sent()


def front(x, cosine, sine, feat, qfeat, attend_own, rest_own, shard_count, number):
    tokens, width = x.shape
    keys, lanes = feat.shape
    rows = attend_own.shape[0]
    window = (keys // tokens, KV_HEADS, tokens, lanes)
    return pl.pallas_call(
        front_kernel,
        out_shape=(
            jax.ShapeDtypeStruct((shard_count,) + attend_own.shape, BF),
            jax.ShapeDtypeStruct((shard_count,) + rest_own.shape, BF),
            jax.ShapeDtypeStruct(window, BF),
            jax.ShapeDtypeStruct((QW, tokens), BF),
            jax.ShapeDtypeStruct((QW, tokens), BF),
            jax.ShapeDtypeStruct((HEADS, 1, tokens), F32),
        ),
        in_specs=[pl.BlockSpec(memory_space=VMEM)] * 6 + [pl.BlockSpec(memory_space=ANY)],
        out_specs=(
            pl.BlockSpec(memory_space=VMEM),
            pl.BlockSpec(memory_space=ANY),
        )
        + (pl.BlockSpec(memory_space=VMEM),) * 4,
        scratch_shapes=attend_forward_scratch(keys, lanes, tokens)
        + [
            VMEM((tokens, width), BF),
            VMEM((KV_HEADS, lanes, tokens), BF),
            DMA((3,)),
            DMA((3, Gather.COUNT)),
            DMA((3, Gather.COUNT)),
            DMA((5, KV_HEADS)),
            DMA((5, KV_HEADS)),
        ],
        compiler_params=pltpu.CompilerParams(
            collective_id=number, has_side_effects=True, vmem_limit_bytes=BIG_VMEM
        ),
        name="front",
    )(x, cosine, sine, feat, qfeat, attend_own, rest_own)


def back_kernel(
    parts_ref,
    win_ref,
    feat_ref,
    qt_ref,
    qfeat_ref,
    gradt_ref,
    mixed_ref,
    lse_ref,
    dq_ref,
    pairs_ref,
    sum_ref,
    kvf,
    kt,
    qa,
    da,
    acc,
    rhs,
    grads,
    ra,
    rb,
    r2,
    r1,
    t2,
    t1,
    collect_send,
    collect_recv,
    *reduce_scratch,
):
    at = Place()
    kv_heads = win_ref.shape[1]
    greet(at, True)
    total = Reduce(at, parts_ref, sum_ref, *reduce_scratch)
    collect = Collect(
        at, grads, pairs_ref, ra, rb, r2, r1, t2, t1, collect_send, collect_recv
    )
    for k in range(4):
        total.start(k)
    attend_backward_setup(feat_ref, kvf, qa, da, rhs)
    total.zero(0)
    events = [
        (0, lambda: total.zero(1)),
        (1, lambda: total.zero(2)),
        (2, lambda: total.zero(3)),
        (4, lambda: total.one(0)),
        (6, lambda: total.one(1)),
        (7, lambda: total.two(0)),
        (8, lambda: total.one(2)),
        (9, lambda: total.two(1)),
        (11, lambda: total.one(3)),
        (12, lambda: total.two(2)),
        (14, lambda: total.two(3)),
    ]

    def key_head(j, _):
        attend_backward_keys(j, win_ref, kvf, kt, acc)

        def head(g, _):
            h = j * GROUP + g
            attend_backward_head(
                h,
                qt_ref,
                qfeat_ref,
                gradt_ref,
                mixed_ref,
                lse_ref,
                dq_ref,
                kvf,
                kt,
                qa,
                da,
                acc,
                rhs,
            )
            at_steps(h, events)
            return 0

        lax.fori_loop(0, GROUP, head, 0)
        attend_backward_done(j, acc, grads)
        collect.start(j)
        pl.when(j > 0)(lambda: collect.one(j - 1))
        pl.when(j > 1)(lambda: collect.two(j - 2))
        pl.when(j > 2)(lambda: collect.three(j - 3))
        return 0

    lax.fori_loop(0, kv_heads, key_head, 0)
    collect.one(kv_heads - 1)
    collect.two(kv_heads - 2)
    total.three()
    collect.two(kv_heads - 1)
    for j in range(kv_heads - 3, kv_heads):
        collect.three(j)
    total.four()
    for j in range(kv_heads):
        collect.sent(j)
    total.five()


def back(parts, window, feat, qt, qfeat, gradt, mixed, lse, number):
    blocks, kv_heads, tokens, lanes = window.shape
    _, rows, columns = parts.shape
    pairs = (kv_heads, tokens, lanes)
    return pl.pallas_call(
        back_kernel,
        out_shape=(
            jax.ShapeDtypeStruct(qt.shape, F32),
            jax.ShapeDtypeStruct(pairs, F32),
            jax.ShapeDtypeStruct((rows, columns), BF),
        ),
        in_specs=[pl.BlockSpec(memory_space=ANY)] + [pl.BlockSpec(memory_space=VMEM)] * 7,
        out_specs=(pl.BlockSpec(memory_space=VMEM),) * 3,
        scratch_shapes=attend_backward_scratch(blocks * tokens, lanes, tokens)
        + [VMEM(window.shape, BF)]
        + [VMEM(pairs, BF)] * 6
        + [DMA((4, kv_heads)), DMA((4, kv_heads))]
        + Reduce.scratch(rows, columns),
        compiler_params=pltpu.CompilerParams(
            collective_id=number, has_side_effects=True, vmem_limit_bytes=BIG_VMEM
        ),
        name="back",
    )(parts, window, feat, qt, qfeat, gradt, mixed, lse)


def reduce_kernel(parts_ref, out_ref, *scratch):
    at = Place()
    greet(at, True)
    total = Reduce(at, parts_ref, out_ref, *scratch)
    for k in range(4):
        total.start(k)
    for k in range(4):
        total.zero(k)
    for k in range(4):
        total.one(k)
    for k in range(4):
        total.two(k)
    total.three()
    total.four()
    total.five()


def reduce_rows(parts, direct, number):
    _, rows, columns = parts.shape
    if not direct:
        own = lax.psum_scatter(parts, "shard", scatter_dimension=0)
        return lax.psum(own, "rep")
    return pl.pallas_call(
        reduce_kernel,
        out_shape=jax.ShapeDtypeStruct((rows, columns), BF),
        in_specs=[pl.BlockSpec(memory_space=ANY)],
        out_specs=pl.BlockSpec(memory_space=VMEM),
        scratch_shapes=Reduce.scratch(rows, columns),
        compiler_params=pltpu.CompilerParams(
            collective_id=number, has_side_effects=True, vmem_limit_bytes=BIG_VMEM
        ),
        name="reduce",
    )(parts)


def spread_pairs(pairs, reach):
    devices = range(lax.axis_size("shard"))
    blocks = []
    for distance in range(reach, 0, -1):
        route = [(i - distance, i) for i in devices if i - distance in devices]
        blocks.append(lax.ppermute(pairs, "shard", route))
    return jnp.stack(blocks + [pairs])


def collect_pairs(grads, reach):
    devices = range(lax.axis_size("shard"))
    own = grads[reach].astype(F32)
    for distance in range(1, reach + 1):
        route = [(i, i - distance) for i in devices if i - distance in devices]
        own = own + lax.ppermute(grads[reach - distance], "shard", route).astype(F32)
    return own


def angles(positions):
    half_dim = HEAD_DIM // 2
    inverse = rope_base ** (-(2.0 * jnp.arange(half_dim, dtype=F32) / HEAD_DIM))
    phases = positions.astype(F32)[:, None] * inverse[None, :]
    return (jnp.cos(phases)[:, None, :], jnp.sin(phases)[:, None, :])


def rotate(tensor, cosine_table, sine_table):
    half_dim = HEAD_DIM // 2
    front, back = tensor[..., :half_dim], tensor[..., half_dim:]
    return jnp.concatenate(
        [front * cosine_table - back * sine_table, back * cosine_table + front * sine_table],
        axis=-1,
    )


def norm_back(upstream, normed, scale_rows):
    mean = jnp.sum(upstream * normed, axis=-1, keepdims=True) * (1.0 / D)
    return scale_rows * (upstream - normed * mean)


def adam_step(weight_now, gradient, first, second, decay_factor):
    old_weight = weight_now.astype(F32)
    moment = beta_one * first + (1.0 - beta_one) * gradient
    square = beta_two * second + (1.0 - beta_two) * gradient * gradient
    corrected = moment / (1.0 - beta_one**STEP)
    divisor = jnp.sqrt(square / (1.0 - beta_two**STEP)) + adam_eps
    update = -learn_rate * (corrected / divisor + decay_factor * old_weight)
    return (gradient, moment, square, old_weight + update, update)


def shards(
    direct,
    block_input,
    block_cotangent,
    lengths,
    attend_gain,
    attend_weight,
    output_weight,
    expand_gain,
    expand_weight,
    shrink_weight,
    attend_gain_first,
    attend_weight_first,
    output_weight_first,
    expand_gain_first,
    expand_weight_first,
    shrink_weight_first,
    attend_gain_second,
    attend_weight_second,
    output_weight_second,
    expand_gain_second,
    expand_weight_second,
    shrink_weight_second,
):
    tokens = block_input.shape[0]
    shard_count = lax.axis_size("shard")
    token_count = tokens * shard_count * lax.axis_size("rep")
    reach = (MAXLEN - 2) // tokens + 1
    own_rows = attend_weight.shape[0]
    rows = -(-(own_rows + 2) // 16) * 16
    width = shard_count * rows

    def padded(tensor):
        blocks = tensor.reshape(tokens, shard_count, own_rows)
        return jnp.pad(blocks, ((0, 0), (0, 0), (0, rows - own_rows))).reshape(tokens, width)

    def unpadded(tensor):
        return tensor.reshape(tokens, shard_count, rows)[:, :, :own_rows].reshape(tokens, D)

    def with_gain(weight, gain):
        tail = jnp.pad(gain[None, :], ((0, rows - own_rows - 1), (0, weight.shape[1] - own_rows)))
        return jnp.concatenate([weight, tail], axis=0)

    def gain_of(planes):
        return jnp.pad(
            planes[:, own_rows, :own_rows], ((0, 0), (0, rows - own_rows))
        ).reshape(1, width).astype(F32)

    def add_gain(planes, term):
        row = term.reshape(shard_count, 1, rows).astype(planes.dtype)
        return lax.dynamic_update_slice(planes, row, (0, own_rows, 0))

    first_row = lax.axis_index("shard") * tokens
    local_index = first_row + jnp.arange(tokens, dtype=jnp.int32)
    key_index = first_row - reach * tokens + jnp.arange((reach + 1) * tokens, dtype=jnp.int32)
    ends = jnp.cumsum(lengths[0], dtype=jnp.int32)
    starts = ends - lengths[0]
    seq_count = lengths.shape[1]
    in_key = (key_index[:, None] >= starts[None, :]) & (key_index[:, None] < ends[None, :])
    in_query = (local_index[None, :] >= starts[:, None]) & (local_index[None, :] < ends[:, None])
    lanes = 2 * HEAD_DIM
    feat = jnp.concatenate(
        [
            in_key.astype(BF),
            (key_index < 0).astype(BF)[:, None],
            jnp.zeros((key_index.shape[0], ONES - seq_count - 1), BF),
            jnp.ones((key_index.shape[0], lanes - ONES), BF),
        ],
        axis=1,
    )
    qfeat = jnp.concatenate(
        [
            jnp.where(in_query, 0.0, NEG).astype(BF),
            jnp.full((1, tokens), NEG, BF),
            jnp.zeros((lanes - seq_count - 1, tokens), BF),
        ],
        axis=0,
    )
    start_index = jnp.sum(in_query * starts[:, None], axis=0, dtype=jnp.int32)
    cosine_table, sine_table = angles(local_index - start_index)

    attend_own = with_gain(attend_weight, attend_gain)
    rest_own = with_gain(
        jnp.concatenate([expand_weight, shrink_weight.T, output_weight.T], axis=1), expand_gain
    )
    inputs = padded(block_input)
    if direct:
        attend_planes, rest_planes, window, qt, mixedt, lse = front(
            inputs,
            cosine_table[:, 0].T,
            sine_table[:, 0].T,
            feat,
            qfeat,
            attend_own,
            rest_own,
            shard_count,
            0,
        )
    else:
        attend_planes = lax.all_gather(attend_own, "shard", axis=0)
        rest_planes = lax.all_gather(rest_own, "shard", axis=0)
    gain_one, gain_two = gain_of(attend_planes), gain_of(rest_planes)
    joint_weight = attend_planes.reshape(width, JW)
    rest = rest_planes.reshape(width, rest_own.shape[1])
    expand_full, shrink_full, out_full = rest[:, : 2 * FF], rest[:, 2 * FF : 3 * FF], rest[:, 3 * FF :]
    real = (jnp.arange(width, dtype=jnp.int32) % rows < own_rows)[None, :]

    inputs = inputs.astype(F32)
    scale_one = lax.rsqrt(jnp.sum(inputs * inputs, axis=-1, keepdims=True) * (1.0 / D) + eps_norm)
    normed_one = inputs * scale_one
    hidden_one = (normed_one * gain_one).astype(BF)
    if not direct:
        joint = dot(hidden_one, joint_weight)
        queries = rotate(joint[:, :QW].reshape(tokens, HEADS, HEAD_DIM), cosine_table, sine_table)
        key_rows = rotate(
            joint[:, QW : QW + KW].reshape(tokens, KV_HEADS, HEAD_DIM), cosine_table, sine_table
        )
        values = joint[:, QW + KW :].reshape(tokens, KV_HEADS, HEAD_DIM)
        pairs = jnp.concatenate([key_rows, values], axis=-1).astype(BF).transpose(1, 0, 2)
        qt = queries.astype(BF).reshape(tokens, QW).T
        window = spread_pairs(pairs, reach)
        mixedt, lse = attend_forward(window, feat, qt, qfeat)
    middle = inputs + dot(mixedt, out_full, 0, 1)
    scale_two = lax.rsqrt(jnp.sum(middle * middle, axis=-1, keepdims=True) * (1.0 / D) + eps_norm)
    normed_two = middle * scale_two
    hidden_two = (normed_two * gain_two).astype(BF)
    gate_up = dot(hidden_two, expand_full)
    gate_value, upper_value = gate_up[:, :FF], gate_up[:, FF:]
    sigmoid_gate = jax.nn.sigmoid(gate_value)
    inner_rows = (gate_value * sigmoid_gate * upper_value).astype(BF)
    block_output = middle + dot(inner_rows, shrink_full, 1, 1)

    cotangent = padded(block_cotangent)
    shrink_term = dot(cotangent, inner_rows, 0, 0)
    inner_grad = dot(cotangent, shrink_full)
    gate_grad = (
        inner_grad * upper_value * sigmoid_gate * (1.0 + gate_value * (1.0 - sigmoid_gate))
    ).astype(BF)
    upper_grad = (inner_grad * gate_value * sigmoid_gate).astype(BF)
    gate_up_grad = jnp.concatenate([gate_grad, upper_grad], axis=1)
    expand_term = dot(hidden_two, gate_up_grad, 0, 0)
    hidden_two_grad = jnp.where(real, dot(gate_up_grad, expand_full, 1, 1), 0.0)
    gain_two_term = jnp.sum(hidden_two_grad * normed_two, axis=0)
    middle_grad = cotangent.astype(F32) + norm_back(
        hidden_two_grad * gain_two, normed_two, scale_two
    )
    branch_grad = middle_grad.astype(BF)
    output_term = dot(branch_grad, mixedt, 0, 1)
    gradt = dot(out_full, branch_grad, 0, 1).astype(BF)
    rest_term = jnp.concatenate(
        [expand_term.astype(BF), shrink_term.astype(BF), output_term.astype(BF)], axis=1
    ).reshape(shard_count, rows, rest_own.shape[1])
    rest_term = add_gain(rest_term, gain_two_term)
    if direct:
        dqt, own_pairs, rest_sum = back(
            rest_term, window, feat, qt, qfeat, gradt, mixedt, lse, 1
        )
    else:
        rest_sum = reduce_rows(rest_term, direct, 3)
        dqt, dwindow = attend_backward(window, feat, qt, qfeat, gradt, mixedt, lse)
        own_pairs = collect_pairs(dwindow, reach)
    own_pairs = own_pairs.transpose(1, 0, 2)
    dq = dqt.T.reshape(tokens, HEADS, HEAD_DIM)
    query_raw = rotate(dq, cosine_table, -sine_table).reshape(tokens, QW)
    key_raw = rotate(own_pairs[..., :HEAD_DIM], cosine_table, -sine_table).reshape(tokens, KW)
    value_raw = own_pairs[..., HEAD_DIM:].reshape(tokens, KW)
    joint_grad = jnp.concatenate([query_raw, key_raw, value_raw], axis=1).astype(BF)
    joint_term = dot(hidden_one, joint_grad, 0, 0).astype(BF)
    hidden_one_grad = jnp.where(real, dot(joint_grad, joint_weight, 1, 1), 0.0)
    gain_one_term = jnp.sum(hidden_one_grad * normed_one, axis=0)
    input_gradient = middle_grad + norm_back(hidden_one_grad * gain_one, normed_one, scale_one)
    attend_sum = reduce_rows(
        add_gain(joint_term.reshape(shard_count, rows, JW), gain_one_term), direct, 2
    )

    grad_scale = grad_factor * token_count ** (-0.5)
    rest_grad, attend_grad = (total.astype(F32) * grad_scale for total in (rest_sum, attend_sum))
    first_gain = adam_step(
        attend_gain, attend_grad[own_rows, :own_rows], attend_gain_first, attend_gain_second, 0.0
    )
    first_joint = adam_step(
        attend_weight,
        attend_grad[:own_rows],
        attend_weight_first,
        attend_weight_second,
        decay_rate,
    )
    first_output = adam_step(
        output_weight,
        rest_grad[:own_rows, 3 * FF :].T,
        output_weight_first,
        output_weight_second,
        decay_rate,
    )
    second_gain = adam_step(
        expand_gain, rest_grad[own_rows, :own_rows], expand_gain_first, expand_gain_second, 0.0
    )
    second_expand = adam_step(
        expand_weight,
        rest_grad[:own_rows, : 2 * FF],
        expand_weight_first,
        expand_weight_second,
        decay_rate,
    )
    second_shrink = adam_step(
        shrink_weight,
        rest_grad[:own_rows, 2 * FF : 3 * FF].T,
        shrink_weight_first,
        shrink_weight_second,
        decay_rate,
    )
    steps = (first_gain, first_joint, first_output, second_gain, second_expand, second_shrink)
    changed = [step[4] if step[0].ndim == 1 else step[3] for step in steps]
    return (
        unpadded(block_output),
        unpadded(input_gradient),
        *[step[0] for step in steps],
        *[step[1] for step in steps],
        *[step[2] for step in steps],
        *changed,
    )


def solution(mesh):
    whole_rows = P(("rep", "shard"), None)
    state = (P("shard"), P("shard", None), P(None, "shard")) * 2
    state = (state[0], state[1], state[2], state[3], state[4], state[5])
    direct = mesh.shape["rep"] == 4 and mesh.shape["shard"] == 8
    return jax.shard_map(
        functools.partial(shards, direct),
        mesh=mesh,
        in_specs=(whole_rows, whole_rows, P("rep", None), *state, *state, *state),
        out_specs=(whole_rows, whole_rows, *state, *state, *state, *state),
        check_vma=False,
    )
```

time: 647 us -> 481 us (0.74)
  Pallas kernels: 458 us -> 301 us
    pallas_call x2 -> x1, Pallas kernels: 180 us -> 38.1 us  [reduce_rows(): pl.pallas_call(reduce_kernel, out_shape=jax.ShapeDtypeStruct((rows, colum...]
    pallas_call x6 -> x2, Pallas kernels: 277 us -> 263 us  [the longest x1 163 us: back(): pl.pallas_call(back_kernel, out_shape=(jax.ShapeDtypeStruct(qt.shape, F32...]
    dot_general x12 -> x11, matrix products: 78.3 us -> 73.8 us  [dot(): lax.dot_general(a, b, (((ca,), (cb,)), ((), ())), preferred_element_type=...]
    unnamed x101 -> x90, local copies, waits for them, and re-layouts: 16.5 us -> 15.6 us
where the time goes in v2:
time: 481 us; the launch traced here: 473 us
  Pallas kernels  301 us (63%)
  matrix products  73.8 us (15%)
  other arithmetic  53.1 us (11%)
  local copies, waits for them, and re-layouts  43.4 us (9%)
    pallas_call x1, Pallas kernels, back(): pl.pallas_call(back_kernel, out_shape=(jax.ShapeDtypeStruct(qt.shape, F32...  163 us
    pallas_call x1, Pallas kernels, front(): pl.pallas_call(front_kernel, out_shape=(jax.ShapeDtypeStruct((shard_count...  99.7 us
    dot_general x11, matrix products, dot(): lax.dot_general(a, b, (((ca,), (cb,)), ((), ())), preferred_element_type=...  73.8 us
    pallas_call x1, Pallas kernels, reduce_rows(): pl.pallas_call(reduce_kernel, out_shape=jax.ShapeDtypeStruct((rows, colum...  38.1 us
    unnamed x90, local copies, waits for them, and re-layouts  15.6 us
    concatenate x1, other arithmetic, shards(): jnp.concatenate([expand_term.astype(BF), shrink_term.astype(BF), output_t...  14.7 us
    add x4, other arithmetic, adam_step(): return (gradient, moment, square, old_weight + update, update)  13.4 us

profile of v2, /device:TPU:0, one launch (start us, length us, event | category | flops | bytes accessed | tf_op | source)
XLA Modules:
  0.0 473.2 jit_solution(2229706079607067308)
XLA Ops:
  5.5 1.8 copy.87
  8.9 1.8 fusion.56.attend_own
  12.7 1.2 and_convert_fusion
  14.1 1.3 maximum_maximum_fusion.feat_ref
  16.1 1.0 multiply_reduce_fusion.1
  17.4 1.2 copy.137
  18.7 1.5 copy.89
  20.1 1.4 pad.26
  21.6 3.2 fusion.16.rest_own
  24.8 99.7 %front.1 = (bf16[8,128,1600]{2,1,0:T(8,128)(2,1)}, bf16[8,128,8640]{2,1,0:T(8,128)(2,1)}, bf16[5,5,512,128]{3,2,1,0:T(8,128)(2,1)}, bf16[960,512]{1,0:T(8,128)(2...) custom-call(bf16[512,1024]{1,0:T(8,128)(2,1)} %bitcast.119, f32[32,512]{1,0:T(8,128)} %get-tuple-element.159.cos_ref, ...), custom_call_target="tpu_custom_call" | custom-call | tf_op jit(solution)/shard_map/front/pallas_call | solution.py:946
  126.0 3.4 multiply_reduce_fusion.3
  129.5 13.1 %fusion.2 = f32[512,5120]{1,0:T(8,128)} fusion(bf16[1024,8640]{1,0:T(8,128)(2,1)} %bitcast.144, f32[512,1024]{1,0:T(8,128)S(1)} %get-tuple-element.161, f32[1024]{0:T(1024)S(1)} %bitcast_convert_fusion.1, f32[512]{0:T(512)S(1)} %add_rsqrt_fusion.1), kind=kOutput, calls=%fused_computation.4 | convolution fusion | flops 5370281984 | bytes 23074816 | tf_op jit(solution)/shard_map/dot_general | solution.py:49
  142.7 9.1 %multiply_convert_fusion.1 = (bf16[512,2560]{1,0:T(8,128)(2,1)}, bf16[512,2560]{1,0:T(8,128)(2,1)}, bf16[512,2560]{1,0:T(8,128)(2,1)}) fusion(f32[512,5120]{1,0:T(8,128)} %fusion.2, bf16[1024,8640]{1,0:T(8,128)(2,1)S(1)} %bitcast.149, bf16[64,8,8,128]{3,2,1,0:T(8,128)(2,1)S(1)} %bitcast.116), kind=kOutput, calls=%fused_computation.9 | convolution fusion | flops 2705326080 | bytes 24641536 | tf_op jit(solution)/shard_map/dot_general | solution.py:49
  151.8 4.6 add_bitcast_fusion
  156.9 2.2 copy.88
  159.1 13.4 %multiply_reduce_fusion = (bf16[1024]{0:T(1024)(128)(2,1)S(1)}, f32[512]{0:T(512)S(1)}, f32[512,1024]{1,0:T(8,128)}) fusion(f32[512,1024]{1,0:T(8,128)} %copy-done.13, f32[512]{0:T(512)S(1)} %add_rsqrt_fusion.1, pred[1024]{0:T(1024)(128)(4,1)S(1)} %fusion.58, f32[1024]{0:T(1024)S(1)} %bitcast_convert_fusion.1, bf16[1024,8640]{1,0:T(8,128)(2,1)} %bitcast.145, ...), kind=kOutput, calls=%fused_computation.41 | convolution fusion | flops 5382863360 | bytes 19934208 | tf_op jit(solution)/shard_map/dot_general | solution.py:49
  172.5 2.1 multiply_add_fusion.1
  174.7 4.1 fusion.32.gradt_ref
  178.8 4.7 convolution_convert_fusion.1
  183.5 2.5 convolution_convert_fusion.3
  185.9 3.9 copy.90
  189.8 9.0 %convolution_convert_fusion = bf16[1024,5120]{1,0:T(8,128)(2,1)S(1)} fusion(bf16[512,2560]{1,0:T(8,128)(2,1)} %get-tuple-element.150, bf16[512,2560]{1,0:T(8,128)(2,1)} %get-tuple-element.149, f32[512,1024]{1,0:T(8,128)} %copy-done.13, f32[1024]{0:T(1024)S(1)} %bitcast_convert_fusion.1, f32[512]{0:T(512)S(1)} %add_rsqrt_fusion.1), kind=kOutput, calls=%fused_computation.1 | convolution fusion | flops 5386010624 | bytes 17831936 | tf_op jit(solution)/shard_map/dot_general | solution.py:49
  198.9 14.7 %pad_maximum_fusion = bf16[1024,8640]{1,0:T(8,128)(2,1)} fusion(bf16[1024,960]{1,0:T(8,128)(2,1)S(1)} %copy-done.2, bf16[1024,2560]{1,0:T(8,128)(2,1)} %convolution_convert_fusion.1, bf16[1024,5120]{1,0:T(8,128)(2,1)S(1)} %convolution_convert_fusion), kind=kLoop, calls=%fused_computation | loop fusion | flops 53084160 | bytes 35389440 | tf_op jit(solution)/shard_map/concatenate | solution.py:1335
  213.6 1.5 dynamic_update_slice.6.parts_ref
  215.0 163.5 %back.1 = (f32[960,512]{1,0:T(8,128)}, f32[5,512,128]{2,1,0:T(8,128)}, bf16[128,8640]{1,0:T(8,128)(2,1)}) custom-call(bf16[8,128,8640]{2,1,0:T(8,128)(2,1)} %dynamic_update_slice.6.parts_ref, bf16[5,5,512,128]{3,2,1,0:T(8,128)(2,1)} %get-tuple-element.37.win_ref, bf16[2560,128]{1,0:T(8,128)(2,1)} %maximum_maximum_fusion.feat_ref, ...), custom_call_target="tpu_custom_call" | custom-call | tf_op jit(solution)/shard_map/back/pallas_call | solution.py:1081
  378.5 1.9 subtract_convert_fusion.1
  380.5 1.0 pad_maximum_fusion.5
  381.5 1.1 slice.142
  382.6 1.6 subtract_convert_fusion
  384.2 1.3 copy.95
  385.5 2.5 pad_maximum_fusion.8
  388.0 2.0 copy.94
  390.0 4.9 %fusion.23 = (bf16[1024]{0:T(1024)(128)(2,1)S(1)}, f32[512]{0:T(512)S(1)}, f32[512,1024]{1,0:T(8,128)S(1)}) fusion(f32[512]{0:T(512)S(1)} %add_rsqrt_fusion, pred[1024]{0:T(1024)(128)(4,1)S(1)} %fusion.58, bf16[64,8,8,128]{3,2,1,0:T(8,128)(2,1)S(1)} %bitcast.109, f32[1024]{0:T(1024)S(1)} %bitcast_convert_fusion, bf16[1024,1600]{1,0:T(8,128)(2,1)} %bitcast.142, ...), kind=kOutput, calls=%fused_computation.40 | convolution fusion | flops 1686829568 | bytes 8072192 | tf_op jit(solution)/shard_map/dot_general | solution.py:49
  396.0 2.0 copy.96
  398.0 5.0 %convolution_convert_fusion.2 = bf16[1024,1600]{0,1:T(8,128)(2,1)} fusion(f32[1024]{0:T(1024)S(1)} %bitcast_convert_fusion, f32[512]{0:T(512)S(1)} %add_rsqrt_fusion, bf16[512,320]{0,1:T(8,128)(2,1)S(1)} %bitcast.130, bf16[512,320]{0,1:T(8,128)(2,1)} %bitcast.132, bf16[512,960]{0,1:T(8,128)(2,1)} %bitcast.128, bf16[64,8,8,128]{3,2,1,0:T(8,128)(2,1)S(1)} %bitcast.111), kind=kOutput, calls=%fused_computation.19 | convolution fusion | flops 1686372352 | bytes 5969920 | tf_op jit(solution)/shard_map/dot_general | solution.py:49
  403.0 4.3 copy.97
  407.6 1.7 copy-done.1
  409.3 38.1 %reduce.2 = bf16[128,1600]{1,0:T(8,128)(2,1)} custom-call(bf16[8,128,1600]{2,1,0:T(8,128)(2,1)} %copy-done.1), custom_call_target="tpu_custom_call" | custom-call | tf_op jit(solution)/shard_map/reduce/pallas_call | solution.py:1124
  447.5 1.1 convert_multiply_fusion.5
  448.6 3.4 convert_add_fusion.3
  453.3 1.4 copy-done
  455.1 1.0 copy.105
  456.1 1.0 copy.104
  458.1 2.0 slice_bitcast_fusion.1
  460.1 2.1 copy.102
  462.2 5.0 %convert_add_fusion.2 = (f32[2560,120]{0,1:T(8,128)}, f32[2560,120]{0,1:T(8,128)}, f32[2560,120]{0,1:T(8,128)}, f32[2560,120]{0,1:T(8,128)}) fusion(bf16[2560,120]{0,1:T(8,128)(2,1)S(1)} %copy-done.8, f32[2560,120]{0,1:T(8,128)} %param.41, f32[2560,120]{0,1:T(8,128)} %param.35, f32[128,8640]{1,0:T(8,128)} %copy-done), kind=kLoop, calls=%fused_computation.55 | loop fusion | flops 4915200 | bytes 9216000 | tf_op jit(solution)/shard_map/add | solution.py:1183
  467.2 1.2 copy-done.9
  468.4 4.6 convert_add_fusion
  (124 shorter events, 15.7 us)
Async XLA Ops:
  0.7 11.0 %copy-start.24 = (f32[960,120]{1,0:T(8,128)S(1)}, f32[960,120]{1,0:T(8,128)}, u32[]{:S(2)}) copy-start(f32[960,120]{1,0:T(8,128)} %param.38) | copy-start | bytes 1382404
  0.7 10.1 %copy-start.23 = (f32[960,120]{1,0:T(8,128)S(1)}, f32[960,120]{1,0:T(8,128)}, u32[]{:S(2)}) copy-start(f32[960,120]{1,0:T(8,128)} %param.32) | copy-start | bytes 1382404
  11.7 3.7 copy-start.20
  17.4 1.3 copy-start.21
  18.7 2.9 copy-start.4
  18.7 2.9 copy-start.25
  21.6 121.0 %copy-start.6 = (bf16[512,8,128]{2,1,0:T(8,128)(2,1)}, bf16[512,8,128]{2,1,0:T(8,128)(2,1)S(1)}, u32[]{:S(2)}) copy-start(bf16[512,8,128]{2,1,0:T(8,128)(2,1)S(1)} %pad.26) | copy-start | bytes 3145732
  126.0 16.6 %slice-start.2 = ((s8[17825792]{0:T(1024)(128)(4,1)}), s8[4194304]{0:T(1024)(128)(4,1)S(1)}, s32[]{:S(2)}) async-start(s8[17825792]{0:T(1024)(128)(4,1)} %bitcast.147), calls=%async_computation.2 | async-start | bytes 8388608
  126.0 16.6 %slice-start.3 = ((s8[17825792]{0:T(1024)(128)(4,1)}), s8[4194304]{0:T(1024)(128)(4,1)S(1)}, s32[]{:S(2)}) async-start(s8[17825792]{0:T(1024)(128)(4,1)} %bitcast.147), calls=%async_computation.3 | async-start | bytes 8388608
  129.5 22.3 %copy-start.13 = (f32[512,1024]{1,0:T(8,128)}, f32[512,1024]{1,0:T(8,128)S(1)}, u32[]{:S(2)}) copy-start(f32[512,1024]{1,0:T(8,128)S(1)} %get-tuple-element.161) | copy-start | bytes 6291460
  129.5 13.1 %slice-start.4 = ((s8[17825792]{0:T(1024)(128)(4,1)}), s8[4194304]{0:T(1024)(128)(4,1)S(1)}, s32[]{:S(2)}) async-start(s8[17825792]{0:T(1024)(128)(4,1)} %bitcast.147), calls=%async_computation.4 | async-start | bytes 8388608
  129.5 13.1 %slice-start.5 = ((s8[17825792]{0:T(1024)(128)(4,1)}), s8[4194304]{0:T(1024)(128)(4,1)S(1)}, s32[]{:S(2)}) async-start(s8[17825792]{0:T(1024)(128)(4,1)} %bitcast.147), calls=%async_computation.5 | async-start | bytes 8388608
  129.5 13.1 %slice-start.6 = ((s8[17825792]{0:T(1024)(128)(4,1)}), s8[1048576]{0:T(1024)(128)(4,1)S(1)}, s32[]{:S(2)}) async-start(s8[17825792]{0:T(1024)(128)(4,1)} %bitcast.147), calls=%async_computation.6 | async-start | bytes 2097152
  159.1 13.4 %copy-start.7 = (bf16[512,8,128]{2,1,0:T(8,128)(2,1)S(1)}, bf16[512,8,128]{2,1,0:T(8,128)(2,1)}, u32[]{:S(2)}) copy-start(bf16[512,8,128]{2,1,0:T(8,128)(2,1)} %copy-done.6) | copy-start | bytes 3145732
  159.1 13.4 %copy-start.14 = (f32[512,1024]{1,0:T(8,128)S(1)}, f32[512,1024]{1,0:T(8,128)}, u32[]{:S(2)}) copy-start(f32[512,1024]{1,0:T(8,128)} %copy-done.13) | copy-start | bytes 6291460
  174.7 4.1 copy-start.31
  178.8 4.7 %copy-start.22 = (bf16[960,512]{1,0:T(8,128)(2,1)S(1)}, bf16[960,512]{1,0:T(8,128)(2,1)}, u32[]{:S(2)}) copy-start(bf16[960,512]{1,0:T(8,128)(2,1)} %get-tuple-element.35.mixed_ref) | copy-start | bytes 2949124
  189.8 9.1 %copy-start.2 = (bf16[1024,960]{1,0:T(8,128)(2,1)S(1)}, bf16[1024,960]{1,0:T(8,128)(2,1)}, u32[]{:S(2)}) copy-start(bf16[1024,960]{1,0:T(8,128)(2,1)} %copy.90) | copy-start | bytes 5898244
  378.5 3.0 copy-start.3
  380.5 2.1 copy-start.18
  380.5 2.1 copy-start.19
  407.6 1.7 copy-start.1
  409.3 39.2 %copy-start.17 = (bf16[120,1600]{1,0:T(8,128)(2,1)S(1)}, bf16[120,1600]{1,0:T(8,128)(2,1)}, u32[]{:S(2)}) copy-start(bf16[120,1600]{1,0:T(8,128)(2,1)} %param.25) | copy-start | bytes 1152004
  448.6 3.4 copy-start.11
  451.9 0.7 copy-start.26
  452.0 0.7 copy-start.27
  452.0 0.7 copy-start.28
  452.0 0.7 copy-start.29
  452.0 0.7 copy-start.30
  452.0 2.7 copy-start.12
  452.0 2.7 copy-start.15
  452.0 2.7 copy-start.16
  452.7 2.1 copy-start
  456.1 6.0 %copy-start.8 = (bf16[2560,120]{0,1:T(8,128)(2,1)S(1)}, bf16[2560,120]{0,1:T(8,128)(2,1)}, u32[]{:S(2)}) copy-start(bf16[2560,120]{0,1:T(8,128)(2,1)} %param.29) | copy-start | bytes 1843204
  458.1 9.1 %copy-start.10 = (f32[120,5120]{1,0:T(8,128)S(1)}, f32[120,5120]{1,0:T(8,128)}, u32[]{:S(2)}) copy-start(f32[120,5120]{1,0:T(8,128)} %param.34) | copy-start | bytes 7372804
  460.1 7.1 %slice-start = ((s8[4456448]{0:T(1024)(128)(4,1)}), s8[262144]{0:T(1024)(128)(4,1)S(1)}, s32[]{:S(2)}) async-start(s8[4456448]{0:T(1024)(128)(4,1)} %bitcast.104), calls=%async_computation | async-start | bytes 524288
  462.2 5.1 %slice-start.1 = ((s8[4456448]{0:T(1024)(128)(4,1)}), s8[4194304]{0:T(1024)(128)(4,1)S(1)}, s32[]{:S(2)}) async-start(s8[4456448]{0:T(1024)(128)(4,1)} %bitcast.104), calls=%async_computation.1 | async-start | bytes 8388608
  462.2 5.1 %copy-start.5 = (bf16[120,5120]{1,0:T(8,128)(2,1)S(1)}, bf16[120,5120]{1,0:T(8,128)(2,1)}, u32[]{:S(2)}) copy-start(bf16[120,5120]{1,0:T(8,128)(2,1)} %param.28) | copy-start | bytes 3686404
  462.2 6.2 %copy-start.9 = (f32[120,5120]{1,0:T(8,128)S(1)}, f32[120,5120]{1,0:T(8,128)}, u32[]{:S(2)}) copy-start(f32[120,5120]{1,0:T(8,128)} %param.40) | copy-start | bytes 7372804

commit v3 on v2

--- a/solution.py
+++ b/solution.py
@@ -630,160 +630,186 @@
 
 
 class Reduce:
-    COUNT = 35
-
-    def __init__(self, at, parts, out, own, r0, r1a, r1b, r2a, r2b, r3, local_sem, send, recv):
-        self.at, self.parts, self.out, self.own = at, parts, out, own
+    COUNT = 14
+
+    def __init__(self, at, chunks, out, own, give, r0, r1a, r1b, r2a, r2b, r3, send, recv, free):
+        self.at, self.chunks, self.out, self.own, self.give = at, chunks, out, own, give
         self.r0, self.r1a, self.r1b, self.r2a, self.r2b, self.r3 = r0, r1a, r1b, r2a, r2b, r3
-        self.local_sem, self.send, self.recv = local_sem, send, recv
+        self.send, self.recv, self.free = send, recv, free
         self.rows = out.shape[0]
         self.quarter, self.half = self.rows // 4, self.rows // 8
+        self.slots = give.shape[0]
 
     @staticmethod
-    def scratch(rows, columns):
+    def scratch(rows, chunks, slots):
         half = rows // 8
+        columns = sum(width for _, width in chunks)
+        widest = max(width for _, width in chunks)
         return [
             VMEM((4, rows, columns), BF),
-            VMEM((4, rows, columns), BF),
-            VMEM((4, 2, half, columns), BF),
-            VMEM((4, 2, half, columns), BF),
+            VMEM((slots, 4, rows, widest), BF),
+            VMEM((slots, 4, rows, widest), BF),
+            VMEM((2, 4, half, columns), BF),
+            VMEM((2, 4, half, columns), BF),
             VMEM((4, half, columns), BF),
             VMEM((4, half, columns), BF),
             VMEM((3, 2 * half, columns), BF),
-            DMA((4,)),
-            DMA((Reduce.COUNT,)),
-            DMA((Reduce.COUNT,)),
+            DMA((len(chunks), Reduce.COUNT)),
+            DMA((len(chunks), Reduce.COUNT)),
+            pltpu.SemaphoreType.REGULAR,
         ]
 
-    def copy(self, index, src, dst, device):
-        return remote(src, dst, self.send.at[index], self.recv.at[index], device)
-
-    def arrive(self, index, ref):
-        self.copy(index, ref, ref, self.at.core_side).wait_recv()
+    def columns(self, n):
+        return pl.ds(*self.chunks[n])
+
+    def copy(self, n, index, src, dst, device):
+        return remote(src, dst, self.send.at[n, index], self.recv.at[n, index], device)
+
+    def arrive(self, n, index, ref):
+        self.copy(n, index, ref, ref, self.at.core_side).wait_recv()
 
     def spot(self, owner, part):
         start = owner * self.quarter + part * self.half
         return pl.ds(pl.multiple_of(start, self.half), self.half)
 
-    def piece(self, owner):
+    def piece(self, n, owner):
         start = pl.multiple_of(owner * self.quarter, self.quarter)
-        return self.out.at[pl.ds(start, self.quarter), :]
-
-    def add_into(self, k, where, ref):
-        old = self.own[k, where, :].astype(F32)
-        self.own[k, where, :] = (old + ref[...].astype(F32)).astype(BF)
-
-    def local_copy(self, k):
-        z = self.at.z_to(k + 1 if k < 3 else 0)
-        return pltpu.make_async_copy(
-            self.parts.at[z * 2 + self.at.c], self.own.at[k], self.local_sem.at[k]
+        return self.out.at[pl.ds(start, self.quarter), self.columns(n)]
+
+    def core_copy(self, n):
+        slot, width = n % self.slots, self.chunks[n][1]
+        return self.copy(
+            n,
+            0,
+            self.give.at[slot, :, :, pl.ds(0, width)],
+            self.r0.at[slot, :, :, pl.ds(0, width)],
+            self.at.core_side,
         )
 
-    def core_copy(self, k):
-        z = self.at.z_to(k + 1 if k < 3 else 0)
-        return self.copy(k, self.parts.at[z * 2 + 1 - self.at.c], self.r0.at[k], self.at.core_side)
-
-    def one_copies(self, k):
-        at, copies = self.at, []
+    def one_copies(self, n):
+        at, copies, cols = self.at, [], self.columns(n)
         for i in range(2):
-            a = self.own.at[k, self.spot(i * 2 + 1 - at.x, 0), :]
-            b = self.own.at[k, self.spot((1 - at.y) * 2 + i, 1), :]
-            copies.append(self.copy(4 + 4 * k + i, a, self.r1a.at[k, i], at.x_side))
-            copies.append(self.copy(6 + 4 * k + i, b, self.r1b.at[k, i], at.y_side))
+            a = self.own.at[:, self.spot(i * 2 + 1 - at.x, 0), cols]
+            b = self.own.at[:, self.spot((1 - at.y) * 2 + i, 1), cols]
+            copies.append(self.copy(n, 1 + i, a, self.r1a.at[i, :, :, cols], at.x_side))
+            copies.append(self.copy(n, 3 + i, b, self.r1b.at[i, :, :, cols], at.y_side))
         return copies
 
-    def two_copies(self, k):
-        at = self.at
-        a, b = self.own.at[k, self.spot(at.ry, 0), :], self.own.at[k, self.spot(at.rx, 1), :]
+    def two_copies(self, n):
+        at, cols = self.at, self.columns(n)
+        a = self.own.at[:, self.spot(at.ry, 0), cols]
+        b = self.own.at[:, self.spot(at.rx, 1), cols]
         return [
-            self.copy(20 + 2 * k, a, self.r2a.at[k], at.y_side),
-            self.copy(21 + 2 * k, b, self.r2b.at[k], at.x_side),
+            self.copy(n, 5, a, self.r2a.at[:, :, cols], at.y_side),
+            self.copy(n, 6, b, self.r2b.at[:, :, cols], at.x_side),
         ]
 
-    def z_copy(self, k):
-        at = self.at
+    def z_copy(self, n, k):
+        at, cols = self.at, self.columns(n)
         mine = pl.ds(pl.multiple_of(at.r * self.quarter, self.quarter), self.quarter)
-        return self.copy(28 + k, self.own.at[k, mine, :], self.r3.at[k], at.z_side(k + 1))
-
-    def back_copies(self):
-        at, piece = self.at, self.piece
-        a, b = self.out.at[self.spot(at.rx, 0), :], self.out.at[self.spot(at.ry, 1), :]
-        return [
-            self.copy(31, piece(at.r), piece(at.r), at.x_side),
-            self.copy(32, piece(at.r), piece(at.r), at.y_side),
-            self.copy(33, a, a, at.y_side),
-            self.copy(34, b, b, at.x_side),
-        ]
-
-    def start(self, k):
-        self.local_copy(k).start()
-        self.core_copy(k).start()
-
-    def zero(self, k):
-        self.local_copy(k).wait()
-        self.arrive(k, self.r0.at[k])
+        src = self.own.at[at.z_to(k), mine, cols]
+        return self.copy(n, 6 + k, src, self.r3.at[k - 1, :, cols], at.z_side(k))
+
+    def back_copy(self, n, i):
+        at, cols = self.at, self.columns(n)
+        if i < 2:
+            ref = self.piece(n, at.r)
+            return self.copy(n, 10 + i, ref, ref, at.x_side if i == 0 else at.y_side)
+        owner, device = (at.rx, at.y_side) if i == 2 else (at.ry, at.x_side)
+        ref = self.out.at[self.spot(owner, i - 2), cols]
+        return self.copy(n, 10 + i, ref, ref, device)
+
+    def claim(self, n):
+        if n >= self.slots:
+            self.core_copy(n - self.slots).wait_send()
+
+    def start(self, n):
+        if n >= self.slots:
+            pl.semaphore_wait(self.free, 1)
+        self.core_copy(n).start()
+
+    def zero(self, n):
+        slot, (first, width) = n % self.slots, self.chunks[n]
+        self.arrive(n, 0, self.r0.at[slot, :, :, pl.ds(0, width)])
+        per_plane = self.rows // (2 * self.half)
 
         def add_rows(i, _):
-            where = pl.ds(pl.multiple_of(i * self.half, self.half), self.half)
-            self.add_into(k, where, self.r0.at[k, where, :])
+            z, where = i // per_plane, pl.ds(
+                pl.multiple_of(lax.rem(i, per_plane) * 2 * self.half, 2 * self.half), 2 * self.half
+            )
+            old = self.own[z, where, first : first + width].astype(F32)
+            new = self.r0[slot, z, where, :width].astype(F32)
+            self.own[z, where, first : first + width] = (old + new).astype(BF)
             return 0
 
-        lax.fori_loop(0, self.rows // self.half, add_rows, 0)
-        for copy in self.one_copies(k):
+        lax.fori_loop(0, 4 * per_plane, add_rows, 0)
+        if n + self.slots < len(self.chunks):
+            pl.semaphore_signal(
+                self.free, inc=1, device_id=self.at.core_side, device_id_type=MESH
+            )
+
+    def push(self, n):
+        for copy in self.one_copies(n):
             copy.start()
 
-    def one(self, k):
-        at = self.at
+    def add(self, n, where, ref):
+        cols = self.columns(n)
+        for z in range(4):
+            old = self.own[z, where, cols].astype(F32)
+            self.own[z, where, cols] = (old + ref[z, :, cols].astype(F32)).astype(BF)
+
+    def one(self, n):
+        at, cols = self.at, self.columns(n)
         for i in range(2):
-            self.arrive(4 + 4 * k + i, self.r1a.at[k, i])
-            self.arrive(6 + 4 * k + i, self.r1b.at[k, i])
-            self.add_into(k, self.spot(i * 2 + at.x, 0), self.r1a.at[k, i])
-            self.add_into(k, self.spot(at.y * 2 + i, 1), self.r1b.at[k, i])
-        for copy in self.two_copies(k):
+            self.arrive(n, 1 + i, self.r1a.at[i, :, :, cols])
+            self.arrive(n, 3 + i, self.r1b.at[i, :, :, cols])
+            self.add(n, self.spot(i * 2 + at.x, 0), self.r1a.at[i])
+            self.add(n, self.spot(at.y * 2 + i, 1), self.r1b.at[i])
+        for copy in self.two_copies(n):
             copy.start()
 
-    def two(self, k):
-        at = self.at
-        self.arrive(20 + 2 * k, self.r2a.at[k])
-        self.arrive(21 + 2 * k, self.r2b.at[k])
-        self.add_into(k, self.spot(at.r, 0), self.r2a.at[k])
-        self.add_into(k, self.spot(at.r, 1), self.r2b.at[k])
-        if k < 3:
-            self.z_copy(k).start()
-
-    def three(self):
-        at = self.at
-        for k in range(3):
-            self.arrive(28 + k, self.r3.at[k])
+    def two(self, n):
+        at, cols = self.at, self.columns(n)
+        self.arrive(n, 5, self.r2a.at[:, :, cols])
+        self.arrive(n, 6, self.r2b.at[:, :, cols])
+        self.add(n, self.spot(at.r, 0), self.r2a)
+        self.add(n, self.spot(at.r, 1), self.r2b)
+        for k in (1, 2, 3):
+            self.z_copy(n, k).start()
+
+    def three(self, n):
+        at, cols = self.at, self.columns(n)
+        for k in (1, 2, 3):
+            self.arrive(n, 6 + k, self.r3.at[k - 1, :, cols])
         for i in range(2):
             where = pl.ds(i * self.half, self.half)
-            total = self.own[3, self.spot(at.r, i), :].astype(F32)
+            total = self.own[at.z, self.spot(at.r, i), cols].astype(F32)
             for k in range(3):
-                total += self.r3[k, where, :].astype(F32)
-            self.out[self.spot(at.r, i), :] = total.astype(BF)
-        copies = self.back_copies()
-        copies[0].start()
-        copies[1].start()
-
-    def four(self):
+                total += self.r3[k, where, cols].astype(F32)
+            self.out[self.spot(at.r, i), cols] = total.astype(BF)
+        self.back_copy(n, 0).start()
+        self.back_copy(n, 1).start()
+
+    def four(self, n):
         at = self.at
-        copies = self.back_copies()
-        self.arrive(31, self.piece(at.rx))
-        copies[2].start()
-        self.arrive(32, self.piece(at.ry))
-        copies[3].start()
-
-    def five(self):
-        at = self.at
-        self.arrive(33, self.out.at[self.spot(at.rd, 0), :])
-        self.arrive(34, self.out.at[self.spot(at.rd, 1), :])
-        for k in range(4):
-            for copy in [self.core_copy(k)] + self.one_copies(k) + self.two_copies(k):
+        self.arrive(n, 10, self.piece(n, at.rx))
+        self.back_copy(n, 2).start()
+        self.arrive(n, 11, self.piece(n, at.ry))
+        self.back_copy(n, 3).start()
+
+    def five(self, n):
+        at, cols = self.at, self.columns(n)
+        self.arrive(n, 12, self.out.at[self.spot(at.rd, 0), cols])
+        self.arrive(n, 13, self.out.at[self.spot(at.rd, 1), cols])
+
+    def sent(self):
+        for n in range(len(self.chunks)):
+            if n + self.slots >= len(self.chunks):
+                self.core_copy(n).wait_send()
+            copies = self.one_copies(n) + self.two_copies(n)
+            copies += [self.z_copy(n, k) for k in (1, 2, 3)]
+            for copy in copies + [self.back_copy(n, i) for i in range(4)]:
                 copy.wait_send()
-        for k in range(3):
-            self.z_copy(k).wait_send()
-        for copy in self.back_copies():
-            copy.wait_send()
 
 
 def at_steps(i, events):
@@ -976,162 +1002,643 @@
     )(x, cosine, sine, feat, qfeat, attend_own, rest_own)
 
 
-def back_kernel(
-    parts_ref,
-    win_ref,
-    feat_ref,
-    qt_ref,
+def pad_features(src, dst, own_rows, rows):
+    for s in range(D // own_rows):
+        dst[:, s * rows : s * rows + own_rows] = src[:, s * own_rows : (s + 1) * own_rows].astype(
+            dst.dtype
+        )
+        dst[:, s * rows + own_rows : (s + 1) * rows] = jnp.zeros(
+            (dst.shape[0], rows - own_rows), dst.dtype
+        )
+
+
+def flip_blocks(value, dst):
+    blocks, rows, _ = dst.shape
+    for s in range(blocks):
+        dst[s] = value[:, s * rows : (s + 1) * rows].T
+
+
+def split_cores(at, flipped, own, give):
+    for z in range(own.shape[0]):
+        own[z] = flipped[2 * z + at.c]
+        give[z] = flipped[2 * z + 1 - at.c]
+
+
+PART = 128
+SUB = 256
+CHUNK = 2 * SUB
+
+
+def rear_chunks():
+    chunks = [(3 * CHUNK * n, 3 * CHUNK) for n in range(FF // CHUNK)]
+    return chunks + [(3 * FF, -(-QW // 128) * 128)]
+
+
+def feed_forward(
+    at,
+    total,
+    x_ref,
+    cot_ref,
+    mixed_ref,
+    rest_ref,
+    out_ref,
+    middle_grad_ref,
+    gradt_ref,
+    events,
+    cot,
+    hidden,
+    middle,
+    acc_out,
+    acc_grad,
+    flipped,
+    hidden_own,
+    hidden_give,
+    cot_own,
+    cot_give,
+    out_weight,
+    gain_rows,
+    gain_term,
+    weights,
+    sems,
+):
+    shard_count, rows, _ = rest_ref.shape
+    width = shard_count * rows
+    tokens = x_ref.shape[0]
+    own_rows = D // shard_count
+    planes = shard_count // 2
+    block = own_rows // 16 * 16
+
+    def weight_copies(n, slot):
+        return [
+            pltpu.make_async_copy(
+                rest_ref.at[:, :, pl.ds(pl.multiple_of(i * FF + n * SUB, 128), SUB)],
+                weights.at[slot, i],
+                sems.at[slot, i],
+            )
+            for i in range(3)
+        ]
+
+    out_copy = pltpu.make_async_copy(
+        rest_ref.at[:, :, pl.ds(3 * FF, QW)], out_weight, sems.at[2, 0]
+    )
+    gain_copy = pltpu.make_async_copy(
+        rest_ref.at[:, pl.ds(block, rows - block), pl.ds(0, 128)], gain_rows, sems.at[2, 1]
+    )
+    out_copy.start()
+    gain_copy.start()
+    for copy in weight_copies(0, 0):
+        copy.start()
+    pad_features(x_ref, middle, own_rows, rows)
+    pad_features(cot_ref, cot, own_rows, rows)
+    flip_blocks(cot, flipped)
+    split_cores(at, flipped, cot_own, cot_give)
+
+    gain_copy.wait()
+    gain = jnp.concatenate(
+        [
+            gain_rows[s, own_rows - block : own_rows - block + 1, :rows].astype(F32)
+            for s in range(shard_count)
+        ],
+        axis=1,
+    )
+    lane = lax.broadcasted_iota(jnp.int32, (1, width), 1)
+    real = lax.rem(lane, rows) < own_rows
+    gain = jnp.where(real, gain, 0.0)
+    out_copy.wait()
+    out_full = out_weight.reshape(width, QW)
+
+    def scale_of(value):
+        return lax.rsqrt(jnp.sum(value * value, axis=-1, keepdims=True) * (1.0 / D) + eps_norm)
+
+    for low in range(0, tokens, PART):
+        where = slice(low, low + PART)
+        value = middle[where, :] + dot(mixed_ref[:, where].T, out_full[...], 1, 1)
+        middle[where, :] = value
+        hidden[where, :] = (value * scale_of(value) * gain).astype(BF)
+    flip_blocks(hidden, flipped)
+    split_cores(at, flipped, hidden_own, hidden_give)
+    acc_out[...] = jnp.zeros_like(acc_out)
+    acc_grad[...] = jnp.zeros_like(acc_grad)
+
+    def put(ref, column, value):
+        where = pl.ds(pl.multiple_of(column, 128), value.shape[1])
+        ref[:, :, where] = value.reshape(planes, rows, value.shape[1]).astype(BF)
+
+    def step(n, _):
+        slot = lax.rem(n, 2)
+        for copy in weight_copies(n, slot):
+            copy.wait()
+
+        @pl.when(n + 1 < FF // SUB)
+        def _():
+            for copy in weight_copies(n + 1, 1 - slot):
+                copy.start()
+
+        gate_weight = weights[slot, 0].reshape(width, SUB)
+        upper_weight = weights[slot, 1].reshape(width, SUB)
+        shrink_weight = weights[slot, 2].reshape(width, SUB)
+        gate = dot(hidden[...], gate_weight)
+        upper = dot(hidden[...], upper_weight)
+        inner_grad = dot(cot[...], shrink_weight)
+        sigmoid = jax.nn.sigmoid(gate)
+        active = gate * sigmoid
+        inner = (active * upper).astype(BF)
+        gate_grad = (inner_grad * upper * sigmoid * (1.0 + gate * (1.0 - sigmoid))).astype(BF)
+        upper_grad = (inner_grad * active).astype(BF)
+        for low in range(0, width, width // 2):
+            cols = slice(low, low + width // 2)
+            acc_out[:, cols] += dot(inner, shrink_weight[cols], 1, 1)
+            acc_grad[:, cols] += dot(gate_grad, gate_weight[cols], 1, 1) + dot(
+                upper_grad, upper_weight[cols], 1, 1
+            )
+        chunk, part = n // 2, lax.rem(n, 2) * SUB
+        first = chunk * 3 * CHUNK + part
+        put(total.own, first, dot(hidden_own[...].reshape(width // 2, tokens), gate_grad))
+        put(total.own, first + CHUNK, dot(hidden_own[...].reshape(width // 2, tokens), upper_grad))
+        put(total.own, first + 2 * CHUNK, dot(cot_own[...].reshape(width // 2, tokens), inner))
+        for n_start in range(2 * total.slots, FF // SUB, 2):
+            pl.when(n == n_start)(lambda: total.claim(n_start // 2))
+        give = total.give.at[lax.rem(chunk, total.slots)]
+        put(give, part, dot(hidden_give[...].reshape(width // 2, tokens), gate_grad))
+        put(give, part + CHUNK, dot(hidden_give[...].reshape(width // 2, tokens), upper_grad))
+        put(give, part + 2 * CHUNK, dot(cot_give[...].reshape(width // 2, tokens), inner))
+        for n_end in range(1, FF // SUB, 2):
+            pl.when(n == n_end)(lambda: total.start(n_end // 2))
+        at_steps(n, events)
+        return 0
+
+    lax.fori_loop(0, FF // SUB, step, 0)
+
+    term = jnp.zeros((1, width), F32)
+    for low in range(0, tokens, PART):
+        where = slice(low, low + PART)
+        value = middle[where, :]
+        result = value + acc_out[where, :]
+        for s in range(shard_count):
+            out_ref[where, s * own_rows : (s + 1) * own_rows] = result[
+                :, s * rows : s * rows + own_rows
+            ]
+        scale = scale_of(value)
+        normed = value * scale
+        hidden_grad = jnp.where(real, acc_grad[where, :], 0.0)
+        term = term + jnp.sum(hidden_grad * normed, axis=0, keepdims=True)
+        upstream = hidden_grad * gain
+        mean = jnp.sum(upstream * normed, axis=-1, keepdims=True) * (1.0 / D)
+        value = cot[where, :].astype(F32) + scale * (upstream - normed * mean)
+        middle_grad_ref[where, :] = value
+        branch = value.astype(BF)
+        hidden[where, :] = branch
+        gradt_ref[:, where] = dot(branch, out_full[...]).T.astype(BF)
+    for s in range(shard_count):
+        gain_term[s] = jnp.broadcast_to(term[:, s * rows : (s + 1) * rows], (8, rows))
+    flip_blocks(hidden, flipped)
+    split_cores(at, flipped, hidden_own, hidden_give)
+    place = lax.broadcasted_iota(jnp.int32, (rows, rows), 0)
+    last = len(total.chunks) - 1
+    total.claim(last)
+    for lhs, core, ref, column in (
+        (hidden_own, at.c, total.own, total.chunks[last][0]),
+        (hidden_give, 1 - at.c, total.give.at[last % total.slots], 0),
+    ):
+        for z in range(planes):
+            product = dot(lhs[z], mixed_ref[...], 1, 1)
+            row = gain_term[2 * z + core][:1]
+            ref[z, :, column : column + rows] = jnp.where(
+                place == own_rows, row, product[:, :rows]
+            ).astype(BF)
+            ref[z, :, column + rows : column + QW] = product[:, rows:].astype(BF)
+            end = column + total.chunks[last][1]
+            ref[z, :, column + QW : end] = jnp.zeros((rows, end - column - QW), BF)
+    total.start(last)
+
+
+def rear_kernel(
+    x_ref,
+    cot_ref,
+    mixed_ref,
+    rest_ref,
+    win_hbm,
+    feat_hbm,
+    qt_hbm,
     qfeat_ref,
-    gradt_ref,
-    mixed_ref,
     lse_ref,
+    out_ref,
+    middle_grad_ref,
     dq_ref,
     pairs_ref,
     sum_ref,
-    kvf,
-    kt,
-    qa,
-    da,
-    acc,
-    rhs,
-    grads,
+    gradt_ref,
     ra,
     rb,
     r2,
     r1,
-    t2,
-    t1,
     collect_send,
     collect_recv,
     *reduce_scratch,
 ):
     at = Place()
-    kv_heads = win_ref.shape[1]
+    tokens = x_ref.shape[0]
+    shard_count, rows, _ = rest_ref.shape
+    width = shard_count * rows
+    kv_heads, _, lanes = pairs_ref.shape
+    keys = feat_hbm.shape[0]
     greet(at, True)
-    total = Reduce(at, parts_ref, sum_ref, *reduce_scratch)
-    collect = Collect(
-        at, grads, pairs_ref, ra, rb, r2, r1, t2, t1, collect_send, collect_recv
+    total = Reduce(at, rear_chunks(), sum_ref, *reduce_scratch)
+
+    def run(*names):
+        def event():
+            for name, n in names:
+                getattr(total, name)(n)
+
+        return event
+
+    forward_events = [
+        (2, run(("zero", 0), ("push", 0))),
+        (4, run(("zero", 1))),
+        (5, run(("one", 0), ("push", 1))),
+        (6, run(("zero", 2), ("two", 0))),
+        (8, run(("zero", 3))),
+        (9, run(("one", 1), ("push", 2), ("three", 0))),
+    ]
+    backward_events = [
+        (0, run(("zero", 4), ("two", 1), ("four", 0))),
+        (2, run(("one", 2), ("push", 3), ("five", 0))),
+        (3, run(("zero", 5), ("two", 2), ("three", 1))),
+        (4, run(("four", 1))),
+        (5, run(("three", 2))),
+        (6, run(("one", 3), ("push", 4), ("five", 1), ("four", 2))),
+        (7, run(("two", 3))),
+        (9, run(("three", 3), ("five", 2))),
+        (10, run(("one", 4), ("push", 5), ("four", 3))),
+        (11, run(("two", 4))),
+        (12, run(("one", 5), ("three", 4), ("five", 3))),
+        (13, run(("two", 5), ("four", 4))),
+        (14, run(("three", 5), ("five", 4))),
+    ]
+
+    pl.run_scoped(
+        functools.partial(
+            feed_forward,
+            at,
+            total,
+            x_ref,
+            cot_ref,
+            mixed_ref,
+            rest_ref,
+            out_ref,
+            middle_grad_ref,
+            gradt_ref,
+            forward_events,
+        ),
+        VMEM((tokens, width), BF),
+        VMEM((tokens, width), BF),
+        VMEM((tokens, width), F32),
+        VMEM((tokens, width), F32),
+        VMEM((tokens, width), F32),
+        VMEM((shard_count, rows, tokens), BF),
+        VMEM((shard_count // 2, rows, tokens), BF),
+        VMEM((shard_count // 2, rows, tokens), BF),
+        VMEM((shard_count // 2, rows, tokens), BF),
+        VMEM((shard_count // 2, rows, tokens), BF),
+        VMEM((shard_count, rows, QW), BF),
+        VMEM((shard_count, rows - D // shard_count // 16 * 16, 128), BF),
+        VMEM((shard_count, 8, rows), F32),
+        VMEM((2, 3, shard_count, rows, SUB), BF),
+        DMA((3, 3)),
     )
-    for k in range(4):
-        total.start(k)
-    attend_backward_setup(feat_ref, kvf, qa, da, rhs)
-    total.zero(0)
-    events = [
-        (0, lambda: total.zero(1)),
-        (1, lambda: total.zero(2)),
-        (2, lambda: total.zero(3)),
-        (4, lambda: total.one(0)),
-        (6, lambda: total.one(1)),
-        (7, lambda: total.two(0)),
-        (8, lambda: total.one(2)),
-        (9, lambda: total.two(1)),
-        (11, lambda: total.one(3)),
-        (12, lambda: total.two(2)),
-        (14, lambda: total.two(3)),
-    ]
-
-    def key_head(j, _):
-        attend_backward_keys(j, win_ref, kvf, kt, acc)
-
-        def head(g, _):
-            h = j * GROUP + g
-            attend_backward_head(
-                h,
-                qt_ref,
-                qfeat_ref,
-                gradt_ref,
-                mixed_ref,
-                lse_ref,
-                dq_ref,
-                kvf,
-                kt,
-                qa,
-                da,
-                acc,
-                rhs,
+
+    def attention(kvf, kt, qa, da, acc, rhs, grads, t2, t1, win_ref, feat_ref, qt_ref, sems):
+        loads = [
+            pltpu.make_async_copy(src, dst, sems.at[i])
+            for i, (src, dst) in enumerate(
+                ((feat_hbm, feat_ref), (win_hbm, win_ref), (qt_hbm, qt_ref))
             )
-            at_steps(h, events)
+        ]
+        for load in loads:
+            load.start()
+        for load in loads:
+            load.wait()
+        collect = Collect(
+            at, grads, pairs_ref, ra, rb, r2, r1, t2, t1, collect_send, collect_recv
+        )
+        attend_backward_setup(feat_ref, kvf, qa, da, rhs)
+
+        def key_head(j, _):
+            attend_backward_keys(j, win_ref, kvf, kt, acc)
+
+            def head(g, _):
+                h = j * GROUP + g
+                attend_backward_head(
+                    h,
+                    qt_ref,
+                    qfeat_ref,
+                    gradt_ref,
+                    mixed_ref,
+                    lse_ref,
+                    dq_ref,
+                    kvf,
+                    kt,
+                    qa,
+                    da,
+                    acc,
+                    rhs,
+                )
+                at_steps(h, backward_events)
+                return 0
+
+            lax.fori_loop(0, GROUP, head, 0)
+            attend_backward_done(j, acc, grads)
+            collect.start(j)
+            pl.when(j > 0)(lambda: collect.one(j - 1))
+            pl.when(j > 1)(lambda: collect.two(j - 2))
+            pl.when(j > 2)(lambda: collect.three(j - 3))
             return 0
 
-        lax.fori_loop(0, GROUP, head, 0)
-        attend_backward_done(j, acc, grads)
-        collect.start(j)
-        pl.when(j > 0)(lambda: collect.one(j - 1))
-        pl.when(j > 1)(lambda: collect.two(j - 2))
-        pl.when(j > 2)(lambda: collect.three(j - 3))
-        return 0
-
-    lax.fori_loop(0, kv_heads, key_head, 0)
-    collect.one(kv_heads - 1)
-    collect.two(kv_heads - 2)
-    total.three()
-    collect.two(kv_heads - 1)
-    for j in range(kv_heads - 3, kv_heads):
-        collect.three(j)
-    total.four()
-    for j in range(kv_heads):
-        collect.sent(j)
-    total.five()
-
-
-def back(parts, window, feat, qt, qfeat, gradt, mixed, lse, number):
+        lax.fori_loop(0, kv_heads, key_head, 0)
+        collect.one(kv_heads - 1)
+        collect.two(kv_heads - 2)
+        total.four(5)
+        collect.two(kv_heads - 1)
+        for j in range(kv_heads - 3, kv_heads):
+            collect.three(j)
+        total.five(5)
+        for j in range(kv_heads):
+            collect.sent(j)
+        total.sent()
+
+    pl.run_scoped(
+        attention,
+        *attend_backward_scratch(keys, lanes, tokens),
+        VMEM(win_hbm.shape, BF),
+        VMEM(pairs_ref.shape, BF),
+        VMEM(pairs_ref.shape, BF),
+        VMEM(win_hbm.shape, BF),
+        VMEM(feat_hbm.shape, BF),
+        VMEM(qt_hbm.shape, BF),
+        DMA((3,)),
+    )
+
+
+def rear(x, cotangent, mixed, rest, window, feat, qt, qfeat, lse, number):
     blocks, kv_heads, tokens, lanes = window.shape
-    _, rows, columns = parts.shape
+    shard_count, rows, _ = rest.shape
+    columns = sum(width for _, width in rear_chunks())
     pairs = (kv_heads, tokens, lanes)
     return pl.pallas_call(
-        back_kernel,
+        rear_kernel,
         out_shape=(
+            jax.ShapeDtypeStruct(x.shape, F32),
+            jax.ShapeDtypeStruct((tokens, shard_count * rows), F32),
             jax.ShapeDtypeStruct(qt.shape, F32),
             jax.ShapeDtypeStruct(pairs, F32),
             jax.ShapeDtypeStruct((rows, columns), BF),
         ),
-        in_specs=[pl.BlockSpec(memory_space=ANY)] + [pl.BlockSpec(memory_space=VMEM)] * 7,
-        out_specs=(pl.BlockSpec(memory_space=VMEM),) * 3,
-        scratch_shapes=attend_backward_scratch(blocks * tokens, lanes, tokens)
-        + [VMEM(window.shape, BF)]
-        + [VMEM(pairs, BF)] * 6
+        in_specs=[pl.BlockSpec(memory_space=VMEM)] * 3
+        + [pl.BlockSpec(memory_space=ANY)] * 4
+        + [pl.BlockSpec(memory_space=VMEM)] * 2,
+        out_specs=(pl.BlockSpec(memory_space=VMEM),) * 5,
+        scratch_shapes=[VMEM(qt.shape, BF)]
+        + [VMEM(pairs, BF)] * 4
         + [DMA((4, kv_heads)), DMA((4, kv_heads))]
-        + Reduce.scratch(rows, columns),
+        + Reduce.scratch(rows, rear_chunks(), 2),
         compiler_params=pltpu.CompilerParams(
             collective_id=number, has_side_effects=True, vmem_limit_bytes=BIG_VMEM
         ),
-        name="back",
-    )(parts, window, feat, qt, qfeat, gradt, mixed, lse)
-
-
-def reduce_kernel(parts_ref, out_ref, *scratch):
+        name="rear",
+    )(x, cotangent, mixed, rest, window, feat, qt, qfeat, lse)
+
+
+def tail_kernel(
+    x_ref,
+    middle_grad_ref,
+    dq_ref,
+    pairs_ref,
+    cos_ref,
+    sin_ref,
+    attend_ref,
+    grad_ref,
+    sum_ref,
+    inputs,
+    hidden,
+    jointt,
+    flipped,
+    hidden_own,
+    hidden_give,
+    gain_term,
+    *reduce_scratch,
+):
     at = Place()
+    shard_count, rows, columns = attend_ref.shape
+    width = shard_count * rows
+    tokens = x_ref.shape[0]
+    own_rows = D // shard_count
     greet(at, True)
-    total = Reduce(at, parts_ref, out_ref, *scratch)
-    for k in range(4):
-        total.start(k)
-    for k in range(4):
-        total.zero(k)
-    for k in range(4):
-        total.one(k)
-    for k in range(4):
-        total.two(k)
-    total.three()
-    total.four()
-    total.five()
-
-
-def reduce_rows(parts, direct, number):
-    _, rows, columns = parts.shape
-    if not direct:
-        own = lax.psum_scatter(parts, "shard", scatter_dimension=0)
-        return lax.psum(own, "rep")
+    total = Reduce(at, [(0, columns)], sum_ref, *reduce_scratch)
+    pad_features(x_ref, inputs, own_rows, rows)
+    lane = lax.broadcasted_iota(jnp.int32, (1, width), 1)
+    real = lax.rem(lane, rows) < own_rows
+    gain = jnp.concatenate(
+        [
+            attend_ref[s, own_rows : own_rows + 1, :rows].astype(F32)
+            for s in range(shard_count)
+        ],
+        axis=1,
+    )
+    gain = jnp.where(real, gain, 0.0)
+
+    def unrotate(head):
+        half = HEAD_DIM // 2
+        front, back = head[:half], head[half:]
+        cosine, sine = cos_ref[...], sin_ref[...]
+        return jnp.concatenate(
+            [front * cosine + back * sine, back * cosine - front * sine], axis=0
+        ).astype(BF)
+
+    for h in range(HEADS):
+        where = slice(h * HEAD_DIM, (h + 1) * HEAD_DIM)
+        jointt[where, :] = unrotate(dq_ref[where, :])
+    for j in range(KV_HEADS):
+        pair = pairs_ref[j].T
+        low = QW + j * HEAD_DIM
+        jointt[low : low + HEAD_DIM, :] = unrotate(pair[:HALF])
+        jointt[low + KW : low + KW + HEAD_DIM, :] = pair[HALF:].astype(BF)
+
+    weight = attend_ref.reshape(width, columns)
+    term = jnp.zeros((1, width), F32)
+    for low in range(0, tokens, PART):
+        where = slice(low, low + PART)
+        value = inputs[where, :]
+        scale = lax.rsqrt(jnp.sum(value * value, axis=-1, keepdims=True) * (1.0 / D) + eps_norm)
+        normed = value * scale
+        hidden[where, :] = (normed * gain).astype(BF)
+        hidden_grad = dot(jointt[:, where].T, weight[...], 1, 1)
+        hidden_grad = jnp.where(real, hidden_grad, 0.0)
+        term = term + jnp.sum(hidden_grad * normed, axis=0, keepdims=True)
+        upstream = hidden_grad * gain
+        mean = jnp.sum(upstream * normed, axis=-1, keepdims=True) * (1.0 / D)
+        result = middle_grad_ref[where, :] + scale * (upstream - normed * mean)
+        for s in range(shard_count):
+            grad_ref[where, s * own_rows : (s + 1) * own_rows] = result[
+                :, s * rows : s * rows + own_rows
+            ]
+    for s in range(shard_count):
+        gain_term[s] = jnp.broadcast_to(term[:, s * rows : (s + 1) * rows], (8, rows))
+    flip_blocks(hidden, flipped)
+    split_cores(at, flipped, hidden_own, hidden_give)
+    place = lax.broadcasted_iota(jnp.int32, (rows, rows), 0)
+    for lhs, core, ref in (
+        (hidden_give, 1 - at.c, total.give.at[0]),
+        (hidden_own, at.c, total.own),
+    ):
+        for z in range(lhs.shape[0]):
+            product = dot(lhs[z], jointt[...], 1, 1)
+            row = gain_term[2 * z + core][:1]
+            ref[z, :, :rows] = jnp.where(place == own_rows, row, product[:, :rows]).astype(BF)
+            ref[z, :, rows:] = product[:, rows:].astype(BF)
+        if ref is not total.own:
+            total.start(0)
+    for step in (total.zero, total.push, total.one, total.two, total.three):
+        step(0)
+    total.four(0)
+    total.five(0)
+    total.sent()
+
+
+def tail(x, middle_grad, dq, pairs, cosine, sine, attend_planes, number):
+    tokens, width = middle_grad.shape
+    shard_count, rows, columns = attend_planes.shape
     return pl.pallas_call(
-        reduce_kernel,
-        out_shape=jax.ShapeDtypeStruct((rows, columns), BF),
-        in_specs=[pl.BlockSpec(memory_space=ANY)],
-        out_specs=pl.BlockSpec(memory_space=VMEM),
-        scratch_shapes=Reduce.scratch(rows, columns),
+        tail_kernel,
+        out_shape=(
+            jax.ShapeDtypeStruct(x.shape, F32),
+            jax.ShapeDtypeStruct((rows, columns), BF),
+        ),
+        in_specs=[pl.BlockSpec(memory_space=VMEM)] * 7,
+        out_specs=(pl.BlockSpec(memory_space=VMEM),) * 2,
+        scratch_shapes=[
+            VMEM((tokens, width), F32),
+            VMEM((tokens, width), BF),
+            VMEM((columns, tokens), BF),
+            VMEM((shard_count, rows, tokens), BF),
+            VMEM((shard_count // 2, rows, tokens), BF),
+            VMEM((shard_count // 2, rows, tokens), BF),
+            VMEM((shard_count, 8, rows), F32),
+        ]
+        + Reduce.scratch(rows, [(0, columns)], 1),
         compiler_params=pltpu.CompilerParams(
             collective_id=number, has_side_effects=True, vmem_limit_bytes=BIG_VMEM
         ),
-        name="reduce",
-    )(parts)
+        name="tail",
+    )(x, middle_grad, dq, pairs, cosine, sine, attend_planes)
+
+
+def adam_parts(old_weight, gradient, first, second, decay_factor):
+    moment = beta_one * first + (1.0 - beta_one) * gradient
+    square = beta_two * second + (1.0 - beta_two) * gradient * gradient
+    corrected = moment * (1.0 / (1.0 - beta_one**STEP))
+    divisor = jnp.sqrt(square * (1.0 / (1.0 - beta_two**STEP))) + adam_eps
+    update = -learn_rate * (corrected / divisor + decay_factor * old_weight)
+    return moment, square, update
+
+
+def adam_kernel(grad_scale, own_rows, *refs):
+    attend_sum, rest_sum, attend_planes, rest_planes = refs[:4]
+    states, results = refs[4:12], refs[12:28]
+    buffers, weights, in_sems, out_sems = refs[28:44], refs[44:46], refs[46], refs[47]
+    shard = lax.axis_index("shard")
+    loads = [
+        pltpu.make_async_copy(attend_planes.at[shard], weights[0], in_sems.at[8]),
+        pltpu.make_async_copy(rest_planes.at[shard], weights[1], in_sems.at[9]),
+    ]
+    order = (0, 1, 3, 2)
+    for n in order:
+        for i in range(2):
+            loads.append(
+                pltpu.make_async_copy(
+                    states[2 * n + i], buffers[4 * n + 1 + i], in_sems.at[2 * n + i]
+                )
+            )
+    for load in loads:
+        load.start()
+    loads[0].wait()
+    loads[1].wait()
+    stores = []
+
+    def update(n, where, total, weight, flip):
+        gradient, moment, square, changed = buffers[4 * n : 4 * n + 4]
+        total = total.astype(F32)
+        weight = weight.astype(F32)
+        if flip:
+            total, weight = total.T[:, :own_rows], weight.T[:, :own_rows]
+        total = total * grad_scale
+        new_moment, new_square, step = adam_parts(
+            weight, total, moment[where], square[where], decay_rate
+        )
+        gradient[where] = total
+        moment[where] = new_moment
+        square[where] = new_square
+        changed[where] = weight + step
+
+    everything = slice(None)
+    for place, n in enumerate(order):
+        loads[2 + 2 * place].wait()
+        loads[3 + 2 * place].wait()
+        if n == 0:
+            columns = weights[0].shape[1]
+            for low in range(0, columns, CHUNK):
+                cols = slice(low, min(low + CHUNK, columns))
+                update(
+                    0,
+                    (everything, cols),
+                    attend_sum[:own_rows, cols],
+                    weights[0][:own_rows, cols],
+                    False,
+                )
+        elif n == 1:
+            cols = slice(3 * FF, 3 * FF + QW)
+            update(1, (everything, everything), rest_sum[:, cols], weights[1][:, cols], True)
+        else:
+            for c in range(FF // CHUNK):
+                for part in (0, 1) if n == 2 else (2,):
+                    low = 3 * CHUNK * c + CHUNK * part
+                    first = part * FF + CHUNK * c
+                    rows = slice(None) if n == 3 else slice(0, own_rows)
+                    total = rest_sum[rows, low : low + CHUNK]
+                    weight = weights[1][rows, first : first + CHUNK]
+                    if n == 3:
+                        where = (slice(c * CHUNK, (c + 1) * CHUNK), everything)
+                    else:
+                        where = (everything, slice(first, first + CHUNK))
+                    update(n, where, total, weight, n == 3)
+        for i in range(4):
+            store = pltpu.make_async_copy(
+                buffers[4 * n + i], results[4 * n + i], out_sems.at[4 * n + i]
+            )
+            store.start()
+            stores.append(store)
+    for store in stores:
+        store.wait()
+
+
+def adam(grad_scale, own_rows, attend_sum, rest_sum, attend_planes, rest_planes, states):
+    flat = [array for pair in states for array in pair]
+    shapes = [pair[0].shape for pair in states]
+    return pl.pallas_call(
+        functools.partial(adam_kernel, grad_scale, own_rows),
+        out_shape=tuple(jax.ShapeDtypeStruct(shape, F32) for shape in shapes for _ in range(4)),
+        in_specs=[pl.BlockSpec(memory_space=VMEM)] * 2 + [pl.BlockSpec(memory_space=ANY)] * 10,
+        out_specs=(pl.BlockSpec(memory_space=ANY),) * 16,
+        scratch_shapes=[VMEM(shape, F32) for shape in shapes for _ in range(4)]
+        + [VMEM(attend_planes.shape[1:], BF), VMEM(rest_planes.shape[1:], BF)]
+        + [DMA((10,)), DMA((16,))],
+        compiler_params=pltpu.CompilerParams(vmem_limit_bytes=BIG_VMEM),
+        name="adam",
+    )(attend_sum, rest_sum, attend_planes, rest_planes, *flat)
+
+
+def reduce_rows(parts):
+    own = lax.psum_scatter(parts, "shard", scatter_dimension=0)
+    return lax.psum(own, "rep")
 
 
 def spread_pairs(pairs, reach):
@@ -1174,13 +1681,10 @@
 
 
 def adam_step(weight_now, gradient, first, second, decay_factor):
-    old_weight = weight_now.astype(F32)
-    moment = beta_one * first + (1.0 - beta_one) * gradient
-    square = beta_two * second + (1.0 - beta_two) * gradient * gradient
-    corrected = moment / (1.0 - beta_one**STEP)
-    divisor = jnp.sqrt(square / (1.0 - beta_two**STEP)) + adam_eps
-    update = -learn_rate * (corrected / divisor + decay_factor * old_weight)
-    return (gradient, moment, square, old_weight + update, update)
+    moment, square, update = adam_parts(
+        weight_now.astype(F32), gradient, first, second, decay_factor
+    )
+    return (gradient, moment, square, update)
 
 
 def shards(
@@ -1231,9 +1735,13 @@
             planes[:, own_rows, :own_rows], ((0, 0), (0, rows - own_rows))
         ).reshape(1, width).astype(F32)
 
-    def add_gain(planes, term):
+    def add_gain(planes, term, column):
         row = term.reshape(shard_count, 1, rows).astype(planes.dtype)
-        return lax.dynamic_update_slice(planes, row, (0, own_rows, 0))
+        return lax.dynamic_update_slice(planes, row, (0, own_rows, column))
+
+    def in_chunks(expand, shrink):
+        parts = jnp.concatenate([expand, shrink], axis=1).reshape(-1, 3, FF // CHUNK, CHUNK)
+        return parts.transpose(0, 2, 1, 3).reshape(-1, 3 * FF)
 
     first_row = lax.axis_index("shard") * tokens
     local_index = first_row + jnp.arange(tokens, dtype=jnp.int32)
@@ -1268,33 +1776,30 @@
     rest_own = with_gain(
         jnp.concatenate([expand_weight, shrink_weight.T, output_weight.T], axis=1), expand_gain
     )
-    inputs = padded(block_input)
     if direct:
+        tables = (cosine_table[:, 0].T, sine_table[:, 0].T)
         attend_planes, rest_planes, window, qt, mixedt, lse = front(
-            inputs,
-            cosine_table[:, 0].T,
-            sine_table[:, 0].T,
-            feat,
-            qfeat,
-            attend_own,
-            rest_own,
-            shard_count,
-            0,
+            padded(block_input), *tables, feat, qfeat, attend_own, rest_own, shard_count, 0
+        )
+        block_output, middle_grad, dqt, own_pairs, rest_sum = rear(
+            block_input, block_cotangent, mixedt, rest_planes, window, feat, qt, qfeat, lse, 1
+        )
+        input_gradient, attend_sum = tail(
+            block_input, middle_grad, dqt, own_pairs, *tables, attend_planes, 2
         )
     else:
         attend_planes = lax.all_gather(attend_own, "shard", axis=0)
         rest_planes = lax.all_gather(rest_own, "shard", axis=0)
-    gain_one, gain_two = gain_of(attend_planes), gain_of(rest_planes)
-    joint_weight = attend_planes.reshape(width, JW)
-    rest = rest_planes.reshape(width, rest_own.shape[1])
-    expand_full, shrink_full, out_full = rest[:, : 2 * FF], rest[:, 2 * FF : 3 * FF], rest[:, 3 * FF :]
-    real = (jnp.arange(width, dtype=jnp.int32) % rows < own_rows)[None, :]
-
-    inputs = inputs.astype(F32)
-    scale_one = lax.rsqrt(jnp.sum(inputs * inputs, axis=-1, keepdims=True) * (1.0 / D) + eps_norm)
-    normed_one = inputs * scale_one
-    hidden_one = (normed_one * gain_one).astype(BF)
-    if not direct:
+        gain_one, gain_two = gain_of(attend_planes), gain_of(rest_planes)
+        joint_weight = attend_planes.reshape(width, JW)
+        rest = rest_planes.reshape(width, rest_own.shape[1])
+        expand_full, shrink_full, out_full = rest[:, : 2 * FF], rest[:, 2 * FF : 3 * FF], rest[:, 3 * FF :]
+        real = (jnp.arange(width, dtype=jnp.int32) % rows < own_rows)[None, :]
+
+        inputs = padded(block_input).astype(F32)
+        scale_one = lax.rsqrt(jnp.sum(inputs * inputs, axis=-1, keepdims=True) * (1.0 / D) + eps_norm)
+        normed_one = inputs * scale_one
+        hidden_one = (normed_one * gain_one).astype(BF)
         joint = dot(hidden_one, joint_weight)
         queries = rotate(joint[:, :QW].reshape(tokens, HEADS, HEAD_DIM), cosine_table, sine_table)
         key_rows = rotate(
@@ -1305,111 +1810,97 @@
         qt = queries.astype(BF).reshape(tokens, QW).T
         window = spread_pairs(pairs, reach)
         mixedt, lse = attend_forward(window, feat, qt, qfeat)
-    middle = inputs + dot(mixedt, out_full, 0, 1)
-    scale_two = lax.rsqrt(jnp.sum(middle * middle, axis=-1, keepdims=True) * (1.0 / D) + eps_norm)
-    normed_two = middle * scale_two
-    hidden_two = (normed_two * gain_two).astype(BF)
-    gate_up = dot(hidden_two, expand_full)
-    gate_value, upper_value = gate_up[:, :FF], gate_up[:, FF:]
-    sigmoid_gate = jax.nn.sigmoid(gate_value)
-    inner_rows = (gate_value * sigmoid_gate * upper_value).astype(BF)
-    block_output = middle + dot(inner_rows, shrink_full, 1, 1)
-
-    cotangent = padded(block_cotangent)
-    shrink_term = dot(cotangent, inner_rows, 0, 0)
-    inner_grad = dot(cotangent, shrink_full)
-    gate_grad = (
-        inner_grad * upper_value * sigmoid_gate * (1.0 + gate_value * (1.0 - sigmoid_gate))
-    ).astype(BF)
-    upper_grad = (inner_grad * gate_value * sigmoid_gate).astype(BF)
-    gate_up_grad = jnp.concatenate([gate_grad, upper_grad], axis=1)
-    expand_term = dot(hidden_two, gate_up_grad, 0, 0)
-    hidden_two_grad = jnp.where(real, dot(gate_up_grad, expand_full, 1, 1), 0.0)
-    gain_two_term = jnp.sum(hidden_two_grad * normed_two, axis=0)
-    middle_grad = cotangent.astype(F32) + norm_back(
-        hidden_two_grad * gain_two, normed_two, scale_two
-    )
-    branch_grad = middle_grad.astype(BF)
-    output_term = dot(branch_grad, mixedt, 0, 1)
-    gradt = dot(out_full, branch_grad, 0, 1).astype(BF)
-    rest_term = jnp.concatenate(
-        [expand_term.astype(BF), shrink_term.astype(BF), output_term.astype(BF)], axis=1
-    ).reshape(shard_count, rows, rest_own.shape[1])
-    rest_term = add_gain(rest_term, gain_two_term)
-    if direct:
-        dqt, own_pairs, rest_sum = back(
-            rest_term, window, feat, qt, qfeat, gradt, mixedt, lse, 1
+        middle = inputs + dot(mixedt, out_full, 0, 1)
+        scale_two = lax.rsqrt(jnp.sum(middle * middle, axis=-1, keepdims=True) * (1.0 / D) + eps_norm)
+        normed_two = middle * scale_two
+        hidden_two = (normed_two * gain_two).astype(BF)
+        gate_up = dot(hidden_two, expand_full)
+        gate_value, upper_value = gate_up[:, :FF], gate_up[:, FF:]
+        sigmoid_gate = jax.nn.sigmoid(gate_value)
+        inner_rows = (gate_value * sigmoid_gate * upper_value).astype(BF)
+        block_output = middle + dot(inner_rows, shrink_full, 1, 1)
+
+        cotangent = padded(block_cotangent)
+        shrink_term = dot(cotangent, inner_rows, 0, 0)
+        inner_grad = dot(cotangent, shrink_full)
+        gate_grad = (
+            inner_grad * upper_value * sigmoid_gate * (1.0 + gate_value * (1.0 - sigmoid_gate))
+        ).astype(BF)
+        upper_grad = (inner_grad * gate_value * sigmoid_gate).astype(BF)
+        gate_up_grad = jnp.concatenate([gate_grad, upper_grad], axis=1)
+        expand_term = dot(hidden_two, gate_up_grad, 0, 0)
+        hidden_two_grad = jnp.where(real, dot(gate_up_grad, expand_full, 1, 1), 0.0)
+        gain_two_term = jnp.sum(hidden_two_grad * normed_two, axis=0)
+        middle_grad = cotangent.astype(F32) + norm_back(
+            hidden_two_grad * gain_two, normed_two, scale_two
         )
-    else:
-        rest_sum = reduce_rows(rest_term, direct, 3)
+        branch_grad = middle_grad.astype(BF)
+        output_term = dot(branch_grad, mixedt, 0, 1)
+        gradt = dot(out_full, branch_grad, 0, 1).astype(BF)
+        rest_term = jnp.concatenate(
+            [in_chunks(expand_term, shrink_term), output_term], axis=1
+        ).astype(BF).reshape(shard_count, rows, rest_own.shape[1])
+        rest_sum = reduce_rows(add_gain(rest_term, gain_two_term, 3 * FF))
         dqt, dwindow = attend_backward(window, feat, qt, qfeat, gradt, mixedt, lse)
         own_pairs = collect_pairs(dwindow, reach)
-    own_pairs = own_pairs.transpose(1, 0, 2)
-    dq = dqt.T.reshape(tokens, HEADS, HEAD_DIM)
-    query_raw = rotate(dq, cosine_table, -sine_table).reshape(tokens, QW)
-    key_raw = rotate(own_pairs[..., :HEAD_DIM], cosine_table, -sine_table).reshape(tokens, KW)
-    value_raw = own_pairs[..., HEAD_DIM:].reshape(tokens, KW)
-    joint_grad = jnp.concatenate([query_raw, key_raw, value_raw], axis=1).astype(BF)
-    joint_term = dot(hidden_one, joint_grad, 0, 0).astype(BF)
-    hidden_one_grad = jnp.where(real, dot(joint_grad, joint_weight, 1, 1), 0.0)
-    gain_one_term = jnp.sum(hidden_one_grad * normed_one, axis=0)
-    input_gradient = middle_grad + norm_back(hidden_one_grad * gain_one, normed_one, scale_one)
-    attend_sum = reduce_rows(
-        add_gain(joint_term.reshape(shard_count, rows, JW), gain_one_term), direct, 2
+        block_output = unpadded(block_output)
+        own_pairs = own_pairs.transpose(1, 0, 2)
+        dq = dqt.T.reshape(tokens, HEADS, HEAD_DIM)
+        query_raw = rotate(dq, cosine_table, -sine_table).reshape(tokens, QW)
+        key_raw = rotate(own_pairs[..., :HEAD_DIM], cosine_table, -sine_table).reshape(tokens, KW)
+        value_raw = own_pairs[..., HEAD_DIM:].reshape(tokens, KW)
+        joint_grad = jnp.concatenate([query_raw, key_raw, value_raw], axis=1).astype(BF)
+        joint_term = dot(hidden_one, joint_grad, 0, 0).astype(BF)
+        hidden_one_grad = jnp.where(real, dot(joint_grad, joint_weight, 1, 1), 0.0)
+        gain_one_term = jnp.sum(hidden_one_grad * normed_one, axis=0)
+        input_gradient = middle_grad + norm_back(hidden_one_grad * gain_one, normed_one, scale_one)
+        attend_sum = reduce_rows(
+            add_gain(joint_term.reshape(shard_count, rows, JW), gain_one_term, 0)
+        )
+        input_gradient = unpadded(input_gradient)
+
+    grad_scale = grad_factor * token_count ** (-0.5)
+    first_gain, second_gain = (
+        adam_step(weight, total.astype(F32) * grad_scale, first, second, 0.0)
+        for weight, total, first, second in (
+            (
+                attend_gain,
+                attend_sum[own_rows, :own_rows],
+                attend_gain_first,
+                attend_gain_second,
+            ),
+            (
+                expand_gain,
+                rest_sum[own_rows, 3 * FF : 3 * FF + own_rows],
+                expand_gain_first,
+                expand_gain_second,
+            ),
+        )
     )
-
-    grad_scale = grad_factor * token_count ** (-0.5)
-    rest_grad, attend_grad = (total.astype(F32) * grad_scale for total in (rest_sum, attend_sum))
-    first_gain = adam_step(
-        attend_gain, attend_grad[own_rows, :own_rows], attend_gain_first, attend_gain_second, 0.0
+    matrices = adam(
+        grad_scale,
+        own_rows,
+        attend_sum,
+        rest_sum,
+        attend_planes,
+        rest_planes,
+        (
+            (attend_weight_first, attend_weight_second),
+            (output_weight_first, output_weight_second),
+            (expand_weight_first, expand_weight_second),
+            (shrink_weight_first, shrink_weight_second),
+        ),
     )
-    first_joint = adam_step(
-        attend_weight,
-        attend_grad[:own_rows],
-        attend_weight_first,
-        attend_weight_second,
-        decay_rate,
-    )
-    first_output = adam_step(
-        output_weight,
-        rest_grad[:own_rows, 3 * FF :].T,
-        output_weight_first,
-        output_weight_second,
-        decay_rate,
-    )
-    second_gain = adam_step(
-        expand_gain, rest_grad[own_rows, :own_rows], expand_gain_first, expand_gain_second, 0.0
-    )
-    second_expand = adam_step(
-        expand_weight,
-        rest_grad[:own_rows, : 2 * FF],
-        expand_weight_first,
-        expand_weight_second,
-        decay_rate,
-    )
-    second_shrink = adam_step(
-        shrink_weight,
-        rest_grad[:own_rows, 2 * FF : 3 * FF].T,
-        shrink_weight_first,
-        shrink_weight_second,
-        decay_rate,
+    first_joint, first_output, second_expand, second_shrink = (
+        matrices[4 * n : 4 * n + 4] for n in range(4)
     )
     steps = (first_gain, first_joint, first_output, second_gain, second_expand, second_shrink)
-    changed = [step[4] if step[0].ndim == 1 else step[3] for step in steps]
-    return (
-        unpadded(block_output),
-        unpadded(input_gradient),
-        *[step[0] for step in steps],
-        *[step[1] for step in steps],
-        *[step[2] for step in steps],
-        *changed,
-    )
+    return (block_output, input_gradient, *[step[i] for i in range(4) for step in steps])
 
 
 def solution(mesh):
     whole_rows = P(("rep", "shard"), None)
     state = (P("shard"), P("shard", None), P(None, "shard")) * 2
-    state = (state[0], state[1], state[2], state[3], state[4], state[5])
     direct = mesh.shape["rep"] == 4 and mesh.shape["shard"] == 8
     return jax.shard_map(
         functools.partial(shards, direct),

time: 481 us -> 378 us (0.79)
  matrix products: 73.8 us -> 0 us
  other arithmetic: 53.1 us -> 8.97 us
  Pallas kernels: 301 us -> 338 us
  local copies, waits for them, and re-layouts: 43.4 us -> 24.4 us
    dot_general x11 -> x0, matrix products: 73.8 us -> none  [dot(): lax.dot_general(a, b, (((ca,), (cb,)), ((), ())), preferred_element_type=...]
    pallas_call x2 -> x3, Pallas kernels: 202 us -> 238 us  [the longest x1 171 us: rear(): pl.pallas_call(rear_kernel, out_shape=(jax.ShapeDtypeStruct(x.shape, F32)...]
    concatenate x3 -> x0, other arithmetic: 18.2 us -> none  [the longest x1 14.7 us: shards(): jnp.concatenate([expand_term.astype(BF), shrink_term.astype(BF), output_t...]
    add x5 -> x0, other arithmetic: 15.5 us -> none  [the longest x4 13.4 us: adam_step(): return (gradient, moment, square, old_weight + update, update)]
    convert_element_type x4 -> x0, local copies, waits for them, and re-layouts: 8.24 us -> none  [the longest x1 4.35 us: shards(): joint_term = dot(hidden_one, joint_grad, 0, 0).astype(BF)]
    slice x6 -> x0, local copies, waits for them, and re-layouts: 8 us -> none  [the longest x2 4.17 us: unpadded(): tensor.reshape(tokens, shard_count, rows)[:, :, :own_rows]]
    unnamed x90 -> x46, local copies, waits for them, and re-layouts: 15.6 us -> 23.1 us
where the time goes in v3:
time: 378 us; the launch traced here: 372 us
  Pallas kernels  338 us (89%)
  local copies, waits for them, and re-layouts  24.4 us (6%)
  other arithmetic  8.97 us (2%)
    pallas_call x1, Pallas kernels, rear(): pl.pallas_call(rear_kernel, out_shape=(jax.ShapeDtypeStruct(x.shape, F32)...  171 us
    pallas_call x1, Pallas kernels, front(): pl.pallas_call(front_kernel, out_shape=(jax.ShapeDtypeStruct((shard_count...  99.7 us
    pallas_call x1, Pallas kernels, tail(): pl.pallas_call(tail_kernel, out_shape=(jax.ShapeDtypeStruct(x.shape, F32)...  52.9 us
    unnamed x46, local copies, waits for them, and re-layouts  23.1 us
    pallas_call x1, Pallas kernels, adam(): pl.pallas_call(functools.partial(adam_kernel, grad_scale, own_rows), out_...  14.1 us

profile of v3, /device:TPU:0, one launch (start us, length us, event | category | flops | bytes accessed | tf_op | source)
XLA Modules:
  0.0 372.1 jit_solution(5934985213312898182)
XLA Ops:
  0.7 2.4 copy.65.x_ref
  3.1 1.3 copy.66.cot_ref
  4.4 0.8 copy.60
  5.2 0.0 copy-start.16
  5.2 0.2 pad.12
  5.4 1.2 copy.78
  6.7 0.2 broadcast_in_dim.44
  6.8 0.1 select_reduce_fusion
  6.9 1.0 multiply_sine_fusion
  7.9 0.2 fusion.2
  8.1 0.0 copy-start.9
  8.2 0.0 copy-start.3
  8.2 0.0 copy-start.7
  8.2 0.0 copy-start.10
  8.2 1.2 and_convert_fusion
  9.4 0.1 pad.27.clone
  9.5 0.1 pad.26.clone
  9.6 1.3 maximum_maximum_fusion.feat_ref.feat_hbm
  10.9 0.1 select_convert_fusion
  10.9 0.1 pad.23.clone
  11.0 0.1 pad.22.clone
  11.1 0.8 maximum_maximum_fusion.1.qfeat_ref
  11.9 0.8 fusion.4.attend_own
  12.7 0.1 copy.64
  12.8 0.0 copy-done.3
  12.8 0.0 copy-done.7
  12.8 0.0 copy-done.10
  12.8 2.0 fusion.1.rest_own
  14.9 99.7 %front.1 = (bf16[8,128,1600]{2,1,0:T(8,128)(2,1)}, bf16[8,128,8640]{2,1,0:T(8,128)(2,1)}, bf16[5,5,512,128]{3,2,1,0:T(8,128)(2,1)}, bf16[960,512]{1,0:T(8,128)(2...) custom-call(bf16[512,1024]{1,0:T(8,128)(2,1)} %bitcast.44, f32[32,512]{1,0:T(8,128)} %get-tuple-element.145.cos_ref, ...), custom_call_target="tpu_custom_call" | custom-call | tf_op jit(solution)/shard_map/front/pallas_call | solution.py:972
  114.6 171.0 %rear.1 = (f32[512,960]{1,0:T(8,128)}, f32[512,1024]{1,0:T(8,128)}, f32[960,512]{1,0:T(8,128)}, f32[5,512,128]{2,1,0:T(8,128)}, bf16[128,8704]{1,0:T(8,128)(2,1)}) custom-call(bf16[512,960]{1,0:T(8,128)(2,1)} %copy.65.x_ref, bf16[512,960]{1,0:T(8,128)(2,1)} %copy.66.cot_ref, bf16[960,512]{1,0:T(8,128)(2,1)} %get-tuple-element.55.mixed_ref, ...), custom_call_target="tpu_custom_call" | custom-call | tf_op jit(solution)/shard_map/rear/pallas_call | solution.py:1387
  285.6 3.2 copy.70
  288.8 52.9 %tail.1 = (f32[512,960]{1,0:T(8,128)}, bf16[128,1600]{1,0:T(8,128)(2,1)}) custom-call(bf16[512,960]{1,0:T(8,128)(2,1)} %copy.65.x_ref, f32[512,1024]{1,0:T(8,128)} %get-tuple-element.61.middle_grad_ref, f32[960,512]{1,0:T(8,128)} %get-tuple-element.62.dq_ref, f32[5,512,128]{2,1,0:T(8,128)} %get-tuple-element.63.pairs_ref, ...), custom_call_target="tpu_custom_call" | custom-call | tf_op jit(solution)/shard_map/tail/pallas_call | solution.py:1510
  341.7 0.0 copy-start.12
  341.7 0.0 copy-start.13
  341.7 0.0 copy-start.14
  341.7 0.0 copy-start.15
  341.8 0.0 copy-start.4
  341.8 3.1 copy.71
  344.8 0.0 copy-start.5
  344.9 0.0 copy-done.12
  344.9 1.3 add_multiply_fusion
  346.2 1.5 copy.68.refs_10_
  347.8 1.5 copy.69.refs_11_
  349.3 14.1 %adam.1 = (f32[120,1600]{1,0:T(8,128)}, f32[120,1600]{1,0:T(8,128)}, f32[120,1600]{1,0:T(8,128)}, f32[120,1600]{1,0:T(8,128)}, f32[960,120]{1,0:T(8,128)}, /*ind...) custom-call(bf16[128,1600]{1,0:T(8,128)(2,1)} %get-tuple-element.66., ...), custom_call_target="tpu_custom_call" | custom-call | tf_op jit(solution)/shard_map/adam/pallas_call | solution.py:1626
  363.4 2.8 copy.72
  366.2 2.9 copy.73
  369.1 1.4 copy.74
  370.5 1.4 copy.75
  (28 shorter events, 0.1 us)
Async XLA Ops:
  0.7 3.7 %copy-start = (bf16[512,960]{0,1:T(8,128)(2,1)S(1)}, bf16[512,960]{0,1:T(8,128)(2,1)}, u32[]{:S(2)}) copy-start(bf16[512,960]{0,1:T(8,128)(2,1)} %param.21) | copy-start | bytes 2949124
  0.7 2.4 copy-start.6
  5.2 1.5 copy-start.16
  6.6 5.2 %copy-start.8 = (bf16[120,1600]{1,0:T(8,128)(2,1)S(1)}, bf16[120,1600]{1,0:T(8,128)(2,1)}, u32[]{:S(2)}) copy-start(bf16[120,1600]{1,0:T(8,128)(2,1)} %param.25) | copy-start | bytes 1152004
  6.6 5.2 %copy-start.11 = (bf16[120]{0:T(256)(128)(2,1)S(1)}, bf16[120]{0:T(256)(128)(2,1)}, u32[]{:S(2)}) copy-start(bf16[120]{0:T(256)(128)(2,1)} %param.24) | copy-start | bytes 724
  8.1 4.5 %copy-start.9 = (bf16[960,120]{1,0:T(8,128)(2,1)S(1)}, bf16[960,120]{1,0:T(8,128)(2,1)}, u32[]{:S(2)}) copy-start(bf16[960,120]{1,0:T(8,128)(2,1)} %param.26) | copy-start | bytes 691204
  8.2 4.6 %copy-start.3 = (bf16[120,5120]{1,0:T(8,128)(2,1)S(1)}, bf16[120,5120]{1,0:T(8,128)(2,1)}, u32[]{:S(2)}) copy-start(bf16[120,5120]{1,0:T(8,128)(2,1)} %param.28) | copy-start | bytes 3686404
  8.2 4.6 %copy-start.7 = (bf16[2560,120]{0,1:T(8,128)(2,1)S(1)}, bf16[2560,120]{0,1:T(8,128)(2,1)}, u32[]{:S(2)}) copy-start(bf16[2560,120]{0,1:T(8,128)(2,1)} %param.29) | copy-start | bytes 1843204
  8.2 4.6 %copy-start.10 = (bf16[120]{0:T(256)(128)(2,1)S(1)}, bf16[120]{0:T(256)(128)(2,1)}, u32[]{:S(2)}) copy-start(bf16[120]{0:T(256)(128)(2,1)} %param.27) | copy-start | bytes 724
  341.7 3.2 copy-start.12
  341.7 3.2 copy-start.13
  341.7 3.2 copy-start.14
  341.7 3.1 copy-start.15
  341.8 4.5 %copy-start.4 = (f32[2560,120]{0,1:T(8,128)S(1)}, f32[2560,120]{0,1:T(8,128)}, u32[]{:S(2)}) copy-start(f32[2560,120]{0,1:T(8,128)} %param.35) | copy-start | bytes 3686404
  344.8 2.9 copy-start.5
  363.4 5.7 %copy-start.2 = (f32[2560,120]{1,0:T(8,128)S(1)}, f32[2560,120]{1,0:T(8,128)}, u32[]{:S(2)}) copy-start(f32[2560,120]{1,0:T(8,128)} %get-tuple-element.129) | copy-start | bytes 3686404
  366.2 4.3 %copy-start.1 = (f32[2560,120]{1,0:T(8,128)S(1)}, f32[2560,120]{1,0:T(8,128)}, u32[]{:S(2)}) copy-start(f32[2560,120]{1,0:T(8,128)} %get-tuple-element.135) | copy-start | bytes 3686404

commit v4 on v3

--- a/solution.py
+++ b/solution.py
@@ -3,6 +3,7 @@
 
 import jax
 import jax.numpy as jnp
+import numpy as np
 from jax import lax
 from jax.experimental import pallas as pl
 from jax.experimental.pallas import tpu as pltpu
@@ -43,6 +44,7 @@
 NEG = -1e30
 EXP_SCALE = HEAD_DIM**-0.5 * math.log2(math.e)
 BIG_VMEM = 60 * 2**20
+PART = 128
 
 
 def dot(a, b, ca=1, cb=0):
@@ -187,7 +189,7 @@
 
 
 def attend_backward_head(
-    h, qt_ref, qfeat_ref, gradt_ref, mixed_ref, lse_ref, dq_ref, kvf, kt, qa, da, acc, rhs
+    h, put_query, qt_ref, qfeat_ref, gradt_ref, mixed_ref, lse_ref, kvf, kt, qa, da, acc, rhs
 ):
     tokens = qt_ref.shape[1]
     lanes = qfeat_ref.shape[0]
@@ -228,7 +230,7 @@
             query_grads[chunk] = term if old is None else old + term
     for chunk in range(tokens // QC):
         low = chunk * QC
-        dq_ref[pl.ds(row, HEAD_DIM), low : low + QC] = query_grads[chunk] * HEAD_DIM**-0.5
+        put_query(row, low, query_grads[chunk] * HEAD_DIM**-0.5)
 
 
 def attend_backward_done(j, acc, dkv_ref):
@@ -257,12 +259,22 @@
     kvf, kt, qa, da, acc, rhs = scratch
     attend_backward_setup(feat_ref, kvf, qa, da, rhs)
 
+    def put_query(row, low, value):
+        dq_ref[pl.ds(row, HEAD_DIM), low : low + QC] = value
+
     def key_head(j, _):
         attend_backward_keys(j, kv_ref, kvf, kt, acc)
 
         def head(g, _):
             attend_backward_head(
-                j * GROUP + g, qt_ref, qfeat_ref, gradt_ref, mixed_ref, lse_ref, dq_ref, *scratch
+                j * GROUP + g,
+                put_query,
+                qt_ref,
+                qfeat_ref,
+                gradt_ref,
+                mixed_ref,
+                lse_ref,
+                *scratch,
             )
             return 0
 
@@ -303,6 +315,7 @@
         self.has_later, self.has_earlier = self.z < 3, self.z > 0
         self.later = (self.r, lax.min(self.s + 2, 7))
         self.earlier = (self.r, lax.max(self.s - 2, 0))
+        self.two_earlier = (self.r, lax.max(self.s - 4, 0))
 
     def z_to(self, k):
         return lax.rem(self.z + k, 4)
@@ -583,7 +596,7 @@
         return self.copy(1, j, self.grads.at[1, j], self.rb.at[j], self.at.core_side)
 
     def far(self, j):
-        return self.copy(2, j, self.t2.at[j], self.r2.at[j], self.at.earlier)
+        return self.copy(2, j, self.t2.at[j], self.r2.at[j], self.at.two_earlier)
 
     def near(self, j):
         return self.copy(3, j, self.t1.at[j], self.r1.at[j], self.at.earlier)
@@ -601,25 +614,21 @@
         self.t2[j] = (self.grads[0, j].astype(F32) + jnp.where(even, none, from_b)).astype(BF)
         pl.when(self.at.z > 1)(self.far(j).start)
         self.t1[j] = (self.grads[2, j].astype(F32) + jnp.where(even, from_b, from_a)).astype(BF)
+        pl.when(self.at.has_earlier)(self.near(j).start)
         self.out[j] = self.grads[4, j].astype(F32) + jnp.where(even, from_a, none)
 
     def two(self, j):
-        at = self.at
-
-        @pl.when(at.has_earlier & at.has_later)
-        def _():
-            self.far(j).wait_recv()
-            self.t1[j] = (self.t1[j].astype(F32) + self.r2[j].astype(F32)).astype(BF)
-
-        pl.when(at.has_earlier)(self.near(j).start)
-
-    def three(self, j):
         at = self.at
 
         @pl.when(at.has_later)
         def _():
             self.near(j).wait_recv()
             self.out[j] = self.out[j] + self.r1[j].astype(F32)
+
+        @pl.when(at.z < 2)
+        def _():
+            self.far(j).wait_recv()
+            self.out[j] = self.out[j] + self.r2[j].astype(F32)
 
     def sent(self, j):
         at = self.at
@@ -814,30 +823,95 @@
 
 def at_steps(i, events):
     for n, event in events:
-        pl.when(i == n)(event)
+        if n >= 0:
+            pl.when(i == n)(event)
+
+
+def flip_blocks(value, dst):
+    blocks, rows, _ = dst.shape
+    for s in range(blocks):
+        dst[s] = value[:, s * rows : (s + 1) * rows].T
+
+
+def sequence_features(lengths_ref, first_row, feat_ref, qfeat_ref):
+    keys, lanes = feat_ref.shape
+    tokens = qfeat_ref.shape[1]
+    count = lengths_ref.shape[1]
+    starts, ends = [], []
+    for i in range(count):
+        starts.append(ends[-1] if ends else 0)
+        ends.append(starts[-1] + lengths_ref[0, i])
+    for low in range(0, keys, tokens):
+        place = lax.broadcasted_iota(jnp.int32, (tokens, lanes), 0)
+        key = first_row - (keys - tokens) + low + place
+        column = lax.broadcasted_iota(jnp.int32, (tokens, lanes), 1)
+        value = jnp.where(column >= ONES, 1.0, 0.0)
+        value = jnp.where((column == count) & (key < 0), 1.0, value)
+        for i in range(count):
+            inside = (column == i) & (key >= starts[i]) & (key < ends[i])
+            value = jnp.where(inside, 1.0, value)
+        feat_ref[low : low + tokens, :] = value.astype(BF)
+    row = lax.broadcasted_iota(jnp.int32, (lanes, tokens), 0)
+    query = first_row + lax.broadcasted_iota(jnp.int32, (lanes, tokens), 1)
+    value = jnp.where(row == count, NEG, 0.0)
+    start = jnp.zeros((1, tokens), jnp.int32)
+    for i in range(count):
+        inside = (query >= starts[i]) & (query < ends[i])
+        value = jnp.where((row == i) & jnp.logical_not(inside), NEG, value)
+        start = jnp.where(inside[:1], starts[i], start)
+    qfeat_ref[...] = value.astype(BF)
+    return query[:1] - start
 
 
 def front_kernel(
-    x_ref,
+    lengths_ref,
+    inverse_ref,
+    xt_ref,
+    cott_ref,
+    attend_gain,
+    attend_weight,
+    expand_gain,
+    expand_weight,
+    shrinkt,
+    output_weight,
+    rest_ref,
+    attend_hbm,
+    win_hbm,
+    feat_hbm,
+    qt_hbm,
+    flipped_hbm,
+    x_hbm,
+    cot_hbm,
+    cott_hbm,
+    middle_hbm,
+    hidden_hbm,
+    hiddent_hbm,
+    mixed_ref,
+    lse_ref,
+    qfeat_ref,
     cos_ref,
     sin_ref,
-    feat_ref,
-    qfeat_ref,
-    attend_own,
-    rest_own,
-    attend_ref,
-    rest_ref,
-    win_ref,
-    qt_ref,
-    mixed_ref,
-    lse_ref,
     kvf,
     vt,
     qa,
     sb,
+    attend_own,
+    rest_own,
+    attend_ref,
+    win_ref,
+    feat_ref,
+    qt_ref,
+    flipped,
+    inputs,
+    cot,
+    cott,
+    middle,
     hidden,
+    hiddent,
     kvt,
+    out_weight,
     local_sems,
+    store_sems,
     gather_send,
     gather_recv,
     spread_send,
@@ -846,7 +920,7 @@
     at = Place()
     shard_count, rows, columns = attend_ref.shape
     width = shard_count * rows
-    tokens = x_ref.shape[0]
+    tokens = xt_ref.shape[1]
     kv_heads = win_ref.shape[1]
     own_rows = D // shard_count
     cut = 2 * FF
@@ -858,40 +932,90 @@
         )
 
     first = gather(0, attend_own, attend_ref, (0, columns))
-    second = gather(1, rest_own, rest_ref, (0, cut))
-    third = gather(2, rest_own, rest_ref, (cut, rest_own.shape[1] - cut))
+    second = gather(1, rest_own, rest_ref, (3 * FF, QW))
+    third = gather(2, rest_own, rest_ref, (0, cut))
+    fourth = gather(3, rest_own, rest_ref, (cut, FF))
     spread = Spread(at, win_ref, spread_send, spread_recv)
-
+    stores = []
+
+    def store(src, dst):
+        copy = pltpu.make_async_copy(src, dst, store_sems.at[len(stores)])
+        copy.start()
+        stores.append(copy)
+
+    def place(ref, low, weight, gain):
+        count = weight.shape[1]
+        block = own_rows // 16 * 16
+        ref[:block, low : low + count] = weight[:block]
+        tail = jnp.concatenate(
+            [weight[block:].astype(F32), jnp.zeros((rows - own_rows, count), F32)], axis=0
+        )
+        if gain is not None:
+            row = jnp.concatenate(
+                [gain[...].astype(F32), jnp.zeros((1, count - own_rows), F32)], axis=1
+            )
+            where = lax.broadcasted_iota(jnp.int32, tail.shape, 0) == own_rows - block
+            tail = jnp.where(where, row, tail)
+        ref[block:, low : low + count] = tail.astype(BF)
+
+    place(attend_own, 0, attend_weight, attend_gain)
     first.start_z()
     first.start_core()
+    place(rest_own, 3 * FF, output_weight[...].T, expand_gain)
     second.start_core()
+    place(rest_own, 0, expand_weight, None)
     third.start_core()
+    place(rest_own, cut, shrinkt, None)
+    fourth.start_core()
     spread.clear()
+    position = sequence_features(lengths_ref, at.s * tokens, feat_ref, qfeat_ref)
+    store(feat_ref, feat_hbm)
     attend_forward_setup(feat_ref, qfeat_ref, kvf, vt, qa)
-    for i in range(3):
-        first.z(i)
+    phases = inverse_ref[...] * position.astype(F32)
+    cos_ref[...] = jnp.cos(phases)
+    sin_ref[...] = jnp.sin(phases)
+    first.z(0)
+    for s in range(shard_count):
+        block = slice(s * rows, (s + 1) * rows)
+        source = slice(s * own_rows, (s + 1) * own_rows)
+        blank = jnp.zeros((rows - own_rows, tokens), F32)
+        value = jnp.concatenate([xt_ref[source, :].astype(F32), blank], axis=0)
+        inputs[:, block] = value.T.astype(BF)
+    first.z(1)
+    for s in range(shard_count):
+        block = slice(s * rows, (s + 1) * rows)
+        source = slice(s * own_rows, (s + 1) * own_rows)
+        value = jnp.concatenate([cott_ref[source, :].astype(F32), blank], axis=0)
+        cott[s] = value.astype(BF)
+        cot[:, block] = value.T.astype(BF)
+    store(inputs, x_hbm)
+    store(cot, cot_hbm)
+    store(cott, cott_hbm)
+    first.z(2)
     second.start_z()
     for i in range(3):
         first.cross(i)
     second.z(0)
+    third.start_z()
     for i in range(3):
         first.last(i)
     first.landed()
-
-    inputs = x_ref[...].astype(F32)
-    scale = lax.rsqrt(jnp.sum(inputs * inputs, axis=-1, keepdims=True) * (1.0 / D) + eps_norm)
+    store(attend_ref, attend_hbm)
+
+    value = inputs[...].astype(F32)
+    scale = scale_of(value)
     for s in range(shard_count):
         lane = slice(s * rows, (s + 1) * rows)
         gain = attend_ref[s, own_rows : own_rows + 1, :rows].astype(F32)
-        hidden[:, lane] = (x_ref[:, lane].astype(F32) * scale * gain).astype(BF)
+        hidden[:, lane] = (inputs[:, lane].astype(F32) * scale * gain).astype(BF)
 
     def project(start):
         stop = min(start + 256, columns)
         weight = attend_ref[:, :, start:stop].reshape(width, stop - start)
-        flipped = dot(hidden[...], weight).T
+        turned = dot(hidden[...], weight).T
         for low in range(0, stop - start, HEAD_DIM):
             column = start + low
-            head = flipped[low : low + HEAD_DIM, :]
+            head = turned[low : low + HEAD_DIM, :]
             if column < QW + KW:
                 half = HEAD_DIM // 2
                 front, back = head[:half], head[half:]
@@ -916,27 +1040,33 @@
         win_ref[4, j] = kvt[j].T
         spread.start(j)
     second.z(1)
-    third.start_z()
+    second.z(2)
     for start in range(0, split, 256):
         project(start)
+    store(qt_ref, qt_hbm)
+    flip_blocks(hidden, flipped)
+    store(flipped, flipped_hbm)
     spread.one(0)
-    second.z(2)
+    third.z(0)
     spread.one(1)
     spread.two(0)
     events = [
-        (0, lambda: third.z(0)),
-        (1, lambda: second.cross(0)),
+        (0, lambda: second.cross(0)),
+        (1, lambda: second.cross(1)),
         (2, lambda: third.z(1)),
-        (3, lambda: second.cross(1)),
+        (2, lambda: second.cross(2)),
+        (3, lambda: second.last(0)),
+        (4, lambda: second.last(1)),
         (4, lambda: third.z(2)),
-        (5, lambda: second.cross(2)),
+        (4, fourth.start_z),
+        (5, lambda: second.last(2)),
         (6, lambda: third.cross(0)),
-        (7, lambda: second.last(0)),
+        (7, lambda: fourth.z(0)),
         (8, lambda: third.cross(1)),
-        (9, lambda: second.last(1)),
+        (9, lambda: fourth.z(1)),
         (10, lambda: third.cross(2)),
-        (11, lambda: second.last(2)),
-        (12, lambda: third.last(0)),
+        (11, lambda: third.last(0)),
+        (12, lambda: fourth.z(2)),
         (13, lambda: third.last(1)),
         (14, lambda: third.last(2)),
     ]
@@ -958,40 +1088,93 @@
         return 0
 
     lax.fori_loop(0, kv_heads, key_head, 0)
+    store(win_ref, win_hbm)
     second.landed()
+    load = pltpu.make_async_copy(
+        rest_ref.at[:, :, pl.ds(3 * FF, QW)], out_weight, local_sems.at[4]
+    )
+    load.start()
+    for i in range(3):
+        fourth.cross(i)
+    load.wait()
+    real = real_lanes(width, rows, own_rows)
+    gain = jnp.concatenate(
+        [out_weight[s, own_rows : own_rows + 1, :rows].astype(F32) for s in range(shard_count)],
+        axis=1,
+    )
+    gain = jnp.where(real, gain, 0.0)
+    out_full = out_weight.reshape(width, QW)
+    for low in range(0, tokens, PART):
+        where = slice(low, low + PART)
+        value = jnp.where(real, dot(mixed_ref[:, where].T, out_full[...], 1, 1), 0.0)
+        value = inputs[where, :].astype(F32) + value
+        middle[where, :] = value
+        hidden[where, :] = (value * scale_of(value) * gain).astype(BF)
+    store(middle, middle_hbm)
+    store(hidden, hidden_hbm)
+    flip_blocks(hidden, hiddent)
+    store(hiddent, hiddent_hbm)
+    for i in range(3):
+        fourth.last(i)
     third.landed()
-    for part in (first, second, third):
+    fourth.landed()
+    for part in (first, second, third, fourth):
         part.sent()
-
-
-def front(x, cosine, sine, feat, qfeat, attend_own, rest_own, shard_count, number):
-    tokens, width = x.shape
-    keys, lanes = feat.shape
-    rows = attend_own.shape[0]
-    window = (keys // tokens, KV_HEADS, tokens, lanes)
+    for copy in stores:
+        copy.wait()
+
+
+def front(lengths, xt, cott, weights, shard_count, number):
+    _, tokens = xt.shape
+    attend_weight, expand_weight, output_weight = weights[1], weights[3], weights[5]
+    own_rows, columns = attend_weight.shape
+    rows = -(-(own_rows + 2) // 16) * 16
+    width = shard_count * rows
+    lanes = 2 * HEAD_DIM
+    blocks = (MAXLEN - 2) // tokens + 2
+    keys = blocks * tokens
+    half = HEAD_DIM // 2
+    inverse = rope_base ** (-(2.0 * np.arange(half, dtype=np.float32) / HEAD_DIM))
+    rest_columns = 3 * FF + QW
+
+    def shape(*sizes, dtype=BF):
+        return jax.ShapeDtypeStruct(sizes, dtype)
+
+    attend, rest = shape(shard_count, rows, columns), shape(shard_count, rows, rest_columns)
+    window = shape(blocks, KV_HEADS, tokens, lanes)
+    feat, heads = shape(keys, lanes), shape(QW, tokens)
+    natural, turned = shape(tokens, width), shape(shard_count, rows, tokens)
+    middle = shape(tokens, width, dtype=F32)
+    in_hbm = (
+        rest, attend, window, feat, heads, turned, natural, natural, turned, middle, natural, turned
+    )
+    table = shape(half, tokens, dtype=F32)
+    in_vmem = (heads, shape(HEADS, 1, tokens, dtype=F32), shape(lanes, tokens), table, table)
+
+    def scratch(struct):
+        return VMEM(struct.shape, struct.dtype)
+
     return pl.pallas_call(
         front_kernel,
-        out_shape=(
-            jax.ShapeDtypeStruct((shard_count,) + attend_own.shape, BF),
-            jax.ShapeDtypeStruct((shard_count,) + rest_own.shape, BF),
-            jax.ShapeDtypeStruct(window, BF),
-            jax.ShapeDtypeStruct((QW, tokens), BF),
-            jax.ShapeDtypeStruct((QW, tokens), BF),
-            jax.ShapeDtypeStruct((HEADS, 1, tokens), F32),
-        ),
-        in_specs=[pl.BlockSpec(memory_space=VMEM)] * 6 + [pl.BlockSpec(memory_space=ANY)],
-        out_specs=(
-            pl.BlockSpec(memory_space=VMEM),
-            pl.BlockSpec(memory_space=ANY),
-        )
-        + (pl.BlockSpec(memory_space=VMEM),) * 4,
+        out_shape=in_hbm + in_vmem,
+        in_specs=[pl.BlockSpec(memory_space=pltpu.SMEM)] + [pl.BlockSpec(memory_space=VMEM)] * 9,
+        out_specs=(pl.BlockSpec(memory_space=ANY),) * len(in_hbm)
+        + (pl.BlockSpec(memory_space=VMEM),) * len(in_vmem),
         scratch_shapes=attend_forward_scratch(keys, lanes, tokens)
+        + [VMEM((rows, columns), BF), VMEM((rows, rest_columns), BF)]
         + [
-            VMEM((tokens, width), BF),
+            scratch(struct)
+            for struct in (
+                attend, window, feat, heads, turned, natural, natural, turned, middle, natural, turned
+            )
+        ]
+        + [
             VMEM((KV_HEADS, lanes, tokens), BF),
-            DMA((3,)),
-            DMA((3, Gather.COUNT)),
-            DMA((3, Gather.COUNT)),
+            VMEM((shard_count, rows, QW), BF),
+            DMA((5,)),
+            DMA((len(in_hbm),)),
+            DMA((4, Gather.COUNT)),
+            DMA((4, Gather.COUNT)),
             DMA((5, KV_HEADS)),
             DMA((5, KV_HEADS)),
         ],
@@ -999,74 +1182,98 @@
             collective_id=number, has_side_effects=True, vmem_limit_bytes=BIG_VMEM
         ),
         name="front",
-    )(x, cosine, sine, feat, qfeat, attend_own, rest_own)
-
-
-def pad_features(src, dst, own_rows, rows):
-    for s in range(D // own_rows):
-        dst[:, s * rows : s * rows + own_rows] = src[:, s * own_rows : (s + 1) * own_rows].astype(
-            dst.dtype
-        )
-        dst[:, s * rows + own_rows : (s + 1) * rows] = jnp.zeros(
-            (dst.shape[0], rows - own_rows), dst.dtype
-        )
-
-
-def flip_blocks(value, dst):
-    blocks, rows, _ = dst.shape
-    for s in range(blocks):
-        dst[s] = value[:, s * rows : (s + 1) * rows].T
-
-
-def split_cores(at, flipped, own, give):
-    for z in range(own.shape[0]):
-        own[z] = flipped[2 * z + at.c]
-        give[z] = flipped[2 * z + 1 - at.c]
-
-
-PART = 128
+    )(lengths, jnp.asarray(inverse, F32)[:, None], xt, cott, *weights)
+
+
 SUB = 256
 CHUNK = 2 * SUB
 
 
-def rear_chunks():
-    chunks = [(3 * CHUNK * n, 3 * CHUNK) for n in range(FF // CHUNK)]
-    return chunks + [(3 * FF, -(-QW // 128) * 128)]
+def up_to_lanes(columns):
+    return -(-columns // 128) * 128
+
+
+def sum_chunks():
+    widths = [3 * CHUNK] * (FF // CHUNK) + [up_to_lanes(QW)] * 2 + [2 * KW]
+    return [(sum(widths[:n]), width) for n, width in enumerate(widths)]
+
+
+OUT_CHUNK = FF // CHUNK
+QUERY_CHUNK, PAIR_CHUNK = OUT_CHUNK + 1, OUT_CHUNK + 2
+
+
+def unrotate(head, cosine, sine):
+    half = HEAD_DIM // 2
+    front, back = head[:half], head[half:]
+    return jnp.concatenate(
+        [front * cosine + back * sine, back * cosine - front * sine], axis=0
+    ).astype(BF)
+
+
+def real_lanes(width, rows, own_rows):
+    return lax.rem(lax.broadcasted_iota(jnp.int32, (1, width), 1), rows) < own_rows
+
+
+def scale_of(value):
+    return lax.rsqrt(jnp.sum(value * value, axis=-1, keepdims=True) * (1.0 / D) + eps_norm)
+
+
+def put_turned(value, dst, rows, own_rows):
+    turned = value.T
+    for s in range(turned.shape[0] // rows):
+        dst[s * own_rows : (s + 1) * own_rows, :] = turned[s * rows : s * rows + own_rows]
+
+
+def put_gradient(total, n, column, ref, z, product, row=None):
+    rows, columns = product.shape
+    first = product[:, :rows]
+    if row is not None:
+        own_rows, gain_row = row
+        place = lax.broadcasted_iota(jnp.int32, (rows, rows), 0)
+        first = jnp.where(place == own_rows, gain_row, first)
+    ref[z, :, column : column + rows] = first.astype(BF)
+    ref[z, :, column + rows : column + columns] = product[:, rows:].astype(BF)
+    width = total.chunks[n][1]
+    if columns < width:
+        ref[z, :, column + columns : column + width] = jnp.zeros((rows, width - columns), BF)
 
 
 def feed_forward(
     at,
     total,
-    x_ref,
-    cot_ref,
     mixed_ref,
+    gradt_ref,
+    middle_hbm,
+    hidden_hbm,
+    hiddent_hbm,
+    cot_hbm,
+    cott_hbm,
     rest_ref,
-    out_ref,
-    middle_grad_ref,
-    gradt_ref,
+    out_hbm,
+    middle_grad_hbm,
     events,
     cot,
     hidden,
     middle,
     acc_out,
     acc_grad,
-    flipped,
     hidden_own,
     hidden_give,
     cot_own,
     cot_give,
+    flipped,
     out_weight,
-    gain_rows,
     gain_term,
     weights,
+    results,
     sems,
+    load_sems,
 ):
     shard_count, rows, _ = rest_ref.shape
     width = shard_count * rows
-    tokens = x_ref.shape[0]
+    tokens = middle.shape[0]
     own_rows = D // shard_count
     planes = shard_count // 2
-    block = own_rows // 16 * 16
 
     def weight_copies(n, slot):
         return [
@@ -1078,47 +1285,23 @@
             for i in range(3)
         ]
 
-    out_copy = pltpu.make_async_copy(
-        rest_ref.at[:, :, pl.ds(3 * FF, QW)], out_weight, sems.at[2, 0]
-    )
-    gain_copy = pltpu.make_async_copy(
-        rest_ref.at[:, pl.ds(block, rows - block), pl.ds(0, 128)], gain_rows, sems.at[2, 1]
-    )
-    out_copy.start()
-    gain_copy.start()
-    for copy in weight_copies(0, 0):
+    pairs = [(hidden_hbm, hidden), (cot_hbm, cot)]
+    for z in range(planes):
+        mine, other = 2 * z + at.c, 2 * z + 1 - at.c
+        pairs += [(hiddent_hbm.at[mine], hidden_own.at[z]), (cott_hbm.at[mine], cot_own.at[z])]
+        pairs += [(hiddent_hbm.at[other], hidden_give.at[z])]
+        pairs += [(cott_hbm.at[other], cot_give.at[z])]
+    pairs += [(middle_hbm, middle), (rest_ref.at[:, :, pl.ds(3 * FF, QW)], out_weight)]
+    loads = [
+        pltpu.make_async_copy(src, dst, load_sems.at[i]) for i, (src, dst) in enumerate(pairs)
+    ]
+    for copy in weight_copies(0, 0) + loads:
         copy.start()
-    pad_features(x_ref, middle, own_rows, rows)
-    pad_features(cot_ref, cot, own_rows, rows)
-    flip_blocks(cot, flipped)
-    split_cores(at, flipped, cot_own, cot_give)
-
-    gain_copy.wait()
-    gain = jnp.concatenate(
-        [
-            gain_rows[s, own_rows - block : own_rows - block + 1, :rows].astype(F32)
-            for s in range(shard_count)
-        ],
-        axis=1,
-    )
-    lane = lax.broadcasted_iota(jnp.int32, (1, width), 1)
-    real = lax.rem(lane, rows) < own_rows
-    gain = jnp.where(real, gain, 0.0)
-    out_copy.wait()
-    out_full = out_weight.reshape(width, QW)
-
-    def scale_of(value):
-        return lax.rsqrt(jnp.sum(value * value, axis=-1, keepdims=True) * (1.0 / D) + eps_norm)
-
-    for low in range(0, tokens, PART):
-        where = slice(low, low + PART)
-        value = middle[where, :] + dot(mixed_ref[:, where].T, out_full[...], 1, 1)
-        middle[where, :] = value
-        hidden[where, :] = (value * scale_of(value) * gain).astype(BF)
-    flip_blocks(hidden, flipped)
-    split_cores(at, flipped, hidden_own, hidden_give)
     acc_out[...] = jnp.zeros_like(acc_out)
     acc_grad[...] = jnp.zeros_like(acc_grad)
+    for load in loads:
+        load.wait()
+    out_full = out_weight.reshape(width, QW)
 
     def put(ref, column, value):
         where = pl.ds(pl.multiple_of(column, 128), value.shape[1])
@@ -1157,27 +1340,38 @@
         put(total.own, first + CHUNK, dot(hidden_own[...].reshape(width // 2, tokens), upper_grad))
         put(total.own, first + 2 * CHUNK, dot(cot_own[...].reshape(width // 2, tokens), inner))
         for n_start in range(2 * total.slots, FF // SUB, 2):
-            pl.when(n == n_start)(lambda: total.claim(n_start // 2))
+            pl.when(n == n_start)(functools.partial(total.claim, n_start // 2))
         give = total.give.at[lax.rem(chunk, total.slots)]
         put(give, part, dot(hidden_give[...].reshape(width // 2, tokens), gate_grad))
         put(give, part + CHUNK, dot(hidden_give[...].reshape(width // 2, tokens), upper_grad))
         put(give, part + 2 * CHUNK, dot(cot_give[...].reshape(width // 2, tokens), inner))
         for n_end in range(1, FF // SUB, 2):
-            pl.when(n == n_end)(lambda: total.start(n_end // 2))
+            pl.when(n == n_end)(functools.partial(total.start, n_end // 2))
         at_steps(n, events)
         return 0
 
     lax.fori_loop(0, FF // SUB, step, 0)
 
+    real = real_lanes(width, rows, own_rows)
+    gain = jnp.concatenate(
+        [out_weight[s, own_rows : own_rows + 1, :rows].astype(F32) for s in range(shard_count)],
+        axis=1,
+    )
+    gain = jnp.where(real, gain, 0.0)
     term = jnp.zeros((1, width), F32)
-    for low in range(0, tokens, PART):
+    stores = []
+    for n, low in enumerate(range(0, tokens, PART)):
         where = slice(low, low + PART)
         value = middle[where, :]
-        result = value + acc_out[where, :]
-        for s in range(shard_count):
-            out_ref[where, s * own_rows : (s + 1) * own_rows] = result[
-                :, s * rows : s * rows + own_rows
-            ]
+        if n >= 2:
+            stores[n - 2].wait()
+        put_turned(value + acc_out[where, :], results.at[n % 2], rows, own_rows)
+        stores.append(
+            pltpu.make_async_copy(
+                results.at[n % 2], out_hbm.at[:, pl.ds(low, PART)], sems.at[2, n % 2]
+            )
+        )
+        stores[n].start()
         scale = scale_of(value)
         normed = value * scale
         hidden_grad = jnp.where(real, acc_grad[where, :], 0.0)
@@ -1185,49 +1379,268 @@
         upstream = hidden_grad * gain
         mean = jnp.sum(upstream * normed, axis=-1, keepdims=True) * (1.0 / D)
         value = cot[where, :].astype(F32) + scale * (upstream - normed * mean)
-        middle_grad_ref[where, :] = value
+        acc_grad[where, :] = value
         branch = value.astype(BF)
         hidden[where, :] = branch
         gradt_ref[:, where] = dot(branch, out_full[...]).T.astype(BF)
+    store = pltpu.make_async_copy(acc_grad, middle_grad_hbm, sems.at[2, 2])
+    store.start()
+    stores[-2:] += [store]
     for s in range(shard_count):
         gain_term[s] = jnp.broadcast_to(term[:, s * rows : (s + 1) * rows], (8, rows))
     flip_blocks(hidden, flipped)
-    split_cores(at, flipped, hidden_own, hidden_give)
-    place = lax.broadcasted_iota(jnp.int32, (rows, rows), 0)
-    last = len(total.chunks) - 1
-    total.claim(last)
+    for z in range(planes):
+        hidden_own[z] = flipped[2 * z + at.c]
+        hidden_give[z] = flipped[2 * z + 1 - at.c]
+    total.claim(OUT_CHUNK)
     for lhs, core, ref, column in (
-        (hidden_own, at.c, total.own, total.chunks[last][0]),
-        (hidden_give, 1 - at.c, total.give.at[last % total.slots], 0),
+        (hidden_give, 1 - at.c, total.give.at[OUT_CHUNK % total.slots], 0),
+        (hidden_own, at.c, total.own, total.chunks[OUT_CHUNK][0]),
     ):
+        product = dot(lhs[...].reshape(width // 2, tokens), mixed_ref[...], 1, 1)
         for z in range(planes):
-            product = dot(lhs[z], mixed_ref[...], 1, 1)
-            row = gain_term[2 * z + core][:1]
-            ref[z, :, column : column + rows] = jnp.where(
-                place == own_rows, row, product[:, :rows]
-            ).astype(BF)
-            ref[z, :, column + rows : column + QW] = product[:, rows:].astype(BF)
-            end = column + total.chunks[last][1]
-            ref[z, :, column + QW : end] = jnp.zeros((rows, end - column - QW), BF)
-    total.start(last)
-
-
-def rear_kernel(
-    x_ref,
-    cot_ref,
+            row = (own_rows, gain_term[2 * z + core][:1])
+            plane = product[z * rows : (z + 1) * rows]
+            put_gradient(total, OUT_CHUNK, column, ref, z, plane, row)
+        if lhs is hidden_give:
+            total.start(OUT_CHUNK)
+    for store in stores[-3:]:
+        store.wait()
+
+
+def attention_backward(
+    at,
+    total,
+    collect,
+    events,
+    cos_ref,
+    sin_ref,
+    qfeat_ref,
+    lse_ref,
     mixed_ref,
-    rest_ref,
+    gradt_ref,
+    jointt,
     win_hbm,
     feat_hbm,
     qt_hbm,
+    kvf,
+    kt,
+    qa,
+    da,
+    acc,
+    rhs,
+    win_ref,
+    feat_ref,
+    qt_ref,
+    sems,
+):
+    loads = [
+        pltpu.make_async_copy(src, dst, sems.at[i])
+        for i, (src, dst) in enumerate(
+            ((feat_hbm, feat_ref), (win_hbm, win_ref), (qt_hbm, qt_ref))
+        )
+    ]
+    for load in loads:
+        load.start()
+    for load in loads:
+        load.wait()
+    attend_backward_setup(feat_ref, kvf, qa, da, rhs)
+    for n, event in events:
+        if n < 0:
+            event()
+
+    def put_query(row, low, value):
+        cols = slice(low, low + QC)
+        jointt[pl.ds(row, HEAD_DIM), cols] = unrotate(value, cos_ref[:, cols], sin_ref[:, cols])
+
+    def key_head(j, _):
+        attend_backward_keys(j, win_ref, kvf, kt, acc)
+
+        def head(g, _):
+            h = j * GROUP + g
+            attend_backward_head(
+                h,
+                put_query,
+                qt_ref,
+                qfeat_ref,
+                gradt_ref,
+                mixed_ref,
+                lse_ref,
+                kvf,
+                kt,
+                qa,
+                da,
+                acc,
+                rhs,
+            )
+            at_steps(h, events)
+            return 0
+
+        lax.fori_loop(0, GROUP, head, 0)
+        attend_backward_done(j, acc, collect.grads)
+        collect.start(j)
+        pl.when(j > 0)(lambda: collect.one(j - 1))
+        pl.when(j > 1)(lambda: collect.two(j - 2))
+        return 0
+
+    lax.fori_loop(0, KV_HEADS, key_head, 0)
+
+
+def projection_backward(
+    at,
+    total,
+    collect,
+    events,
+    cos_ref,
+    sin_ref,
+    jointt,
+    flipped,
+    x_hbm,
+    middle_grad_hbm,
+    attend_hbm,
+    grad_hbm,
+    attend_ref,
+    inputs,
+    middle_grad,
+    hidden_grad,
+    gain_term,
+    results,
+    sems,
+):
+    shard_count, rows, columns = attend_ref.shape
+    width = shard_count * rows
+    tokens = inputs.shape[0]
+    own_rows = D // shard_count
+    planes = shard_count // 2
+    loads = [
+        pltpu.make_async_copy(src, dst, sems.at[i])
+        for i, (src, dst) in enumerate(
+            ((attend_hbm, attend_ref), (x_hbm, inputs), (middle_grad_hbm, middle_grad))
+        )
+    ]
+    for load in loads:
+        load.start()
+    last = KV_HEADS - 1
+    sides = (
+        (1 - at.c, lambda n: (total.give.at[n % total.slots], 0)),
+        (at.c, lambda n: (total.own, total.chunks[n][0])),
+    )
+
+    def gradients(n, rows_of_joint, gain):
+        total.claim(n)
+        for side, (core, target) in enumerate(sides):
+            ref, column = target(n)
+            for z in range(planes):
+                plane = 2 * z + core
+                product = dot(flipped[plane], jointt[rows_of_joint, :], 1, 1)
+                row = (own_rows, gain_term[plane][:1]) if gain else None
+                put_gradient(total, n, column, ref, z, product, row)
+            if side == 0:
+                total.start(n)
+
+    gradients(QUERY_CHUNK, slice(0, QW), False)
+    collect.one(last)
+    total.zero(QUERY_CHUNK)
+    total.push(QUERY_CHUNK)
+    events[0]()
+    for load in loads:
+        load.wait()
+    weight = attend_ref.reshape(width, columns)
+    for low in range(0, tokens, PART):
+        where = slice(low, low + PART)
+        hidden_grad[where, :] = dot(jointt[:QW, where].T, weight[:, :QW], 1, 1)
+    events[1]()
+    collect.two(last - 1)
+    collect.two(last)
+    for j in range(KV_HEADS):
+        pair = collect.out[j].T
+        low = QW + j * HEAD_DIM
+        jointt[low : low + HEAD_DIM, :] = unrotate(pair[:HALF], cos_ref[...], sin_ref[...])
+        jointt[low + KW : low + KW + HEAD_DIM, :] = pair[HALF:].astype(BF)
+    real = real_lanes(width, rows, own_rows)
+    term = jnp.zeros((1, width), F32)
+    for low in range(0, tokens, PART):
+        where = slice(low, low + PART)
+        value = inputs[where, :].astype(F32)
+        normed = value * scale_of(value)
+        value = hidden_grad[where, :] + dot(jointt[QW:, where].T, weight[:, QW:], 1, 1)
+        value = jnp.where(real, value, 0.0)
+        hidden_grad[where, :] = value
+        term = term + jnp.sum(value * normed, axis=0, keepdims=True)
+    for s in range(shard_count):
+        gain_term[s] = jnp.broadcast_to(term[:, s * rows : (s + 1) * rows], (8, rows))
+    gradients(PAIR_CHUNK, slice(QW, columns), True)
+    total.one(QUERY_CHUNK)
+    total.zero(PAIR_CHUNK)
+    total.push(PAIR_CHUNK)
+    events[2]()
+    total.two(QUERY_CHUNK)
+    gain = jnp.concatenate(
+        [
+            attend_ref[s, own_rows : own_rows + 1, :rows].astype(F32)
+            for s in range(shard_count)
+        ],
+        axis=1,
+    )
+    gain = jnp.where(real, gain, 0.0)
+    stores = []
+    for n, low in enumerate(range(0, tokens, PART)):
+        where = slice(low, low + PART)
+        value = inputs[where, :].astype(F32)
+        scale = scale_of(value)
+        normed = value * scale
+        upstream = hidden_grad[where, :] * gain
+        mean = jnp.sum(upstream * normed, axis=-1, keepdims=True) * (1.0 / D)
+        result = middle_grad[where, :] + scale * (upstream - normed * mean)
+        if n >= 2:
+            stores[n - 2].wait()
+        put_turned(result, results.at[n % 2], rows, own_rows)
+        stores.append(
+            pltpu.make_async_copy(
+                results.at[n % 2], grad_hbm.at[:, pl.ds(low, PART)], sems.at[3 + n % 2]
+            )
+        )
+        stores[n].start()
+    total.one(PAIR_CHUNK)
+    total.three(QUERY_CHUNK)
+    total.two(PAIR_CHUNK)
+    total.four(QUERY_CHUNK)
+    total.three(PAIR_CHUNK)
+    total.five(QUERY_CHUNK)
+    total.four(PAIR_CHUNK)
+    total.five(PAIR_CHUNK)
+    for j in range(KV_HEADS):
+        collect.sent(j)
+    total.sent()
+    for store in stores[-2:]:
+        store.wait()
+
+
+def rear_kernel(
+    mixed_ref,
+    lse_ref,
     qfeat_ref,
-    lse_ref,
-    out_ref,
-    middle_grad_ref,
-    dq_ref,
-    pairs_ref,
+    cos_ref,
+    sin_ref,
+    rest_ref,
+    attend_hbm,
+    win_hbm,
+    feat_hbm,
+    qt_hbm,
+    flipped_hbm,
+    x_hbm,
+    cot_hbm,
+    cott_hbm,
+    middle_hbm,
+    hidden_hbm,
+    hiddent_hbm,
     sum_ref,
+    out_hbm,
+    grad_hbm,
+    middle_grad_hbm,
     gradt_ref,
+    jointt,
+    pairs,
     ra,
     rb,
     r2,
@@ -1237,13 +1650,13 @@
     *reduce_scratch,
 ):
     at = Place()
-    tokens = x_ref.shape[0]
+    tokens = x_hbm.shape[0]
     shard_count, rows, _ = rest_ref.shape
     width = shard_count * rows
-    kv_heads, _, lanes = pairs_ref.shape
+    lanes = pairs.shape[2]
     keys = feat_hbm.shape[0]
     greet(at, True)
-    total = Reduce(at, rear_chunks(), sum_ref, *reduce_scratch)
+    total = Reduce(at, sum_chunks(), sum_ref, *reduce_scratch)
 
     def run(*names):
         def event():
@@ -1252,42 +1665,40 @@
 
         return event
 
+    def round_of(t):
+        due = [("one", t), ("push", t + 1), ("two", t - 1), ("three", t - 2), ("four", t - 3)]
+        return [(name, n) for name, n in due + [("five", t - 4)] if 0 <= n <= OUT_CHUNK]
+
     forward_events = [
         (2, run(("zero", 0), ("push", 0))),
         (4, run(("zero", 1))),
-        (5, run(("one", 0), ("push", 1))),
-        (6, run(("zero", 2), ("two", 0))),
+        (6, run(("zero", 2), *round_of(0))),
         (8, run(("zero", 3))),
-        (9, run(("one", 1), ("push", 2), ("three", 0))),
     ]
     backward_events = [
-        (0, run(("zero", 4), ("two", 1), ("four", 0))),
-        (2, run(("one", 2), ("push", 3), ("five", 0))),
-        (3, run(("zero", 5), ("two", 2), ("three", 1))),
-        (4, run(("four", 1))),
-        (5, run(("three", 2))),
-        (6, run(("one", 3), ("push", 4), ("five", 1), ("four", 2))),
-        (7, run(("two", 3))),
-        (9, run(("three", 3), ("five", 2))),
-        (10, run(("one", 4), ("push", 5), ("four", 3))),
-        (11, run(("two", 4))),
-        (12, run(("one", 5), ("three", 4), ("five", 3))),
-        (13, run(("two", 5), ("four", 4))),
-        (14, run(("three", 5), ("five", 4))),
+        (-1, run(("zero", 4), *round_of(1))),
+        (3, run(("zero", 5), *round_of(2))),
+        (6, run(*round_of(3))),
+        (9, run(*round_of(4))),
+        (12, run(*round_of(5))),
     ]
+    last_events = [run(*round_of(6)), run(*round_of(7), *round_of(8)), run(*round_of(9))]
 
     pl.run_scoped(
         functools.partial(
             feed_forward,
             at,
             total,
-            x_ref,
-            cot_ref,
             mixed_ref,
+            gradt_ref,
+            middle_hbm,
+            hidden_hbm,
+            hiddent_hbm,
+            cot_hbm,
+            cott_hbm,
             rest_ref,
-            out_ref,
-            middle_grad_ref,
-            gradt_ref,
+            out_hbm,
+            middle_grad_hbm,
             forward_events,
         ),
         VMEM((tokens, width), BF),
@@ -1295,241 +1706,109 @@
         VMEM((tokens, width), F32),
         VMEM((tokens, width), F32),
         VMEM((tokens, width), F32),
-        VMEM((shard_count, rows, tokens), BF),
         VMEM((shard_count // 2, rows, tokens), BF),
         VMEM((shard_count // 2, rows, tokens), BF),
         VMEM((shard_count // 2, rows, tokens), BF),
         VMEM((shard_count // 2, rows, tokens), BF),
+        VMEM((shard_count, rows, tokens), BF),
         VMEM((shard_count, rows, QW), BF),
-        VMEM((shard_count, rows - D // shard_count // 16 * 16, 128), BF),
         VMEM((shard_count, 8, rows), F32),
         VMEM((2, 3, shard_count, rows, SUB), BF),
+        VMEM((2, D, PART), F32),
         DMA((3, 3)),
+        DMA((4 + 2 * shard_count,)),
     )
 
-    def attention(kvf, kt, qa, da, acc, rhs, grads, t2, t1, win_ref, feat_ref, qt_ref, sems):
-        loads = [
-            pltpu.make_async_copy(src, dst, sems.at[i])
-            for i, (src, dst) in enumerate(
-                ((feat_hbm, feat_ref), (win_hbm, win_ref), (qt_hbm, qt_ref))
-            )
-        ]
-        for load in loads:
-            load.start()
-        for load in loads:
-            load.wait()
-        collect = Collect(
-            at, grads, pairs_ref, ra, rb, r2, r1, t2, t1, collect_send, collect_recv
+    def attention(grads, t2, t1, flipped, flipped_sem):
+        collect = Collect(at, grads, pairs, ra, rb, r2, r1, t2, t1, collect_send, collect_recv)
+        load = pltpu.make_async_copy(flipped_hbm, flipped, flipped_sem)
+        load.start()
+        pl.run_scoped(
+            functools.partial(
+                attention_backward,
+                at,
+                total,
+                collect,
+                backward_events,
+                cos_ref,
+                sin_ref,
+                qfeat_ref,
+                lse_ref,
+                mixed_ref,
+                gradt_ref,
+                jointt,
+                win_hbm,
+                feat_hbm,
+                qt_hbm,
+            ),
+            *attend_backward_scratch(keys, lanes, tokens),
+            VMEM(win_hbm.shape, BF),
+            VMEM(feat_hbm.shape, BF),
+            VMEM(qt_hbm.shape, BF),
+            DMA((3,)),
         )
-        attend_backward_setup(feat_ref, kvf, qa, da, rhs)
-
-        def key_head(j, _):
-            attend_backward_keys(j, win_ref, kvf, kt, acc)
-
-            def head(g, _):
-                h = j * GROUP + g
-                attend_backward_head(
-                    h,
-                    qt_ref,
-                    qfeat_ref,
-                    gradt_ref,
-                    mixed_ref,
-                    lse_ref,
-                    dq_ref,
-                    kvf,
-                    kt,
-                    qa,
-                    da,
-                    acc,
-                    rhs,
-                )
-                at_steps(h, backward_events)
-                return 0
-
-            lax.fori_loop(0, GROUP, head, 0)
-            attend_backward_done(j, acc, grads)
-            collect.start(j)
-            pl.when(j > 0)(lambda: collect.one(j - 1))
-            pl.when(j > 1)(lambda: collect.two(j - 2))
-            pl.when(j > 2)(lambda: collect.three(j - 3))
-            return 0
-
-        lax.fori_loop(0, kv_heads, key_head, 0)
-        collect.one(kv_heads - 1)
-        collect.two(kv_heads - 2)
-        total.four(5)
-        collect.two(kv_heads - 1)
-        for j in range(kv_heads - 3, kv_heads):
-            collect.three(j)
-        total.five(5)
-        for j in range(kv_heads):
-            collect.sent(j)
-        total.sent()
+        load.wait()
+        pl.run_scoped(
+            functools.partial(
+                projection_backward,
+                at,
+                total,
+                collect,
+                last_events,
+                cos_ref,
+                sin_ref,
+                jointt,
+                flipped,
+                x_hbm,
+                middle_grad_hbm,
+                attend_hbm,
+                grad_hbm,
+            ),
+            VMEM(attend_hbm.shape, BF),
+            VMEM((tokens, width), BF),
+            VMEM((tokens, width), F32),
+            VMEM((tokens, width), F32),
+            VMEM((shard_count, 8, rows), F32),
+            VMEM((2, D, PART), F32),
+            DMA((5,)),
+        )
 
     pl.run_scoped(
         attention,
-        *attend_backward_scratch(keys, lanes, tokens),
         VMEM(win_hbm.shape, BF),
-        VMEM(pairs_ref.shape, BF),
-        VMEM(pairs_ref.shape, BF),
-        VMEM(win_hbm.shape, BF),
-        VMEM(feat_hbm.shape, BF),
-        VMEM(qt_hbm.shape, BF),
-        DMA((3,)),
+        VMEM(pairs.shape, BF),
+        VMEM(pairs.shape, BF),
+        VMEM(flipped_hbm.shape, BF),
+        DMA,
     )
 
 
-def rear(x, cotangent, mixed, rest, window, feat, qt, qfeat, lse, number):
-    blocks, kv_heads, tokens, lanes = window.shape
+def rear(in_hbm, in_vmem, number):
+    rest, attend, window, _, qt, _, x = in_hbm[:7]
+    _, kv_heads, tokens, lanes = window.shape
     shard_count, rows, _ = rest.shape
-    columns = sum(width for _, width in rear_chunks())
+    columns = sum(width for _, width in sum_chunks())
     pairs = (kv_heads, tokens, lanes)
     return pl.pallas_call(
         rear_kernel,
         out_shape=(
-            jax.ShapeDtypeStruct(x.shape, F32),
+            jax.ShapeDtypeStruct((rows, columns), BF),
+            jax.ShapeDtypeStruct((D, tokens), F32),
+            jax.ShapeDtypeStruct((D, tokens), F32),
             jax.ShapeDtypeStruct((tokens, shard_count * rows), F32),
-            jax.ShapeDtypeStruct(qt.shape, F32),
-            jax.ShapeDtypeStruct(pairs, F32),
-            jax.ShapeDtypeStruct((rows, columns), BF),
         ),
-        in_specs=[pl.BlockSpec(memory_space=VMEM)] * 3
-        + [pl.BlockSpec(memory_space=ANY)] * 4
-        + [pl.BlockSpec(memory_space=VMEM)] * 2,
-        out_specs=(pl.BlockSpec(memory_space=VMEM),) * 5,
-        scratch_shapes=[VMEM(qt.shape, BF)]
+        in_specs=[pl.BlockSpec(memory_space=VMEM)] * len(in_vmem)
+        + [pl.BlockSpec(memory_space=ANY)] * len(in_hbm),
+        out_specs=(pl.BlockSpec(memory_space=VMEM),) + (pl.BlockSpec(memory_space=ANY),) * 3,
+        scratch_shapes=[VMEM(qt.shape, BF), VMEM((JW, tokens), BF), VMEM(pairs, F32)]
         + [VMEM(pairs, BF)] * 4
         + [DMA((4, kv_heads)), DMA((4, kv_heads))]
-        + Reduce.scratch(rows, rear_chunks(), 2),
+        + Reduce.scratch(rows, sum_chunks(), 2),
         compiler_params=pltpu.CompilerParams(
             collective_id=number, has_side_effects=True, vmem_limit_bytes=BIG_VMEM
         ),
         name="rear",
-    )(x, cotangent, mixed, rest, window, feat, qt, qfeat, lse)
-
-
-def tail_kernel(
-    x_ref,
-    middle_grad_ref,
-    dq_ref,
-    pairs_ref,
-    cos_ref,
-    sin_ref,
-    attend_ref,
-    grad_ref,
-    sum_ref,
-    inputs,
-    hidden,
-    jointt,
-    flipped,
-    hidden_own,
-    hidden_give,
-    gain_term,
-    *reduce_scratch,
-):
-    at = Place()
-    shard_count, rows, columns = attend_ref.shape
-    width = shard_count * rows
-    tokens = x_ref.shape[0]
-    own_rows = D // shard_count
-    greet(at, True)
-    total = Reduce(at, [(0, columns)], sum_ref, *reduce_scratch)
-    pad_features(x_ref, inputs, own_rows, rows)
-    lane = lax.broadcasted_iota(jnp.int32, (1, width), 1)
-    real = lax.rem(lane, rows) < own_rows
-    gain = jnp.concatenate(
-        [
-            attend_ref[s, own_rows : own_rows + 1, :rows].astype(F32)
-            for s in range(shard_count)
-        ],
-        axis=1,
-    )
-    gain = jnp.where(real, gain, 0.0)
-
-    def unrotate(head):
-        half = HEAD_DIM // 2
-        front, back = head[:half], head[half:]
-        cosine, sine = cos_ref[...], sin_ref[...]
-        return jnp.concatenate(
-            [front * cosine + back * sine, back * cosine - front * sine], axis=0
-        ).astype(BF)
-
-    for h in range(HEADS):
-        where = slice(h * HEAD_DIM, (h + 1) * HEAD_DIM)
-        jointt[where, :] = unrotate(dq_ref[where, :])
-    for j in range(KV_HEADS):
-        pair = pairs_ref[j].T
-        low = QW + j * HEAD_DIM
-        jointt[low : low + HEAD_DIM, :] = unrotate(pair[:HALF])
-        jointt[low + KW : low + KW + HEAD_DIM, :] = pair[HALF:].astype(BF)
-
-    weight = attend_ref.reshape(width, columns)
-    term = jnp.zeros((1, width), F32)
-    for low in range(0, tokens, PART):
-        where = slice(low, low + PART)
-        value = inputs[where, :]
-        scale = lax.rsqrt(jnp.sum(value * value, axis=-1, keepdims=True) * (1.0 / D) + eps_norm)
-        normed = value * scale
-        hidden[where, :] = (normed * gain).astype(BF)
-        hidden_grad = dot(jointt[:, where].T, weight[...], 1, 1)
-        hidden_grad = jnp.where(real, hidden_grad, 0.0)
-        term = term + jnp.sum(hidden_grad * normed, axis=0, keepdims=True)
-        upstream = hidden_grad * gain
-        mean = jnp.sum(upstream * normed, axis=-1, keepdims=True) * (1.0 / D)
-        result = middle_grad_ref[where, :] + scale * (upstream - normed * mean)
-        for s in range(shard_count):
-            grad_ref[where, s * own_rows : (s + 1) * own_rows] = result[
-                :, s * rows : s * rows + own_rows
-            ]
-    for s in range(shard_count):
-        gain_term[s] = jnp.broadcast_to(term[:, s * rows : (s + 1) * rows], (8, rows))
-    flip_blocks(hidden, flipped)
-    split_cores(at, flipped, hidden_own, hidden_give)
-    place = lax.broadcasted_iota(jnp.int32, (rows, rows), 0)
-    for lhs, core, ref in (
-        (hidden_give, 1 - at.c, total.give.at[0]),
-        (hidden_own, at.c, total.own),
-    ):
-        for z in range(lhs.shape[0]):
-            product = dot(lhs[z], jointt[...], 1, 1)
-            row = gain_term[2 * z + core][:1]
-            ref[z, :, :rows] = jnp.where(place == own_rows, row, product[:, :rows]).astype(BF)
-            ref[z, :, rows:] = product[:, rows:].astype(BF)
-        if ref is not total.own:
-            total.start(0)
-    for step in (total.zero, total.push, total.one, total.two, total.three):
-        step(0)
-    total.four(0)
-    total.five(0)
-    total.sent()
-
-
-def tail(x, middle_grad, dq, pairs, cosine, sine, attend_planes, number):
-    tokens, width = middle_grad.shape
-    shard_count, rows, columns = attend_planes.shape
-    return pl.pallas_call(
-        tail_kernel,
-        out_shape=(
-            jax.ShapeDtypeStruct(x.shape, F32),
-            jax.ShapeDtypeStruct((rows, columns), BF),
-        ),
-        in_specs=[pl.BlockSpec(memory_space=VMEM)] * 7,
-        out_specs=(pl.BlockSpec(memory_space=VMEM),) * 2,
-        scratch_shapes=[
-            VMEM((tokens, width), F32),
-            VMEM((tokens, width), BF),
-            VMEM((columns, tokens), BF),
-            VMEM((shard_count, rows, tokens), BF),
-            VMEM((shard_count // 2, rows, tokens), BF),
-            VMEM((shard_count // 2, rows, tokens), BF),
-            VMEM((shard_count, 8, rows), F32),
-        ]
-        + Reduce.scratch(rows, [(0, columns)], 1),
-        compiler_params=pltpu.CompilerParams(
-            collective_id=number, has_side_effects=True, vmem_limit_bytes=BIG_VMEM
-        ),
-        name="tail",
-    )(x, middle_grad, dq, pairs, cosine, sine, attend_planes)
+    )(*in_vmem, *in_hbm)
 
 
 def adam_parts(old_weight, gradient, first, second, decay_factor):
@@ -1542,9 +1821,11 @@
 
 
 def adam_kernel(grad_scale, own_rows, *refs):
-    attend_sum, rest_sum, attend_planes, rest_planes = refs[:4]
-    states, results = refs[4:12], refs[12:28]
-    buffers, weights, in_sems, out_sems = refs[28:44], refs[44:46], refs[46], refs[47]
+    sums, attend_planes, rest_planes = refs[:3]
+    states, passed_in, results, passed_out = refs[3:11], refs[11:13], refs[13:29], refs[29:31]
+    buffers, weights, staged = refs[31:47], refs[47:49], refs[49:51]
+    in_sems, out_sems = refs[51], refs[52]
+    chunks = sum_chunks()
     shard = lax.axis_index("shard")
     loads = [
         pltpu.make_async_copy(attend_planes.at[shard], weights[0], in_sems.at[8]),
@@ -1558,6 +1839,8 @@
                     states[2 * n + i], buffers[4 * n + 1 + i], in_sems.at[2 * n + i]
                 )
             )
+    for i in range(2):
+        loads.append(pltpu.make_async_copy(passed_in[i], staged[i], in_sems.at[10 + i]))
     for load in loads:
         load.start()
     loads[0].wait()
@@ -1584,61 +1867,64 @@
         loads[2 + 2 * place].wait()
         loads[3 + 2 * place].wait()
         if n == 0:
-            columns = weights[0].shape[1]
-            for low in range(0, columns, CHUNK):
-                cols = slice(low, min(low + CHUNK, columns))
+            for chunk, first, count in ((QUERY_CHUNK, 0, QW), (PAIR_CHUNK, QW, 2 * KW)):
+                low, cols = chunks[chunk][0], slice(first, first + count)
                 update(
                     0,
                     (everything, cols),
-                    attend_sum[:own_rows, cols],
+                    sums[:own_rows, low : low + count],
                     weights[0][:own_rows, cols],
                     False,
                 )
         elif n == 1:
+            low = chunks[OUT_CHUNK][0]
             cols = slice(3 * FF, 3 * FF + QW)
-            update(1, (everything, everything), rest_sum[:, cols], weights[1][:, cols], True)
+            update(
+                1, (everything, everything), sums[:, low : low + QW], weights[1][:, cols], True
+            )
         else:
             for c in range(FF // CHUNK):
                 for part in (0, 1) if n == 2 else (2,):
                     low = 3 * CHUNK * c + CHUNK * part
                     first = part * FF + CHUNK * c
-                    rows = slice(None) if n == 3 else slice(0, own_rows)
-                    total = rest_sum[rows, low : low + CHUNK]
-                    weight = weights[1][rows, first : first + CHUNK]
-                    if n == 3:
-                        where = (slice(c * CHUNK, (c + 1) * CHUNK), everything)
-                    else:
-                        where = (everything, slice(first, first + CHUNK))
-                    update(n, where, total, weight, n == 3)
+                    total = sums[:own_rows, low : low + CHUNK]
+                    weight = weights[1][:own_rows, first : first + CHUNK]
+                    column = first if n == 2 else first - 2 * FF
+                    cols = slice(column, column + CHUNK)
+                    update(n, (everything, cols), total, weight, False)
         for i in range(4):
             store = pltpu.make_async_copy(
                 buffers[4 * n + i], results[4 * n + i], out_sems.at[4 * n + i]
             )
             store.start()
             stores.append(store)
+        if place < 2:
+            loads[10 + place].wait()
+            store = pltpu.make_async_copy(
+                staged[place], passed_out[place], out_sems.at[16 + place]
+            )
+            store.start()
+            stores.append(store)
     for store in stores:
         store.wait()
 
 
-def adam(grad_scale, own_rows, attend_sum, rest_sum, attend_planes, rest_planes, states):
+def adam(grad_scale, own_rows, sums, attend_planes, rest_planes, states, passed):
     flat = [array for pair in states for array in pair]
     shapes = [pair[0].shape for pair in states]
     return pl.pallas_call(
         functools.partial(adam_kernel, grad_scale, own_rows),
-        out_shape=tuple(jax.ShapeDtypeStruct(shape, F32) for shape in shapes for _ in range(4)),
-        in_specs=[pl.BlockSpec(memory_space=VMEM)] * 2 + [pl.BlockSpec(memory_space=ANY)] * 10,
-        out_specs=(pl.BlockSpec(memory_space=ANY),) * 16,
+        out_shape=tuple(jax.ShapeDtypeStruct(shape, F32) for shape in shapes for _ in range(4))
+        + tuple(jax.ShapeDtypeStruct(array.shape, array.dtype) for array in passed),
+        in_specs=[pl.BlockSpec(memory_space=VMEM)] + [pl.BlockSpec(memory_space=ANY)] * 12,
+        out_specs=(pl.BlockSpec(memory_space=ANY),) * 18,
         scratch_shapes=[VMEM(shape, F32) for shape in shapes for _ in range(4)]
         + [VMEM(attend_planes.shape[1:], BF), VMEM(rest_planes.shape[1:], BF)]
-        + [DMA((10,)), DMA((16,))],
+        + [VMEM(array.shape, F32) for array in passed]
+        + [DMA((12,)), DMA((18,))],
         compiler_params=pltpu.CompilerParams(vmem_limit_bytes=BIG_VMEM),
         name="adam",
-    )(attend_sum, rest_sum, attend_planes, rest_planes, *flat)
-
-
-def reduce_rows(parts):
-    own = lax.psum_scatter(parts, "shard", scatter_dimension=0)
-    return lax.psum(own, "rep")
+    )(sums, attend_planes, rest_planes, *flat, *passed)
 
 
 def spread_pairs(pairs, reach):
@@ -1727,12 +2013,14 @@
         return tensor.reshape(tokens, shard_count, rows)[:, :, :own_rows].reshape(tokens, D)
 
     def with_gain(weight, gain):
+        if gain is None:
+            return jnp.pad(weight, ((0, rows - own_rows), (0, 0)))
         tail = jnp.pad(gain[None, :], ((0, rows - own_rows - 1), (0, weight.shape[1] - own_rows)))
         return jnp.concatenate([weight, tail], axis=0)
 
-    def gain_of(planes):
+    def gain_of(planes, column):
         return jnp.pad(
-            planes[:, own_rows, :own_rows], ((0, 0), (0, rows - own_rows))
+            planes[:, own_rows, column : column + own_rows], ((0, 0), (0, rows - own_rows))
         ).reshape(1, width).astype(F32)
 
     def add_gain(planes, term, column):
@@ -1743,54 +2031,58 @@
         parts = jnp.concatenate([expand, shrink], axis=1).reshape(-1, 3, FF // CHUNK, CHUNK)
         return parts.transpose(0, 2, 1, 3).reshape(-1, 3 * FF)
 
-    first_row = lax.axis_index("shard") * tokens
-    local_index = first_row + jnp.arange(tokens, dtype=jnp.int32)
-    key_index = first_row - reach * tokens + jnp.arange((reach + 1) * tokens, dtype=jnp.int32)
-    ends = jnp.cumsum(lengths[0], dtype=jnp.int32)
-    starts = ends - lengths[0]
-    seq_count = lengths.shape[1]
-    in_key = (key_index[:, None] >= starts[None, :]) & (key_index[:, None] < ends[None, :])
-    in_query = (local_index[None, :] >= starts[:, None]) & (local_index[None, :] < ends[:, None])
-    lanes = 2 * HEAD_DIM
-    feat = jnp.concatenate(
-        [
-            in_key.astype(BF),
-            (key_index < 0).astype(BF)[:, None],
-            jnp.zeros((key_index.shape[0], ONES - seq_count - 1), BF),
-            jnp.ones((key_index.shape[0], lanes - ONES), BF),
-        ],
-        axis=1,
-    )
-    qfeat = jnp.concatenate(
-        [
-            jnp.where(in_query, 0.0, NEG).astype(BF),
-            jnp.full((1, tokens), NEG, BF),
-            jnp.zeros((lanes - seq_count - 1, tokens), BF),
-        ],
-        axis=0,
-    )
-    start_index = jnp.sum(in_query * starts[:, None], axis=0, dtype=jnp.int32)
-    cosine_table, sine_table = angles(local_index - start_index)
-
-    attend_own = with_gain(attend_weight, attend_gain)
-    rest_own = with_gain(
-        jnp.concatenate([expand_weight, shrink_weight.T, output_weight.T], axis=1), expand_gain
-    )
     if direct:
-        tables = (cosine_table[:, 0].T, sine_table[:, 0].T)
-        attend_planes, rest_planes, window, qt, mixedt, lse = front(
-            padded(block_input), *tables, feat, qfeat, attend_own, rest_own, shard_count, 0
+        weights = (
+            attend_gain[None, :],
+            attend_weight,
+            expand_gain[None, :],
+            expand_weight,
+            shrink_weight.T,
+            output_weight,
         )
-        block_output, middle_grad, dqt, own_pairs, rest_sum = rear(
-            block_input, block_cotangent, mixedt, rest_planes, window, feat, qt, qfeat, lse, 1
+        made = front(lengths, block_input.T, block_cotangent.T, weights, shard_count, 0)
+        rest_planes, attend_planes = made[:2]
+        sums, block_output, input_gradient, _ = rear(made[:12], made[12:], 1)
+    else:
+        first_row = lax.axis_index("shard") * tokens
+        local_index = first_row + jnp.arange(tokens, dtype=jnp.int32)
+        key_index = first_row - reach * tokens + jnp.arange((reach + 1) * tokens, dtype=jnp.int32)
+        ends = jnp.cumsum(lengths[0], dtype=jnp.int32)
+        starts = ends - lengths[0]
+        seq_count = lengths.shape[1]
+        in_key = (key_index[:, None] >= starts[None, :]) & (key_index[:, None] < ends[None, :])
+        in_query = (local_index[None, :] >= starts[:, None]) & (local_index[None, :] < ends[:, None])
+        lanes = 2 * HEAD_DIM
+        feat = jnp.concatenate(
+            [
+                in_key.astype(BF),
+                (key_index < 0).astype(BF)[:, None],
+                jnp.zeros((key_index.shape[0], ONES - seq_count - 1), BF),
+                jnp.ones((key_index.shape[0], lanes - ONES), BF),
+            ],
+            axis=1,
         )
-        input_gradient, attend_sum = tail(
-            block_input, middle_grad, dqt, own_pairs, *tables, attend_planes, 2
+        qfeat = jnp.concatenate(
+            [
+                jnp.where(in_query, 0.0, NEG).astype(BF),
+                jnp.full((1, tokens), NEG, BF),
+                jnp.zeros((lanes - seq_count - 1, tokens), BF),
+            ],
+            axis=0,
         )
-    else:
+        start_index = jnp.sum(in_query * starts[:, None], axis=0, dtype=jnp.int32)
+        cosine_table, sine_table = angles(local_index - start_index)
+        attend_own = with_gain(attend_weight, attend_gain)
+        rest_own = jnp.concatenate(
+            [
+                with_gain(jnp.concatenate([expand_weight, shrink_weight.T], axis=1), None),
+                with_gain(output_weight.T, expand_gain),
+            ],
+            axis=1,
+        )
         attend_planes = lax.all_gather(attend_own, "shard", axis=0)
         rest_planes = lax.all_gather(rest_own, "shard", axis=0)
-        gain_one, gain_two = gain_of(attend_planes), gain_of(rest_planes)
+        gain_one, gain_two = gain_of(attend_planes, 0), gain_of(rest_planes, 3 * FF)
         joint_weight = attend_planes.reshape(width, JW)
         rest = rest_planes.reshape(width, rest_own.shape[1])
         expand_full, shrink_full, out_full = rest[:, : 2 * FF], rest[:, 2 * FF : 3 * FF], rest[:, 3 * FF :]
@@ -1810,7 +2102,7 @@
         qt = queries.astype(BF).reshape(tokens, QW).T
         window = spread_pairs(pairs, reach)
         mixedt, lse = attend_forward(window, feat, qt, qfeat)
-        middle = inputs + dot(mixedt, out_full, 0, 1)
+        middle = inputs + jnp.where(real, dot(mixedt, out_full, 0, 1), 0.0)
         scale_two = lax.rsqrt(jnp.sum(middle * middle, axis=-1, keepdims=True) * (1.0 / D) + eps_norm)
         normed_two = middle * scale_two
         hidden_two = (normed_two * gain_two).astype(BF)
@@ -1837,13 +2129,9 @@
         branch_grad = middle_grad.astype(BF)
         output_term = dot(branch_grad, mixedt, 0, 1)
         gradt = dot(out_full, branch_grad, 0, 1).astype(BF)
-        rest_term = jnp.concatenate(
-            [in_chunks(expand_term, shrink_term), output_term], axis=1
-        ).astype(BF).reshape(shard_count, rows, rest_own.shape[1])
-        rest_sum = reduce_rows(add_gain(rest_term, gain_two_term, 3 * FF))
         dqt, dwindow = attend_backward(window, feat, qt, qfeat, gradt, mixedt, lse)
         own_pairs = collect_pairs(dwindow, reach)
-        block_output = unpadded(block_output)
+        block_output = unpadded(block_output).T
         own_pairs = own_pairs.transpose(1, 0, 2)
         dq = dqt.T.reshape(tokens, HEADS, HEAD_DIM)
         query_raw = rotate(dq, cosine_table, -sine_table).reshape(tokens, QW)
@@ -1854,24 +2142,38 @@
         hidden_one_grad = jnp.where(real, dot(joint_grad, joint_weight, 1, 1), 0.0)
         gain_one_term = jnp.sum(hidden_one_grad * normed_one, axis=0)
         input_gradient = middle_grad + norm_back(hidden_one_grad * gain_one, normed_one, scale_one)
-        attend_sum = reduce_rows(
-            add_gain(joint_term.reshape(shard_count, rows, JW), gain_one_term, 0)
-        )
-        input_gradient = unpadded(input_gradient)
+        to_lanes = ((0, 0), (0, up_to_lanes(QW) - QW))
+        terms = jnp.concatenate(
+            [
+                in_chunks(expand_term, shrink_term).astype(BF),
+                jnp.pad(output_term.astype(BF), to_lanes),
+                jnp.pad(joint_term[:, :QW], to_lanes),
+                joint_term[:, QW:],
+            ],
+            axis=1,
+        ).reshape(shard_count, rows, -1)
+        terms = add_gain(terms, gain_two_term, sum_chunks()[OUT_CHUNK][0])
+        terms = add_gain(terms, gain_one_term, sum_chunks()[PAIR_CHUNK][0])
+        sums = lax.psum(lax.psum_scatter(terms, "shard", scatter_dimension=0), "rep")
+        input_gradient = unpadded(input_gradient).T
 
     grad_scale = grad_factor * token_count ** (-0.5)
+    def gain_sum(chunk):
+        first = sum_chunks()[chunk][0]
+        return sums[own_rows, first : first + own_rows]
+
     first_gain, second_gain = (
         adam_step(weight, total.astype(F32) * grad_scale, first, second, 0.0)
         for weight, total, first, second in (
             (
                 attend_gain,
-                attend_sum[own_rows, :own_rows],
+                gain_sum(PAIR_CHUNK),
                 attend_gain_first,
                 attend_gain_second,
             ),
             (
                 expand_gain,
-                rest_sum[own_rows, 3 * FF : 3 * FF + own_rows],
+                gain_sum(OUT_CHUNK),
                 expand_gain_first,
                 expand_gain_second,
             ),
@@ -1880,20 +2182,22 @@
     matrices = adam(
         grad_scale,
         own_rows,
-        attend_sum,
-        rest_sum,
+        sums,
         attend_planes,
         rest_planes,
         (
             (attend_weight_first, attend_weight_second),
             (output_weight_first, output_weight_second),
             (expand_weight_first, expand_weight_second),
-            (shrink_weight_first, shrink_weight_second),
+            (shrink_weight_first.T, shrink_weight_second.T),
         ),
+        (block_output, input_gradient),
     )
     first_joint, first_output, second_expand, second_shrink = (
         matrices[4 * n : 4 * n + 4] for n in range(4)
     )
+    second_shrink = [result.T for result in second_shrink]
+    block_output, input_gradient = (result.T for result in matrices[16:])
     steps = (first_gain, first_joint, first_output, second_gain, second_expand, second_shrink)
     return (block_output, input_gradient, *[step[i] for i in range(4) for step in steps])
 

time: 378 us -> 328 us (0.87)
  local copies, waits for them, and re-layouts: 24.4 us -> 0.04 us
  Pallas kernels: 338 us -> 321 us
  other arithmetic: 8.97 us -> 1.23 us
    unnamed x46 -> x12, local copies, waits for them, and re-layouts: 23.1 us -> 0.04 us
    pallas_call x3 -> x2, Pallas kernels: 324 us -> 305 us  [the longest x1 193 us: rear(): pl.pallas_call(rear_kernel, out_shape=(jax.ShapeDtypeStruct((rows, column...]
    concatenate x4 -> x0, other arithmetic: 4.88 us -> none  [the longest x2 2.84 us: with_gain(): return jnp.concatenate([weight, tail], axis=0)]
where the time goes in v4:
time: 328 us; the launch traced here: 323 us
  Pallas kernels  321 us (98%)
    pallas_call x1, Pallas kernels, rear(): pl.pallas_call(rear_kernel, out_shape=(jax.ShapeDtypeStruct((rows, column...  193 us
    pallas_call x1, Pallas kernels, front(): pl.pallas_call(front_kernel, out_shape=in_hbm + in_vmem, in_specs=[pl.Blo...  112 us
    pallas_call x1, Pallas kernels, adam(): pl.pallas_call(functools.partial(adam_kernel, grad_scale, own_rows), out_...  15.6 us

profile of v4, /device:TPU:0, one launch (start us, length us, event | category | flops | bytes accessed | tf_op | source)
XLA Modules:
  0.0 323.1 jit_solution(7960488073621747142)
XLA Ops:
  0.7 112.4 %front.1 = (bf16[8,128,8640]{2,1,0:T(8,128)(2,1)}, bf16[8,128,1600]{2,1,0:T(8,128)(2,1)}, bf16[5,5,512,128]{3,2,1,0:T(8,128)(2,1)}, bf16[2560,128]{1,0:T(8,128)(...) custom-call(s32[1,3]{1,0:T(1,128)} %lengths_ref.1, ...), custom_call_target="tpu_custom_call" | custom-call | tf_op jit(solution)/shard_map/front/pallas_call | solution.py:1157
  113.0 192.7 %rear.1 = (bf16[128,10368]{1,0:T(8,128)(2,1)}, f32[960,512]{1,0:T(8,128)}, f32[960,512]{1,0:T(8,128)}, f32[512,1024]{1,0:T(8,128)}) custom-call(bf16[960,512]{1,0:T(8,128)(2,1)} %get-tuple-element.64.mixed_ref, f32[15,1,512]{2,1,0:T(1,128)} %get-tuple-element.65.lse_ref, bf16[128,512]{1,0:T(8,128)(2,1)} %get-tuple-element.66.qfeat_ref, ...), custom_call_target="tpu_custom_call" | custom-call | tf_op jit(solution)/shard_map/rear/pallas_call | solution.py:1792
  305.7 0.0 copy-start
  305.7 0.0 copy-start.1
  305.7 0.0 copy-start.2
  305.7 0.0 copy-start.3
  305.8 0.0 copy-start.4
  305.8 0.0 copy-start.5
  305.8 15.6 %adam.1 = (f32[120,1600]{1,0:T(8,128)}, f32[120,1600]{1,0:T(8,128)}, f32[120,1600]{1,0:T(8,128)}, f32[120,1600]{1,0:T(8,128)}, f32[960,120]{1,0:T(8,128)}, /*ind...) custom-call(bf16[128,10368]{1,0:T(8,128)(2,1)} %get-tuple-element.81, ...), custom_call_target="tpu_custom_call" | custom-call | tf_op jit(solution)/shard_map/adam/pallas_call | solution.py:1915
  321.3 0.0 copy-done
  321.4 0.0 copy-done.1
  321.4 0.0 copy-done.2
  321.4 0.0 copy-done.3
  321.4 0.0 copy-done.4
  321.4 0.0 copy-done.5
  321.4 1.2 add_multiply_fusion
Async XLA Ops:
  305.7 15.6 %copy-start = (bf16[120]{0:T(256)(128)(2,1)S(1)}, bf16[120]{0:T(256)(128)(2,1)}, u32[]{:S(2)}) copy-start(bf16[120]{0:T(256)(128)(2,1)} %param.25) | copy-start | bytes 724
  305.7 15.6 %copy-start.1 = (bf16[120]{0:T(256)(128)(2,1)S(1)}, bf16[120]{0:T(256)(128)(2,1)}, u32[]{:S(2)}) copy-start(bf16[120]{0:T(256)(128)(2,1)} %param.28) | copy-start | bytes 724
  305.7 15.6 %copy-start.2 = (f32[120]{0:T(128)S(1)}, f32[120]{0:T(128)}, u32[]{:S(2)}) copy-start(f32[120]{0:T(128)} %param.40) | copy-start | bytes 1444
  305.7 15.6 %copy-start.3 = (f32[120]{0:T(128)S(1)}, f32[120]{0:T(128)}, u32[]{:S(2)}) copy-start(f32[120]{0:T(128)} %param.34) | copy-start | bytes 1444
  305.8 15.6 %copy-start.4 = (f32[120]{0:T(128)S(1)}, f32[120]{0:T(128)}, u32[]{:S(2)}) copy-start(f32[120]{0:T(128)} %param.37) | copy-start | bytes 1444
  305.8 15.6 %copy-start.5 = (f32[120]{0:T(128)S(1)}, f32[120]{0:T(128)}, u32[]{:S(2)}) copy-start(f32[120]{0:T(128)} %param.31) | copy-start | bytes 1444

commit v5 on v4

--- a/solution.py
+++ b/solution.py
@@ -595,8 +595,9 @@
     def twin_b(self, j):
         return self.copy(1, j, self.grads.at[1, j], self.rb.at[j], self.at.core_side)
 
-    def far(self, j):
-        return self.copy(2, j, self.t2.at[j], self.r2.at[j], self.at.two_earlier)
+    def far(self, j, relayed=True):
+        device = self.at.earlier if relayed else self.at.two_earlier
+        return self.copy(2, j, self.t2.at[j], self.r2.at[j], device)
 
     def near(self, j):
         return self.copy(3, j, self.t1.at[j], self.r1.at[j], self.at.earlier)
@@ -605,19 +606,30 @@
         self.twin_b(j).start()
         self.twin_a(j).start()
 
-    def one(self, j):
+    def one(self, j, relayed=True):
         self.twin_b(j).wait_recv()
         self.twin_a(j).wait_recv()
         even = self.at.c == 0
         from_a, from_b = self.ra[j].astype(F32), self.rb[j].astype(F32)
         none = jnp.zeros_like(from_a)
         self.t2[j] = (self.grads[0, j].astype(F32) + jnp.where(even, none, from_b)).astype(BF)
-        pl.when(self.at.z > 1)(self.far(j).start)
+        pl.when(self.at.z > 1)(self.far(j, relayed).start)
         self.t1[j] = (self.grads[2, j].astype(F32) + jnp.where(even, from_b, from_a)).astype(BF)
-        pl.when(self.at.has_earlier)(self.near(j).start)
+        if not relayed:
+            pl.when(self.at.has_earlier)(self.near(j).start)
         self.out[j] = self.grads[4, j].astype(F32) + jnp.where(even, from_a, none)
 
     def two(self, j):
+        at = self.at
+
+        @pl.when(at.has_earlier & at.has_later)
+        def _():
+            self.far(j).wait_recv()
+            self.t1[j] = (self.t1[j].astype(F32) + self.r2[j].astype(F32)).astype(BF)
+
+        pl.when(at.has_earlier)(self.near(j).start)
+
+    def three(self, j, relayed=True):
         at = self.at
 
         @pl.when(at.has_later)
@@ -625,10 +637,11 @@
             self.near(j).wait_recv()
             self.out[j] = self.out[j] + self.r1[j].astype(F32)
 
-        @pl.when(at.z < 2)
-        def _():
-            self.far(j).wait_recv()
-            self.out[j] = self.out[j] + self.r2[j].astype(F32)
+        if not relayed:
+            @pl.when(at.z < 2)
+            def _():
+                self.far(j).wait_recv()
+                self.out[j] = self.out[j] + self.r2[j].astype(F32)
 
     def sent(self, j):
         at = self.at
@@ -740,18 +753,8 @@
     def zero(self, n):
         slot, (first, width) = n % self.slots, self.chunks[n]
         self.arrive(n, 0, self.r0.at[slot, :, :, pl.ds(0, width)])
-        per_plane = self.rows // (2 * self.half)
-
-        def add_rows(i, _):
-            z, where = i // per_plane, pl.ds(
-                pl.multiple_of(lax.rem(i, per_plane) * 2 * self.half, 2 * self.half), 2 * self.half
-            )
-            old = self.own[z, where, first : first + width].astype(F32)
-            new = self.r0[slot, z, where, :width].astype(F32)
-            self.own[z, where, first : first + width] = (old + new).astype(BF)
-            return 0
-
-        lax.fori_loop(0, 4 * per_plane, add_rows, 0)
+        for z in range(4):
+            self.own[z, :, first : first + width] += self.r0[slot, z, :, :width]
         if n + self.slots < len(self.chunks):
             pl.semaphore_signal(
                 self.free, inc=1, device_id=self.at.core_side, device_id_type=MESH
@@ -764,8 +767,7 @@
     def add(self, n, where, ref):
         cols = self.columns(n)
         for z in range(4):
-            old = self.own[z, where, cols].astype(F32)
-            self.own[z, where, cols] = (old + ref[z, :, cols].astype(F32)).astype(BF)
+            self.own[z, where, cols] += ref[z, :, cols]
 
     def one(self, n):
         at, cols = self.at, self.columns(n)
@@ -993,12 +995,13 @@
     store(cott, cott_hbm)
     first.z(2)
     second.start_z()
+    third.start_z()
     for i in range(3):
         first.cross(i)
     second.z(0)
-    third.start_z()
     for i in range(3):
         first.last(i)
+    second.z(1)
     first.landed()
     store(attend_ref, attend_hbm)
 
@@ -1039,36 +1042,38 @@
     for j in range(kv_heads):
         win_ref[4, j] = kvt[j].T
         spread.start(j)
-    second.z(1)
+    third.z(0)
     second.z(2)
     for start in range(0, split, 256):
         project(start)
+    third.z(1)
+    fourth.start_z()
+    second.cross(0)
     store(qt_ref, qt_hbm)
     flip_blocks(hidden, flipped)
     store(flipped, flipped_hbm)
     spread.one(0)
-    third.z(0)
+    third.cross(0)
     spread.one(1)
+    second.cross(1)
     spread.two(0)
     events = [
-        (0, lambda: second.cross(0)),
-        (1, lambda: second.cross(1)),
-        (2, lambda: third.z(1)),
-        (2, lambda: second.cross(2)),
-        (3, lambda: second.last(0)),
+        (0, lambda: third.z(2)),
+        (1, lambda: second.cross(2)),
+        (2, lambda: second.last(0)),
+        (2, lambda: fourth.z(0)),
+        (3, lambda: third.cross(1)),
         (4, lambda: second.last(1)),
-        (4, lambda: third.z(2)),
-        (4, fourth.start_z),
+        (5, lambda: fourth.z(1)),
         (5, lambda: second.last(2)),
-        (6, lambda: third.cross(0)),
-        (7, lambda: fourth.z(0)),
-        (8, lambda: third.cross(1)),
-        (9, lambda: fourth.z(1)),
-        (10, lambda: third.cross(2)),
-        (11, lambda: third.last(0)),
-        (12, lambda: fourth.z(2)),
-        (13, lambda: third.last(1)),
-        (14, lambda: third.last(2)),
+        (6, lambda: third.cross(2)),
+        (7, lambda: third.last(0)),
+        (8, lambda: fourth.cross(0)),
+        (9, lambda: fourth.z(2)),
+        (10, lambda: third.last(1)),
+        (11, lambda: fourth.cross(1)),
+        (12, lambda: third.last(2)),
+        (13, lambda: fourth.last(0)),
     ]
 
     def key_head(j, _):
@@ -1094,8 +1099,8 @@
         rest_ref.at[:, :, pl.ds(3 * FF, QW)], out_weight, local_sems.at[4]
     )
     load.start()
-    for i in range(3):
-        fourth.cross(i)
+    fourth.cross(2)
+    fourth.last(1)
     load.wait()
     real = real_lanes(width, rows, own_rows)
     gain = jnp.concatenate(
@@ -1114,8 +1119,7 @@
     store(hidden, hidden_hbm)
     flip_blocks(hidden, hiddent)
     store(hiddent, hiddent_hbm)
-    for i in range(3):
-        fourth.last(i)
+    fourth.last(2)
     third.landed()
     fourth.landed()
     for part in (first, second, third, fourth):
@@ -1299,9 +1303,8 @@
         copy.start()
     acc_out[...] = jnp.zeros_like(acc_out)
     acc_grad[...] = jnp.zeros_like(acc_grad)
-    for load in loads:
+    for load in loads[:-2]:
         load.wait()
-    out_full = out_weight.reshape(width, QW)
 
     def put(ref, column, value):
         where = pl.ds(pl.multiple_of(column, 128), value.shape[1])
@@ -1352,6 +1355,9 @@
 
     lax.fori_loop(0, FF // SUB, step, 0)
 
+    for load in loads[-2:]:
+        load.wait()
+    out_full = out_weight.reshape(width, QW)
     real = real_lanes(width, rows, own_rows)
     gain = jnp.concatenate(
         [out_weight[s, own_rows : own_rows + 1, :rows].astype(F32) for s in range(shard_count)],
@@ -1383,6 +1389,9 @@
         branch = value.astype(BF)
         hidden[where, :] = branch
         gradt_ref[:, where] = dot(branch, out_full[...]).T.astype(BF)
+        for step_number, event in events:
+            if step_number == FF // SUB + n:
+                event()
     store = pltpu.make_async_copy(acc_grad, middle_grad_hbm, sems.at[2, 2])
     store.start()
     stores[-2:] += [store]
@@ -1481,6 +1490,7 @@
         collect.start(j)
         pl.when(j > 0)(lambda: collect.one(j - 1))
         pl.when(j > 1)(lambda: collect.two(j - 2))
+        pl.when(j > 2)(lambda: collect.three(j - 3))
         return 0
 
     lax.fori_loop(0, KV_HEADS, key_head, 0)
@@ -1494,7 +1504,8 @@
     cos_ref,
     sin_ref,
     jointt,
-    flipped,
+    hidden_own,
+    hidden_give,
     x_hbm,
     middle_grad_hbm,
     attend_hbm,
@@ -1522,36 +1533,39 @@
         load.start()
     last = KV_HEADS - 1
     sides = (
-        (1 - at.c, lambda n: (total.give.at[n % total.slots], 0)),
-        (at.c, lambda n: (total.own, total.chunks[n][0])),
+        (1 - at.c, hidden_give, lambda n: (total.give.at[n % total.slots], 0)),
+        (at.c, hidden_own, lambda n: (total.own, total.chunks[n][0])),
     )
 
     def gradients(n, rows_of_joint, gain):
         total.claim(n)
-        for side, (core, target) in enumerate(sides):
+        for side, (core, lhs, target) in enumerate(sides):
             ref, column = target(n)
+            product = dot(
+                lhs[...].reshape(planes * rows, tokens), jointt[rows_of_joint, :], 1, 1
+            )
             for z in range(planes):
-                plane = 2 * z + core
-                product = dot(flipped[plane], jointt[rows_of_joint, :], 1, 1)
-                row = (own_rows, gain_term[plane][:1]) if gain else None
-                put_gradient(total, n, column, ref, z, product, row)
+                row = (own_rows, gain_term[2 * z + core][:1]) if gain else None
+                plane = product[z * rows : (z + 1) * rows]
+                put_gradient(total, n, column, ref, z, plane, row)
             if side == 0:
                 total.start(n)
 
     gradients(QUERY_CHUNK, slice(0, QW), False)
-    collect.one(last)
-    total.zero(QUERY_CHUNK)
-    total.push(QUERY_CHUNK)
-    events[0]()
+    collect.one(last, False)
+    collect.two(last - 1)
     for load in loads:
         load.wait()
     weight = attend_ref.reshape(width, columns)
     for low in range(0, tokens, PART):
         where = slice(low, low + PART)
         hidden_grad[where, :] = dot(jointt[:QW, where].T, weight[:, :QW], 1, 1)
-    events[1]()
-    collect.two(last - 1)
-    collect.two(last)
+    total.zero(QUERY_CHUNK)
+    total.push(QUERY_CHUNK)
+    events[0]()
+    collect.three(last - 2)
+    collect.three(last - 1)
+    collect.three(last, False)
     for j in range(KV_HEADS):
         pair = collect.out[j].T
         low = QW + j * HEAD_DIM
@@ -1570,6 +1584,7 @@
     for s in range(shard_count):
         gain_term[s] = jnp.broadcast_to(term[:, s * rows : (s + 1) * rows], (8, rows))
     gradients(PAIR_CHUNK, slice(QW, columns), True)
+    events[1]()
     total.one(QUERY_CHUNK)
     total.zero(PAIR_CHUNK)
     total.push(PAIR_CHUNK)
@@ -1666,23 +1681,27 @@
         return event
 
     def round_of(t):
-        due = [("one", t), ("push", t + 1), ("two", t - 1), ("three", t - 2), ("four", t - 3)]
-        return [(name, n) for name, n in due + [("five", t - 4)] if 0 <= n <= OUT_CHUNK]
+        due = [("one", t), ("push", t + 1), ("two", t - 1), ("three", t - 3), ("four", t - 4)]
+        return [(name, n) for name, n in due + [("five", t - 5)] if 0 <= n <= OUT_CHUNK]
 
     forward_events = [
         (2, run(("zero", 0), ("push", 0))),
         (4, run(("zero", 1))),
         (6, run(("zero", 2), *round_of(0))),
         (8, run(("zero", 3))),
+        (12, run(("zero", 4), *round_of(1))),
     ]
     backward_events = [
-        (-1, run(("zero", 4), *round_of(1))),
-        (3, run(("zero", 5), *round_of(2))),
-        (6, run(*round_of(3))),
-        (9, run(*round_of(4))),
-        (12, run(*round_of(5))),
+        (0, run(("zero", 5))),
+        (1, run(*round_of(2))),
+        (4, run(*round_of(3))),
+        (7, run(*round_of(4))),
+        (10, run(*round_of(5))),
+        (12, run(*round_of(6))),
+        (13, run(*round_of(7))),
+        (14, run(*round_of(8))),
     ]
-    last_events = [run(*round_of(6)), run(*round_of(7), *round_of(8)), run(*round_of(9))]
+    last_events = [run(), run(*round_of(9)), run(*round_of(10))]
 
     pl.run_scoped(
         functools.partial(
@@ -1719,10 +1738,15 @@
         DMA((4 + 2 * shard_count,)),
     )
 
-    def attention(grads, t2, t1, flipped, flipped_sem):
+    def attention(grads, t2, t1, hidden_own, hidden_give, sems):
         collect = Collect(at, grads, pairs, ra, rb, r2, r1, t2, t1, collect_send, collect_recv)
-        load = pltpu.make_async_copy(flipped_hbm, flipped, flipped_sem)
-        load.start()
+        loads = []
+        for z in range(shard_count // 2):
+            for i, (dst, core) in enumerate(((hidden_own, at.c), (hidden_give, 1 - at.c))):
+                src = flipped_hbm.at[2 * z + core]
+                loads.append(pltpu.make_async_copy(src, dst.at[z], sems.at[i, z]))
+        for load in loads:
+            load.start()
         pl.run_scoped(
             functools.partial(
                 attention_backward,
@@ -1747,7 +1771,8 @@
             VMEM(qt_hbm.shape, BF),
             DMA((3,)),
         )
-        load.wait()
+        for load in loads:
+            load.wait()
         pl.run_scoped(
             functools.partial(
                 projection_backward,
@@ -1758,7 +1783,8 @@
                 cos_ref,
                 sin_ref,
                 jointt,
-                flipped,
+                hidden_own,
+                hidden_give,
                 x_hbm,
                 middle_grad_hbm,
                 attend_hbm,
@@ -1778,8 +1804,9 @@
         VMEM(win_hbm.shape, BF),
         VMEM(pairs.shape, BF),
         VMEM(pairs.shape, BF),
-        VMEM(flipped_hbm.shape, BF),
-        DMA,
+        VMEM((shard_count // 2, rows, tokens), BF),
+        VMEM((shard_count // 2, rows, tokens), BF),
+        DMA((2, shard_count // 2)),
     )
 
 

time: 328 us -> 301 us (0.918)
  Pallas kernels: 321 us -> 294 us
    pallas_call x1, Pallas kernels: 112 us -> 96.8 us  [front(): pl.pallas_call(front_kernel, out_shape=in_hbm + in_vmem, in_specs=[pl.Blo...]
    pallas_call x1, Pallas kernels: 193 us -> 181 us  [rear(): pl.pallas_call(rear_kernel, out_shape=(jax.ShapeDtypeStruct((rows, column...]
where the time goes in v5:
time: 301 us; the launch traced here: 296 us
  Pallas kernels  294 us (98%)
    pallas_call x1, Pallas kernels, rear(): pl.pallas_call(rear_kernel, out_shape=(jax.ShapeDtypeStruct((rows, column...  181 us
    pallas_call x1, Pallas kernels, front(): pl.pallas_call(front_kernel, out_shape=in_hbm + in_vmem, in_specs=[pl.Blo...  96.8 us
    pallas_call x1, Pallas kernels, adam(): pl.pallas_call(functools.partial(adam_kernel, grad_scale, own_rows), out_...  15.6 us

profile of v5, /device:TPU:0, one launch (start us, length us, event | category | flops | bytes accessed | tf_op | source)
XLA Modules:
  0.0 296.0 jit_solution(16760012903854227445)
XLA Ops:
  0.7 96.8 %front.1 = (bf16[8,128,8640]{2,1,0:T(8,128)(2,1)}, bf16[8,128,1600]{2,1,0:T(8,128)(2,1)}, bf16[5,5,512,128]{3,2,1,0:T(8,128)(2,1)}, bf16[2560,128]{1,0:T(8,128)(...) custom-call(s32[1,3]{1,0:T(1,128)} %lengths_ref.1, ...), custom_call_target="tpu_custom_call" | custom-call | tf_op jit(solution)/shard_map/front/pallas_call | solution.py:1161
  97.4 181.2 %rear.1 = (bf16[128,10368]{1,0:T(8,128)(2,1)}, f32[960,512]{1,0:T(8,128)}, f32[960,512]{1,0:T(8,128)}, f32[512,1024]{1,0:T(8,128)}) custom-call(bf16[960,512]{1,0:T(8,128)(2,1)} %get-tuple-element.64.mixed_ref, f32[15,1,512]{2,1,0:T(1,128)} %get-tuple-element.65.lse_ref, bf16[128,512]{1,0:T(8,128)(2,1)} %get-tuple-element.66.qfeat_ref, ...), custom_call_target="tpu_custom_call" | custom-call | tf_op jit(solution)/shard_map/rear/pallas_call | solution.py:1819
  278.6 0.0 copy-start
  278.7 0.0 copy-start.1
  278.7 0.0 copy-start.2
  278.7 0.0 copy-start.3
  278.7 0.0 copy-start.4
  278.7 0.0 copy-start.5
  278.7 15.6 %adam.1 = (f32[120,1600]{1,0:T(8,128)}, f32[120,1600]{1,0:T(8,128)}, f32[120,1600]{1,0:T(8,128)}, f32[120,1600]{1,0:T(8,128)}, f32[960,120]{1,0:T(8,128)}, /*ind...) custom-call(bf16[128,10368]{1,0:T(8,128)(2,1)} %get-tuple-element.81, ...), custom_call_target="tpu_custom_call" | custom-call | tf_op jit(solution)/shard_map/adam/pallas_call | solution.py:1942
  294.3 0.0 copy-done
  294.3 0.0 copy-done.1
  294.3 0.0 copy-done.2
  294.3 0.0 copy-done.3
  294.3 0.0 copy-done.4
  294.3 0.0 copy-done.5
  294.3 1.2 add_multiply_fusion
Async XLA Ops:
  278.6 15.6 %copy-start = (bf16[120]{0:T(256)(128)(2,1)S(1)}, bf16[120]{0:T(256)(128)(2,1)}, u32[]{:S(2)}) copy-start(bf16[120]{0:T(256)(128)(2,1)} %param.25) | copy-start | bytes 724
  278.7 15.6 %copy-start.1 = (bf16[120]{0:T(256)(128)(2,1)S(1)}, bf16[120]{0:T(256)(128)(2,1)}, u32[]{:S(2)}) copy-start(bf16[120]{0:T(256)(128)(2,1)} %param.28) | copy-start | bytes 724
  278.7 15.6 %copy-start.2 = (f32[120]{0:T(128)S(1)}, f32[120]{0:T(128)}, u32[]{:S(2)}) copy-start(f32[120]{0:T(128)} %param.40) | copy-start | bytes 1444
  278.7 15.6 %copy-start.3 = (f32[120]{0:T(128)S(1)}, f32[120]{0:T(128)}, u32[]{:S(2)}) copy-start(f32[120]{0:T(128)} %param.34) | copy-start | bytes 1444
  278.7 15.6 %copy-start.4 = (f32[120]{0:T(128)S(1)}, f32[120]{0:T(128)}, u32[]{:S(2)}) copy-start(f32[120]{0:T(128)} %param.37) | copy-start | bytes 1444
  278.7 15.6 %copy-start.5 = (f32[120]{0:T(128)S(1)}, f32[120]{0:T(128)}, u32[]{:S(2)}) copy-start(f32[120]{0:T(128)} %param.31) | copy-start | bytes 1444

commit v6 on v5

--- a/solution.py
+++ b/solution.py
@@ -1858,7 +1858,7 @@
         pltpu.make_async_copy(attend_planes.at[shard], weights[0], in_sems.at[8]),
         pltpu.make_async_copy(rest_planes.at[shard], weights[1], in_sems.at[9]),
     ]
-    order = (0, 1, 3, 2)
+    order = (2, 3, 0, 1)
     for n in order:
         for i in range(2):
             loads.append(

time: 301 us -> 300 us (level)
  no operation moved by 1% of the time
where the time goes in v6:
time: 300 us; the launch traced here: 295 us
  Pallas kernels  292 us (97%)
    pallas_call x1, Pallas kernels, rear(): pl.pallas_call(rear_kernel, out_shape=(jax.ShapeDtypeStruct((rows, column...  181 us
    pallas_call x1, Pallas kernels, front(): pl.pallas_call(front_kernel, out_shape=in_hbm + in_vmem, in_specs=[pl.Blo...  96.8 us
    pallas_call x1, Pallas kernels, adam(): pl.pallas_call(functools.partial(adam_kernel, grad_scale, own_rows), out_...  14.5 us

profile of v6, /device:TPU:0, one launch (start us, length us, event | category | flops | bytes accessed | tf_op | source)
XLA Modules:
  0.0 294.9 jit_solution(12201011586649460427)
XLA Ops:
  0.7 96.8 %front.1 = (bf16[8,128,8640]{2,1,0:T(8,128)(2,1)}, bf16[8,128,1600]{2,1,0:T(8,128)(2,1)}, bf16[5,5,512,128]{3,2,1,0:T(8,128)(2,1)}, bf16[2560,128]{1,0:T(8,128)(...) custom-call(s32[1,3]{1,0:T(1,128)} %lengths_ref.1, ...), custom_call_target="tpu_custom_call" | custom-call | tf_op jit(solution)/shard_map/front/pallas_call | solution.py:1161
  97.4 181.2 %rear.1 = (bf16[128,10368]{1,0:T(8,128)(2,1)}, f32[960,512]{1,0:T(8,128)}, f32[960,512]{1,0:T(8,128)}, f32[512,1024]{1,0:T(8,128)}) custom-call(bf16[960,512]{1,0:T(8,128)(2,1)} %get-tuple-element.64.mixed_ref, f32[15,1,512]{2,1,0:T(1,128)} %get-tuple-element.65.lse_ref, bf16[128,512]{1,0:T(8,128)(2,1)} %get-tuple-element.66.qfeat_ref, ...), custom_call_target="tpu_custom_call" | custom-call | tf_op jit(solution)/shard_map/rear/pallas_call | solution.py:1819
  278.6 0.0 copy-start
  278.7 0.0 copy-start.1
  278.7 0.0 copy-start.2
  278.7 0.0 copy-start.3
  278.7 0.0 copy-start.4
  278.7 0.0 copy-start.5
  278.7 14.5 %adam.1 = (f32[120,1600]{1,0:T(8,128)}, f32[120,1600]{1,0:T(8,128)}, f32[120,1600]{1,0:T(8,128)}, f32[120,1600]{1,0:T(8,128)}, f32[960,120]{1,0:T(8,128)}, /*ind...) custom-call(bf16[128,10368]{1,0:T(8,128)(2,1)} %get-tuple-element.81, ...), custom_call_target="tpu_custom_call" | custom-call | tf_op jit(solution)/shard_map/adam/pallas_call | solution.py:1942
  293.2 0.0 copy-done
  293.2 0.0 copy-done.1
  293.2 0.0 copy-done.2
  293.2 0.0 copy-done.3
  293.2 0.0 copy-done.4
  293.2 0.0 copy-done.5
  293.2 1.2 add_multiply_fusion
Async XLA Ops:
  278.6 14.5 %copy-start = (bf16[120]{0:T(256)(128)(2,1)S(1)}, bf16[120]{0:T(256)(128)(2,1)}, u32[]{:S(2)}) copy-start(bf16[120]{0:T(256)(128)(2,1)} %param.25) | copy-start | bytes 724
  278.7 14.5 %copy-start.1 = (bf16[120]{0:T(256)(128)(2,1)S(1)}, bf16[120]{0:T(256)(128)(2,1)}, u32[]{:S(2)}) copy-start(bf16[120]{0:T(256)(128)(2,1)} %param.28) | copy-start | bytes 724
  278.7 14.5 %copy-start.2 = (f32[120]{0:T(128)S(1)}, f32[120]{0:T(128)}, u32[]{:S(2)}) copy-start(f32[120]{0:T(128)} %param.40) | copy-start | bytes 1444
  278.7 14.5 %copy-start.3 = (f32[120]{0:T(128)S(1)}, f32[120]{0:T(128)}, u32[]{:S(2)}) copy-start(f32[120]{0:T(128)} %param.34) | copy-start | bytes 1444
  278.7 14.5 %copy-start.4 = (f32[120]{0:T(128)S(1)}, f32[120]{0:T(128)}, u32[]{:S(2)}) copy-start(f32[120]{0:T(128)} %param.37) | copy-start | bytes 1444
  278.7 14.5 %copy-start.5 = (f32[120]{0:T(128)S(1)}, f32[120]{0:T(128)}, u32[]{:S(2)}) copy-start(f32[120]{0:T(128)} %param.31) | copy-start | bytes 1444
